TPU v7x, 32 devices: a whole 2x2x4 slice. The times are simulated.
32 devices in a mesh: gx: 4 (over y, core), vert: 8 (over z, x).
Axes of the slice: x: 2, y: 2, z: 4, core: 2. Of those that a mesh axis runs over, the one named last changes fastest.
Arguments:
- dist: float32 [4096, 32, 128], P('vert', 'gx'), may hold values from 0.14 to 1.43
- inflow: float32 [4096, 128], P('vert'), may hold values from 0.25 to 1
- speed_x: float32 [4096], P('vert'), may hold values from 0.25 to 3
- transverse: float32 [2, 4096], P(None, 'vert'), may hold values from -1 to 1
- quad_weight: float32 [4096], P('vert'), may hold values from 0.5 to 2
- side: int32 [4096], P('vert'), may hold values from 0 to 1, as said below
Outputs:
- new_dist: float32 [4096, 32, 128], P('vert', 'gx')
- new_moments: float32 [13, 32, 128], P(None, 'gx')
Inputs may be any that keep to these rules, and one draw needn't show every extreme that they name: `side`: all velocities within one shard of the vert axis share the same value, and half of those shards hold 1.
All inputs are finite; a program needn't handle non-finite values.
Results may differ from a plain program's by a relative error of at most 0.0003.
Values sent between devices are 32-bit elements; how exact they have to be, the bound alone decides.
No kernel may reach another device: no remote copies, remote signals or barrier semaphores. Data moves between devices by JAX's collectives and lax.ppermute only.
A program may use at most 64 MiB of HBM per device.

v0:
```python
import functools

import jax
import jax.numpy as jnp
from jax import lax
from jax.experimental import pallas as pl
from jax.experimental.pallas import tpu as pltpu
from jax.sharding import PartitionSpec as P

NZ = 32
KAPPA_CELL = 0.02
LOG2E = 1.4426950408889634
SHEAR = 0.19
NMOM = 13
ROWS = 16


def params(**kw):
    return pltpu.CompilerParams(vmem_limit_bytes=40 * 1024 * 1024, **kw)


def cost(flops, nbytes):
    return pl.CostEstimate(flops=flops, bytes_accessed=nbytes, transcendentals=0)


def split(a):
    high = a.astype(jnp.bfloat16)
    low = (a - high.astype(jnp.float32)).astype(jnp.bfloat16)
    return high, low


def project(table, plane):
    high, low = split(plane)
    first = jnp.dot(table, high, preferred_element_type=jnp.float32)
    second = jnp.dot(table[:ROWS], low, preferred_element_type=jnp.float32)
    return first[:ROWS] + first[ROWS:] + second


def moments_kernel(total, nx, side_ref, speed_ref, cross_ref, weight_ref, dist_ref, mom_ref, table_ref):
    count = speed_ref.shape[1]
    speed = speed_ref[...]
    x = jnp.where(side_ref[...] == 1, speed, -speed)
    y = cross_ref[0:1, :]
    z = cross_ref[1:2, :]
    xx, yy, zz = x * x, y * y, z * z
    square = xx + yy + zz
    rows = [jnp.ones_like(x), x, y, z, xx, yy, zz, x * y, x * z, y * z, x * square, y * square, z * square]
    rows += [jnp.zeros_like(x)] * (ROWS - NMOM)
    full = jnp.concatenate(rows, axis=0) * (weight_ref[...] * (1.0 / total))
    high, low = split(full)
    table = jnp.concatenate([high, low], axis=0)
    table_ref[...] = table
    first = pl.program_id(0) == 0
    for i in range(0, nx, 2):
        planes = [dist_ref[pl.ds(i + k, count, stride=nx), :] for k in range(min(2, nx - i))]
        lanes = planes[0].shape[1]
        got = project(table, jnp.concatenate(planes, axis=1))
        for k in range(len(planes)):
            part = got[:NMOM, k * lanes : (k + 1) * lanes]
            place = pl.ds(i + k, NMOM, stride=nx)

            @pl.when(first)
            def _():
                mom_ref[place, :] = part

            @pl.when(jnp.logical_not(first))
            def _():
                mom_ref[place, :] += part


def old_moments(total, nx, side, speed, cross, weight, dist):
    count, lanes = speed.shape[1], dist.shape[1]
    chunk = min(count, 256)
    steps = count // chunk
    vec = lambda r: pl.BlockSpec((r, chunk), lambda i: (0, i))
    return pl.pallas_call(
        functools.partial(moments_kernel, total, nx),
        grid=(steps,),
        in_specs=[vec(1), vec(1), vec(2), vec(1), pl.BlockSpec((chunk * nx, lanes), lambda i: (i, 0))],
        out_specs=[pl.BlockSpec((NMOM * nx, lanes), lambda i: (0, 0)), vec(2 * ROWS)],
        out_shape=[
            jax.ShapeDtypeStruct((NMOM * nx, lanes), jnp.float32),
            jax.ShapeDtypeStruct((2 * ROWS, count), jnp.bfloat16),
        ],
        compiler_params=params(),
        cost_estimate=cost(2 * 48 * count * nx * lanes, 4 * count * nx * lanes),
        name="moments",
    )(side, speed, cross, weight, dist)


def slope_kernel(nx, side_ref, speed_ref, cross_ref, dist_ref, slope_ref, comp_ref):
    count = speed_ref.shape[1]
    lanes = dist_ref.shape[1]
    speed = speed_ref[...]
    x = jnp.where(side_ref[...] == 1, speed, -speed)
    stacked = jnp.concatenate([x, cross_ref[...], jnp.zeros((5, count), jnp.float32)], axis=0)
    columns = jnp.transpose(stacked)
    for k in range(3):
        comp_ref[k] = jnp.broadcast_to(columns[:, k : k + 1], (count, lanes))
    group = 32

    def one(g, carry):
        at = pl.multiple_of(g * group, group)
        y = comp_ref[1, pl.ds(at, group), :]
        z = comp_ref[2, pl.ds(at, group), :]
        lane = lax.broadcasted_iota(jnp.int32, (group, lanes), 1)
        from_y = jnp.where(y > 0, lane + (lanes - NZ), lane + NZ) & (lanes - 1)
        from_z = (lane & ~(NZ - 1)) | (jnp.where(z > 0, lane + (NZ - 1), lane + 1) & (NZ - 1))
        ay, az = KAPPA_CELL * jnp.abs(y), KAPPA_CELL * jnp.abs(z)
        both = ay + az
        for i in range(nx):
            d = dist_ref[pl.ds(at * nx + i, group, stride=nx), :]
            near_y = jnp.take_along_axis(d, from_y, axis=1)
            near_z = jnp.take_along_axis(d, from_z, axis=1)
            slope_ref[i, pl.ds(at, group), :] = both * d - ay * near_y - az * near_z
        return carry

    lax.fori_loop(0, count // group, one, 0)


def slopes(nx, side, speed, cross, dist):
    count, lanes = speed.shape[1], dist.shape[1]
    chunk = min(count, 128)
    vec = lambda r: pl.BlockSpec((r, chunk), lambda i: (0, i))
    return pl.pallas_call(
        functools.partial(slope_kernel, nx),
        grid=(count // chunk,),
        in_specs=[vec(1), vec(1), vec(2), pl.BlockSpec((chunk * nx, lanes), lambda i: (i, 0))],
        out_specs=[
            pl.BlockSpec((nx, chunk, lanes), lambda i: (0, i, 0)),
            pl.BlockSpec((3, chunk, lanes), lambda i: (0, i, 0)),
        ],
        out_shape=[
            jax.ShapeDtypeStruct((nx, count, lanes), jnp.float32),
            jax.ShapeDtypeStruct((3, count, lanes), jnp.float32),
        ],
        compiler_params=params(),
        cost_estimate=cost(20 * count * nx * lanes, 8 * count * nx * lanes),
        name="slope",
    )(side, speed, cross, dist)


def map_kernel(nx, side_ref, ma_ref, mb_ref, comp_ref, slope_ref, inflow_ref,
               decay_ref, source_ref, face_ref, state):
    lanes = inflow_ref.shape[1]
    count = inflow_ref.shape[0]
    m = [ma_ref[k * nx : (k + 1) * nx, :] + mb_ref[k * nx : (k + 1) * nx, :] for k in range(NMOM)]
    n = m[0]
    inv_n = 1.0 / n
    u = [m[1] * inv_n, m[2] * inv_n, m[3] * inv_n]
    energy = m[4] + m[5] + m[6]
    uu = u[0] * u[0] + u[1] * u[1] + u[2] * u[2]
    temp = (energy * inv_n - uu) * (1.0 / 3.0)
    second = ((m[4], m[7], m[8]), (m[7], m[5], m[9]), (m[8], m[9], m[6]))
    inv_t = 1.0 / temp
    flux_scale = inv_n * inv_t * inv_t * (1.0 / 15.0)
    nu = KAPPA_CELL * n * jnp.exp(SHEAR * jnp.log(temp))
    for k in range(3):
        inner = u[0] * second[k][0] + u[1] * second[k][1] + u[2] * second[k][2]
        q = 0.5 * (m[10 + k] - 2.0 * inner - u[k] * energy + 2.0 * n * u[k] * uu)
        state[k] = u[k]
        state[3 + k] = q * flux_scale
    state[6] = inv_t
    state[7] = inv_t * (-0.5 * LOG2E)
    state[8] = nu * n * inv_t * jnp.sqrt(inv_t)
    state[9] = nu
    forward = side_ref[0, 0] == 1
    group = 32

    for j in range(nx):
        at_x = jnp.where(forward, j, nx - 1 - j)
        before = jnp.where(forward, j - 1, nx - j)
        s = [jnp.broadcast_to(state[k, pl.ds(at_x, 1), :], (8, lanes)) for k in range(10)]
        s = [jnp.concatenate([a] * (group // 8), axis=0) for a in s]

        def one(g, carry):
            at = pl.multiple_of(g * group, group)
            rows = pl.ds(at, group)
            cx = comp_ref[0, rows, :]
            wx = cx - s[0]
            wy = comp_ref[1, rows, :] - s[1]
            wz = comp_ref[2, rows, :] - s[2]
            ww = wx * wx + wy * wy + wz * wz
            wq = wx * s[3] + wy * s[4] + wz * s[5]
            shape = 1.0 + wq * (ww * s[6] - 5.0)
            target = s[8] * jnp.exp2(ww * s[7]) * shape
            speed = jnp.abs(cx)
            inv = 1.0 / (speed + s[9])
            decay = speed * inv
            source = (target - slope_ref[at_x, rows, :]) * inv
            if j > 0:
                source = decay * source_ref[before, rows, :] + source
                decay = decay * decay_ref[before, rows, :]
            decay_ref[at_x, rows, :] = decay
            source_ref[at_x, rows, :] = source
            if j == nx - 1:
                face_ref[rows, :] = decay * inflow_ref[rows, :] + source
            return carry

        lax.fori_loop(0, count // group, one, 0)


def maps(nx, side, ma, mb, comp, slope, inflow):
    count, lanes = inflow.shape
    whole = pl.BlockSpec(memory_space=pltpu.VMEM)
    return pl.pallas_call(
        functools.partial(map_kernel, nx),
        in_specs=[pl.BlockSpec(memory_space=pltpu.SMEM)] + [whole] * 5,
        out_specs=[whole] * 3,
        out_shape=[
            jax.ShapeDtypeStruct((nx, count, lanes), jnp.float32),
            jax.ShapeDtypeStruct((nx, count, lanes), jnp.float32),
            jax.ShapeDtypeStruct((count, lanes), jnp.float32),
        ],
        scratch_shapes=[pltpu.VMEM((10, nx, lanes), jnp.float32)],
        compiler_params=params(),
        cost_estimate=cost(40 * count * nx * lanes, 12 * count * nx * lanes),
        name="maps",
    )(side, ma, mb, comp, slope, inflow)


def finish_kernel(nx, table_ref, entry_ref, decay_ref, source_ref, dist_ref, mom_ref):
    entry = entry_ref[...]
    count, lanes = entry.shape
    table = table_ref[...]
    for i in range(0, nx, 2):
        planes = []
        for k in range(min(2, nx - i)):
            plane = decay_ref[i + k] * entry + source_ref[i + k]
            dist_ref[pl.ds(i + k, count, stride=nx), :] = plane
            planes.append(plane)
        got = project(table, jnp.concatenate(planes, axis=1))
        for k in range(len(planes)):
            mom_ref[pl.ds(i + k, NMOM, stride=nx), :] = got[:NMOM, k * lanes : (k + 1) * lanes]


def finish(nx, table, entry, decay, source):
    count, lanes = entry.shape
    whole = pl.BlockSpec(memory_space=pltpu.VMEM)
    return pl.pallas_call(
        functools.partial(finish_kernel, nx),
        in_specs=[whole] * 4,
        out_specs=[whole] * 2,
        out_shape=[
            jax.ShapeDtypeStruct((count * nx, lanes), jnp.float32),
            jax.ShapeDtypeStruct((NMOM * nx, lanes), jnp.float32),
        ],
        compiler_params=params(),
        cost_estimate=cost(2 * 48 * count * nx * lanes, 12 * count * nx * lanes),
        name="finish",
    )(table, entry, decay, source)


def stages_of(n):
    out, bit = [], 1
    while bit < n:
        if bit * 4 <= n:
            out.append((bit, 2 * bit, 3 * bit))
            bit *= 4
        else:
            out.append((bit,))
            bit *= 2
    return out


def exchange(a, axis, mask):
    n = lax.axis_size(axis)
    return lax.ppermute(a, axis, [(i, i ^ mask) for i in range(n)])


def partial_sums(a, axis):
    n = lax.axis_size(axis)
    if n & (n - 1) or n == 1:
        total = lax.psum(a, axis)
        return total, jnp.zeros_like(total)
    stages = stages_of(n)
    for masks in stages[:-1]:
        a = functools.reduce(jnp.add, [exchange(a, axis, m) for m in masks], a)
    other = functools.reduce(jnp.add, [exchange(a, axis, m) for m in stages[-1]])
    return a, other


def hop(face, n, step):
    up = [(step, step + 1)]
    down = [(n - 1 - step, n - 2 - step)]
    if n % 2 == 0:
        got = lax.ppermute(face, "gx", up + down)
        return got, got
    return lax.ppermute(face, "gx", up), lax.ppermute(face, "gx", down)


def local(total, dist, inflow, speed_x, transverse, quad_weight, side):
    count, nx, lanes = dist.shape
    flat = dist.reshape(count * nx, lanes)
    side_row = side.reshape(1, count)
    speed = speed_x.reshape(1, count)
    weight = quad_weight.reshape(1, count)
    partial, table = old_moments(total, nx, side_row, speed, transverse, weight, flat)
    slope, comp = slopes(nx, side_row, speed, transverse, flat)
    ma, mb = partial_sums(partial, "vert")
    decay, source, face = maps(nx, side_row[:, :1], ma, mb, comp, slope, inflow)
    n = lax.axis_size("gx")
    place = lax.axis_index("gx")
    forward = side[0] == 1
    place = jnp.where(forward, place, n - 1 - place)
    entry = inflow
    if n > 1:
        last_decay = jnp.where(forward, decay[nx - 1], decay[0])
        last_source = jnp.where(forward, source[nx - 1], source[0])
    for step in range(n - 1):
        low, high = hop(face, n, step)
        entry = jnp.where(place == step + 1, jnp.where(forward, low, high), entry)
        if step < n - 2:
            face = last_decay * entry + last_source
    new_flat, new_partial = finish(nx, table, entry, decay, source)
    na, nb = partial_sums(new_partial, "vert")
    return new_flat.reshape(count, nx, lanes), (na + nb).reshape(NMOM, nx, lanes)


def solution(mesh):
    def whole(dist, inflow, speed_x, transverse, quad_weight, side):
        body = functools.partial(local, dist.shape[0])
        return jax.shard_map(
            body,
            mesh=mesh,
            in_specs=(P("vert", "gx", None), P("vert", None), P("vert"), P(None, "vert"), P("vert"), P("vert")),
            out_specs=(P("vert", "gx", None), P(None, "gx", None)),
            check_vma=False,
        )(dist, inflow, speed_x, transverse, quad_weight, side)

    return whole
```

profile of v0, /device:TPU:0, one launch (start us, length us, event | category | flops | bytes accessed | tf_op | source)
XLA Modules:
  0.0 59.6 jit_solution(12794463057589721563)
XLA Ops:
  0.6 0.0 copy-start.8
  0.6 0.0 copy-start.6
  0.7 0.0 copy-start
  0.7 1.6 %copy-done = f32[512,8,128]{2,1,0:T(8,128)S(1)} copy-done((f32[512,8,128]{2,1,0:T(8,128)S(1)}, f32[512,8,128]{2,1,0:T(8,128)}, u32[]{:S(2)}) %copy-start) | copy-done | bytes 2097176
  2.3 0.0 copy-start.5
  2.3 0.7 %copy-done.5 = f32[2,512]{1,0:T(2,128)S(1)} copy-done((f32[2,512]{1,0:T(2,128)S(1)}, f32[2,512]{1,0:T(2,128)}, u32[]{:S(2)}) %copy-start.5) | copy-done | bytes 4120
  2.9 0.7 %copy-done.7 = f32[512]{0:T(512)S(1)} copy-done((f32[512]{0:T(512)S(1)}, f32[512]{0:T(512)}, u32[]{:S(2)}) %copy-start.7) | copy-done | bytes 2072
  3.6 0.7 %copy-done.9 = s32[512]{0:T(512)S(1)} copy-done((s32[512]{0:T(512)S(1)}, s32[512]{0:T(512)}, u32[]{:S(2)}) %copy-start.9) | copy-done | bytes 2072
  4.3 0.7 %copy-done.10 = f32[512]{0:T(512)S(1)} copy-done((f32[512]{0:T(512)S(1)}, f32[512]{0:T(512)}, u32[]{:S(2)}) %copy-start.10) | copy-done | bytes 2072
  5.0 1.7 %moments.1 = (f32[104,128]{1,0:T(8,128)S(1)}, bf16[32,512]{1,0:T(8,128)(2,1)S(1)}) custom-call(s32[1,512]{1,0:T(1,128)S(1)} %bitcast.22, f32[1,512]{1,0:T(1,128)S(1)} %bitcast.20, f32[2,512]{1,0:T(2,128)S(1)} %copy-done.5, f32[1,512]{1,0:T(1,128)S(1)} %bitcast.25, f32[4096,128]{1,0:T(8,128)S(1)} %bitcast.18), custom_call_target="tpu_custom_call" | custom-call | flops 50331648 | bytes 2097152 | tf_op jit(solution)/shard_map/moments/pallas_call | solution.py:76
  6.7 4.0 %collective-permute-start.2 = (f32[104,128]{1,0:T(8,128)S(1)}, f32[104,128]{1,0:T(8,128)S(1)}, u32[]{:S(2)}, u32[]{:S(2)}) collective-permute-start(f32[104,128]{1,0:T(8,128)S(1)} %get-tuple-element.12), channel_id=1, source_target_pairs={{0,3},{1,2},{2,1},{3,0},{4,7},{5,6},{6,5},{7,4},{8,11},{9,10},{10,... | collective-permute-start | bytes 159752 | tf_op jit(solution)/shard_map/ppermute | solution.py:268
  10.7 0.4 collective-permute-start.1
  11.1 0.2 collective-permute-start
  11.3 1.5 %collective-permute-done.2 = f32[104,128]{1,0:T(8,128)S(1)} collective-permute-done((f32[104,128]{1,0:T(8,128)S(1)}, f32[104,128]{1,0:T(8,128)S(1)}, u32[]{:S(2)}, u32[]{:S(2)}) %collective-permute-start.2) | collective-permute-done | bytes 53280 | tf_op jit(solution)/shard_map/ppermute | solution.py:268
  12.8 2.0 %collective-permute-done.1 = f32[104,128]{1,0:T(8,128)S(1)} collective-permute-done((f32[104,128]{1,0:T(8,128)S(1)}, f32[104,128]{1,0:T(8,128)S(1)}, u32[]{:S(2)}, u32[]{:S(2)}) %collective-permute-start.1) | collective-permute-done | bytes 53280 | tf_op jit(solution)/shard_map/ppermute | solution.py:268
  14.8 0.4 collective-permute-done
  15.3 2.7 %collective-permute-start.3 = (f32[104,128]{1,0:T(8,128)S(1)}, f32[104,128]{1,0:T(8,128)S(1)}, u32[]{:S(2)}, u32[]{:S(2)}) collective-permute-start(f32[104,128]{1,0:T(8,128)S(1)} %add_add_fusion.1.ma_ref), channel_id=1, source_target_pairs={{0,4},{1,5},{2,6},{3,7},{4,0},{5,1},{6,2},{7,3},{8,12},{9,13},{10,... | collective-permute-start | bytes 159752 | tf_op jit(solution)/shard_map/ppermute | solution.py:268
  17.9 0.5 slice.24.side_ref
  18.4 0.0 copy-done.8
  18.4 0.0 copy-done.6
  18.4 0.0 copy-done.1
  18.4 5.2 %slope.1 = (f32[8,512,128]{2,1,0:T(8,128)S(1)}, f32[3,512,128]{2,1,0:T(8,128)S(1)}) custom-call(s32[1,512]{1,0:T(1,128)S(1)} %bitcast.24, f32[1,512]{1,0:T(1,128)S(1)} %bitcast.21, f32[2,512]{1,0:T(2,128)S(1)} %copy-done.6, f32[4096,128]{1,0:T(8,128)S(1)} %bitcast.19), custom_call_target="tpu_custom_call" | custom-call | flops 10485760 | bytes 4194304 | tf_op jit(solution)/shard_map/slope/pallas_call | solution.py:125
  23.7 0.0 collective-permute-done.3.mb_ref
  23.7 0.0 copy-done.4
  23.7 3.6 %maps.1 = (f32[8,512,128]{2,1,0:T(8,128)S(1)}, f32[8,512,128]{2,1,0:T(8,128)S(1)}, f32[512,128]{1,0:T(8,128)S(1)}) custom-call(s32[1,1]{1,0:T(1,128)} %slice.24.side_ref, f32[104,128]{1,0:T(8,128)S(1)} %add_add_fusion.1.ma_ref, f32[104,128]{1,0:T(8,128)S(1)} %collective-permute-done.3.mb_ref, f32[3,512,128]{2,1,0:T(8,128)S(1)} %get-tuple-element.13.comp_ref, ...), custom_call_target="tpu_custom_call" | custom-call | flops 20971520 | bytes 6291456 | tf_op jit(solution)/shard_map/maps/pallas_call | solution.py:206
  27.3 0.0 copy-start.2
  27.4 1.3 %copy-done.2 = f32[8,512,128]{2,1,0:T(8,128)} copy-done((f32[8,512,128]{2,1,0:T(8,128)}, f32[8,512,128]{2,1,0:T(8,128)S(1)}, u32[]{:S(2)}) %copy-start.2) | copy-done | bytes 2097176
  28.7 1.3 %collective-permute-start.4 = (f32[512,128]{1,0:T(8,128)S(1)}, f32[512,128]{1,0:T(8,128)S(1)}, u32[]{:S(2)}, u32[]{:S(2)}) collective-permute-start(f32[512,128]{1,0:T(8,128)S(1)} %get-tuple-element.16), channel_id=1, source_target_pairs={{0,8},{24,16},{1,9},{25,17},{2,10},{26,18},{3,11},{27,19},{4,12},{... | collective-permute-start | bytes 786440 | tf_op jit(solution)/shard_map/ppermute | solution.py:287
  30.0 0.5 slice.18
  31.1 0.0 collective-permute-done.4
  31.1 1.1 %bitcast_add_fusion.1 = (f32[512,128]{1,0:T(8,128)S(1)}, f32[512,128]{1,0:T(8,128)S(1)}) fusion(f32[8,512,128]{2,1,0:T(8,128)S(1)} %get-tuple-element.15.decay_ref, pred[]{:T(512)} %bitcast.4, f32[8,512,128]{2,1,0:T(8,128)} %copy-done.2, f32[512,128]{1,0:T(8,128)S(1)} %collective-permute-done.4, f32[512,128]{1,0:T(8,128)S(1)} %copy-done.4, pred[]{:T(512)S(6)} %eq.19), kind=kLoop, calls=%fused_computation.1 | loop fusion | flops 327680 | bytes 2097154 | tf_op jit(solution)/shard_map/add | solution.py:314
  32.3 0.7 %collective-permute-start.5 = (f32[512,128]{1,0:T(8,128)S(1)}, f32[512,128]{1,0:T(8,128)S(1)}, u32[]{:S(2)}, u32[]{:S(2)}) collective-permute-start(f32[512,128]{1,0:T(8,128)S(1)} %get-tuple-element.20), channel_id=1, source_target_pairs={{8,16},{16,8},{9,17},{17,9},{10,18},{18,10},{11,19},{19,11},{12,20... | collective-permute-start | bytes 786440 | tf_op jit(solution)/shard_map/ppermute | solution.py:287
  33.0 0.0 collective-permute-done.5
  33.0 1.1 %bitcast_add_fusion = f32[512,128]{1,0:T(8,128)S(1)} fusion(f32[512,128]{1,0:T(8,128)S(1)} %collective-permute-done.5, f32[512,128]{1,0:T(8,128)S(1)} %get-tuple-element.21, pred[]{:T(512)S(6)} %eq.18, f32[8,512,128]{2,1,0:T(8,128)S(1)} %get-tuple-element.15.decay_ref, pred[]{:T(512)} %bitcast.4, f32[8,512,128]{2,1,0:T(8,128)} %copy-done.2), kind=kLoop, calls=%fused_computation | loop fusion | flops 327680 | bytes 1835010 | tf_op jit(solution)/shard_map/add | solution.py:314
  34.1 1.3 %collective-permute-start.6 = (f32[512,128]{1,0:T(8,128)S(1)}, f32[512,128]{1,0:T(8,128)S(1)}, u32[]{:S(2)}, u32[]{:S(2)}) collective-permute-start(f32[512,128]{1,0:T(8,128)S(1)} %bitcast_add_fusion), channel_id=1, source_target_pairs={{16,24},{8,0},{17,25},{9,1},{18,26},{10,2},{19,27},{11,3},{20,28},... | collective-permute-start | bytes 786440 | tf_op jit(solution)/shard_map/ppermute | solution.py:287
  35.4 8.8 %collective-permute-done.6 = f32[512,128]{1,0:T(8,128)S(1)} collective-permute-done((f32[512,128]{1,0:T(8,128)S(1)}, f32[512,128]{1,0:T(8,128)S(1)}, u32[]{:S(2)}, u32[]{:S(2)}) %collective-permute-start.6) | collective-permute-done | bytes 262176 | tf_op jit(solution)/shard_map/ppermute | solution.py:287
  44.2 0.0 copy-start.3
  44.2 1.6 %copy-done.3 = f32[8,512,128]{2,1,0:T(8,128)S(1)} copy-done((f32[8,512,128]{2,1,0:T(8,128)S(1)}, f32[8,512,128]{2,1,0:T(8,128)}, u32[]{:S(2)}) %copy-start.3) | copy-done | bytes 2097176
  45.8 1.9 %finish.1 = (f32[4096,128]{1,0:T(8,128)}, f32[104,128]{1,0:T(8,128)S(1)}) custom-call(bf16[32,512]{1,0:T(8,128)(2,1)S(1)} %get-tuple-element.11.table_ref, f32[512,128]{1,0:T(8,128)S(1)} %broadcast_select_fusion.2.entry_ref, f32[8,512,128]{2,1,0:T(8,128)S(1)} %get-tuple-element.15.decay_ref, f32[8,512,128]{2,1,0:T(8,128)S(1)} %copy-done.3), custom_call_target="tpu_custom_call" | custom-call | flops 50331648 | bytes 6291456 | tf_op jit(solution)/shard_map/finish/pallas_call | solution.py:240
  47.7 1.5 %collective-permute-start.9 = (f32[104,128]{1,0:T(8,128)S(1)}, f32[104,128]{1,0:T(8,128)S(1)}, u32[]{:S(2)}, u32[]{:S(2)}) collective-permute-start(f32[104,128]{1,0:T(8,128)S(1)} %get-tuple-element.19), channel_id=1, source_target_pairs={{0,3},{1,2},{2,1},{3,0},{4,7},{5,6},{6,5},{7,4},{8,11},{9,10},{10,... | collective-permute-start | bytes 159752 | tf_op jit(solution)/shard_map/ppermute | solution.py:268
  49.2 0.4 collective-permute-start.8
  49.7 1.5 %collective-permute-start.7 = (f32[104,128]{1,0:T(8,128)S(1)}, f32[104,128]{1,0:T(8,128)S(1)}, u32[]{:S(2)}, u32[]{:S(2)}) collective-permute-start(f32[104,128]{1,0:T(8,128)S(1)} %get-tuple-element.19), channel_id=1, source_target_pairs={{0,1},{1,0},{2,3},{3,2},{4,5},{5,4},{6,7},{7,6},{8,9},{9,8},{10,11... | collective-permute-start | bytes 159752 | tf_op jit(solution)/shard_map/ppermute | solution.py:268
  51.2 1.7 %collective-permute-done.9 = f32[104,128]{1,0:T(8,128)S(1)} collective-permute-done((f32[104,128]{1,0:T(8,128)S(1)}, f32[104,128]{1,0:T(8,128)S(1)}, u32[]{:S(2)}, u32[]{:S(2)}) %collective-permute-start.9) | collective-permute-done | bytes 53280 | tf_op jit(solution)/shard_map/ppermute | solution.py:268
  52.9 0.5 collective-permute-done.8
  53.4 0.4 collective-permute-done.7
  53.8 0.4 collective-permute-start.10
  54.2 4.7 %collective-permute-done.10 = f32[104,128]{1,0:T(8,128)S(1)} collective-permute-done((f32[104,128]{1,0:T(8,128)S(1)}, f32[104,128]{1,0:T(8,128)S(1)}, u32[]{:S(2)}, u32[]{:S(2)}) %collective-permute-start.10) | collective-permute-done | bytes 53280 | tf_op jit(solution)/shard_map/ppermute | solution.py:268
  58.9 0.6 %add_bitcast_fusion = f32[13,8,128]{2,1,0:T(8,128)} fusion(f32[104,128]{1,0:T(8,128)S(1)} %add_add_fusion, f32[104,128]{1,0:T(8,128)S(1)} %collective-permute-done.10), kind=kLoop, calls=%fused_computation.9 | loop fusion | flops 13312 | bytes 159744 | tf_op jit(solution)/shard_map/reshape | solution.py:317
  (8 shorter events, 0.1 us)
Async XLA Ops:
  0.6 17.8 %copy-start.8 = (f32[512]{0:T(512)S(1)}, f32[512]{0:T(512)}, u32[]{:S(2)}) copy-start(f32[512]{0:T(512)} %param.8) | copy-start | bytes 6148
  0.6 17.8 %copy-start.6 = (f32[2,512]{1,0:T(2,128)S(1)}, f32[2,512]{1,0:T(2,128)}, u32[]{:S(2)}) copy-start(f32[2,512]{1,0:T(2,128)} %cross_ref.3) | copy-start | bytes 12292
  0.7 1.6 %copy-start = (f32[512,8,128]{2,1,0:T(8,128)S(1)}, f32[512,8,128]{2,1,0:T(8,128)}, u32[]{:S(2)}) copy-start(f32[512,8,128]{2,1,0:T(8,128)} %param.6) | copy-start | bytes 6291460
  2.3 0.7 %copy-start.5 = (f32[2,512]{1,0:T(2,128)S(1)}, f32[2,512]{1,0:T(2,128)}, u32[]{:S(2)}) copy-start(f32[2,512]{1,0:T(2,128)} %cross_ref.3) | copy-start | bytes 12292
  2.9 0.7 %copy-start.7 = (f32[512]{0:T(512)S(1)}, f32[512]{0:T(512)}, u32[]{:S(2)}) copy-start(f32[512]{0:T(512)} %param.8) | copy-start | bytes 6148
  3.6 0.7 %copy-start.9 = (s32[512]{0:T(512)S(1)}, s32[512]{0:T(512)}, u32[]{:S(2)}) copy-start(s32[512]{0:T(512)} %param.11) | copy-start | bytes 6148
  4.3 0.7 %copy-start.10 = (f32[512]{0:T(512)S(1)}, f32[512]{0:T(512)}, u32[]{:S(2)}) copy-start(f32[512]{0:T(512)} %param.10) | copy-start | bytes 6148
  5.0 13.5 %copy-start.1 = (f32[512,8,128]{2,1,0:T(8,128)S(1)}, f32[512,8,128]{2,1,0:T(8,128)}, u32[]{:S(2)}) copy-start(f32[512,8,128]{2,1,0:T(8,128)} %param.6) | copy-start | bytes 6291460
  5.0 18.7 %copy-start.4 = (f32[512,128]{1,0:T(8,128)S(1)}, f32[512,128]{1,0:T(8,128)}, u32[]{:S(2)}) copy-start(f32[512,128]{1,0:T(8,128)} %inflow_ref.1) | copy-start | bytes 786436
  6.7 6.1 %collective-permute-start.2 = (f32[104,128]{1,0:T(8,128)S(1)}, f32[104,128]{1,0:T(8,128)S(1)}, u32[]{:S(2)}, u32[]{:S(2)}) collective-permute-start(f32[104,128]{1,0:T(8,128)S(1)} %get-tuple-element.12), channel_id=1, source_target_pairs={{0,3},{1,2},{2,1},{3,0},{4,7},{5,6},{6,5},{7,4},{8,11},{9,10},{10,... | collective-permute-start | bytes 159752 | tf_op jit(solution)/shard_map/ppermute | solution.py:268
  10.7 4.1 %collective-permute-start.1 = (f32[104,128]{1,0:T(8,128)S(1)}, f32[104,128]{1,0:T(8,128)S(1)}, u32[]{:S(2)}, u32[]{:S(2)}) collective-permute-start(f32[104,128]{1,0:T(8,128)S(1)} %get-tuple-element.12), channel_id=1, source_target_pairs={{0,2},{1,3},{2,0},{3,1},{4,6},{5,7},{6,4},{7,5},{8,10},{9,11},{10,... | collective-permute-start | bytes 159752 | tf_op jit(solution)/shard_map/ppermute | solution.py:268
  11.1 4.1 %collective-permute-start = (f32[104,128]{1,0:T(8,128)S(1)}, f32[104,128]{1,0:T(8,128)S(1)}, u32[]{:S(2)}, u32[]{:S(2)}) collective-permute-start(f32[104,128]{1,0:T(8,128)S(1)} %get-tuple-element.12), channel_id=1, source_target_pairs={{0,1},{1,0},{2,3},{3,2},{4,5},{5,4},{6,7},{7,6},{8,9},{9,8},{10,11... | collective-permute-start | bytes 159752 | tf_op jit(solution)/shard_map/ppermute | solution.py:268
  15.3 8.4 %collective-permute-start.3 = (f32[104,128]{1,0:T(8,128)S(1)}, f32[104,128]{1,0:T(8,128)S(1)}, u32[]{:S(2)}, u32[]{:S(2)}) collective-permute-start(f32[104,128]{1,0:T(8,128)S(1)} %add_add_fusion.1.ma_ref), channel_id=1, source_target_pairs={{0,4},{1,5},{2,6},{3,7},{4,0},{5,1},{6,2},{7,3},{8,12},{9,13},{10,... | collective-permute-start | bytes 159752 | tf_op jit(solution)/shard_map/ppermute | solution.py:268
  27.3 1.3 %copy-start.2 = (f32[8,512,128]{2,1,0:T(8,128)}, f32[8,512,128]{2,1,0:T(8,128)S(1)}, u32[]{:S(2)}) copy-start(f32[8,512,128]{2,1,0:T(8,128)S(1)} %get-tuple-element.17.source_ref) | copy-start | bytes 6291460
  28.7 2.5 %collective-permute-start.4 = (f32[512,128]{1,0:T(8,128)S(1)}, f32[512,128]{1,0:T(8,128)S(1)}, u32[]{:S(2)}, u32[]{:S(2)}) collective-permute-start(f32[512,128]{1,0:T(8,128)S(1)} %get-tuple-element.16), channel_id=1, source_target_pairs={{0,8},{24,16},{1,9},{25,17},{2,10},{26,18},{3,11},{27,19},{4,12},{... | collective-permute-start | bytes 786440 | tf_op jit(solution)/shard_map/ppermute | solution.py:287
  32.3 0.7 %collective-permute-start.5 = (f32[512,128]{1,0:T(8,128)S(1)}, f32[512,128]{1,0:T(8,128)S(1)}, u32[]{:S(2)}, u32[]{:S(2)}) collective-permute-start(f32[512,128]{1,0:T(8,128)S(1)} %get-tuple-element.20), channel_id=1, source_target_pairs={{8,16},{16,8},{9,17},{17,9},{10,18},{18,10},{11,19},{19,11},{12,20... | collective-permute-start | bytes 786440 | tf_op jit(solution)/shard_map/ppermute | solution.py:287
  34.1 10.1 %collective-permute-start.6 = (f32[512,128]{1,0:T(8,128)S(1)}, f32[512,128]{1,0:T(8,128)S(1)}, u32[]{:S(2)}, u32[]{:S(2)}) collective-permute-start(f32[512,128]{1,0:T(8,128)S(1)} %bitcast_add_fusion), channel_id=1, source_target_pairs={{16,24},{8,0},{17,25},{9,1},{18,26},{10,2},{19,27},{11,3},{20,28},... | collective-permute-start | bytes 786440 | tf_op jit(solution)/shard_map/ppermute | solution.py:287
  44.2 1.6 %copy-start.3 = (f32[8,512,128]{2,1,0:T(8,128)S(1)}, f32[8,512,128]{2,1,0:T(8,128)}, u32[]{:S(2)}) copy-start(f32[8,512,128]{2,1,0:T(8,128)} %copy-done.2) | copy-start | bytes 6291460
  47.7 5.2 %collective-permute-start.9 = (f32[104,128]{1,0:T(8,128)S(1)}, f32[104,128]{1,0:T(8,128)S(1)}, u32[]{:S(2)}, u32[]{:S(2)}) collective-permute-start(f32[104,128]{1,0:T(8,128)S(1)} %get-tuple-element.19), channel_id=1, source_target_pairs={{0,3},{1,2},{2,1},{3,0},{4,7},{5,6},{6,5},{7,4},{8,11},{9,10},{10,... | collective-permute-start | bytes 159752 | tf_op jit(solution)/shard_map/ppermute | solution.py:268
  49.2 4.1 %collective-permute-start.8 = (f32[104,128]{1,0:T(8,128)S(1)}, f32[104,128]{1,0:T(8,128)S(1)}, u32[]{:S(2)}, u32[]{:S(2)}) collective-permute-start(f32[104,128]{1,0:T(8,128)S(1)} %get-tuple-element.19), channel_id=1, source_target_pairs={{0,2},{1,3},{2,0},{3,1},{4,6},{5,7},{6,4},{7,5},{8,10},{9,11},{10,... | collective-permute-start | bytes 159752 | tf_op jit(solution)/shard_map/ppermute | solution.py:268
  49.7 4.1 %collective-permute-start.7 = (f32[104,128]{1,0:T(8,128)S(1)}, f32[104,128]{1,0:T(8,128)S(1)}, u32[]{:S(2)}, u32[]{:S(2)}) collective-permute-start(f32[104,128]{1,0:T(8,128)S(1)} %get-tuple-element.19), channel_id=1, source_target_pairs={{0,1},{1,0},{2,3},{3,2},{4,5},{5,4},{6,7},{7,6},{8,9},{9,8},{10,11... | collective-permute-start | bytes 159752 | tf_op jit(solution)/shard_map/ppermute | solution.py:268
  53.8 5.1 %collective-permute-start.10 = (f32[104,128]{1,0:T(8,128)S(1)}, f32[104,128]{1,0:T(8,128)S(1)}, u32[]{:S(2)}, u32[]{:S(2)}) collective-permute-start(f32[104,128]{1,0:T(8,128)S(1)} %add_add_fusion), channel_id=1, source_target_pairs={{0,4},{1,5},{2,6},{3,7},{4,0},{5,1},{6,2},{7,3},{8,12},{9,13},{10,... | collective-permute-start | bytes 159752 | tf_op jit(solution)/shard_map/ppermute | solution.py:268
where the time goes:
time: 60 us; the launch traced here: 59.6 us
  waiting for transfers between devices  20.1 us (34%)
  starting transfers between devices  14.5 us (24%)
  Pallas kernels  12.4 us (21%)
  local copies, waits for them, and re-layouts  8.27 us (14%)
  other arithmetic  2.92 us (5%)
  between operations  1.45 us (2%)
    ppermute x8, waiting for transfers between devices, exchange(): return lax.ppermute(a, axis, [(i, i ^ mask) for i in range(n)])  11.3 us
    ppermute x8, starting transfers between devices, exchange(): return lax.ppermute(a, axis, [(i, i ^ mask) for i in range(n)])  11.2 us
    ppermute x3, waiting for transfers between devices, hop(): got = lax.ppermute(face, 'gx', up + down)  8.82 us
    unnamed x22, local copies, waits for them, and re-layouts  7.24 us
    pallas_call x1, Pallas kernels, slopes(): pl.pallas_call(functools.partial(slope_kernel, nx), grid=(count // chunk,...  5.23 us
    pallas_call x1, Pallas kernels, maps(): pl.pallas_call(functools.partial(map_kernel, nx), in_specs=[pl.BlockSpec(...  3.63 us
    ppermute x3, starting transfers between devices, hop(): got = lax.ppermute(face, 'gx', up + down)  3.26 us
    add x2, other arithmetic, local(): face = last_decay * entry + last_source  2.22 us
  transfers between devices with their start and end apart: 11, of which 8 were waited for; matrix products, arithmetic and copies ran while one was open for 2% of the time, Pallas kernels for 9%

commit v1 on v0

v1 whole, which is shorter than its diff:
```python
import functools

import jax
import jax.numpy as jnp
from jax import lax
from jax.experimental import pallas as pl
from jax.experimental.pallas import tpu as pltpu
from jax.sharding import PartitionSpec as P

NZ = 32
KAPPA_CELL = 0.02
LOG2E = 1.4426950408889634
SHEAR = 0.19
NMOM = 13
ROWS = 16


def params(**kw):
    return pltpu.CompilerParams(vmem_limit_bytes=20 * 1024 * 1024, **kw)


def cost(flops, nbytes):
    return pl.CostEstimate(flops=flops, bytes_accessed=nbytes, transcendentals=0)


def split(a):
    high = a.astype(jnp.bfloat16)
    low = (a - high.astype(jnp.float32)).astype(jnp.bfloat16)
    return high, low


def project(table, plane):
    high, low = split(plane)
    first = jnp.dot(table, high, preferred_element_type=jnp.float32)
    second = jnp.dot(table[:ROWS], low, preferred_element_type=jnp.float32)
    return first[:ROWS] + first[ROWS:] + second


def moments_kernel(total, nx, chunks, side_hbm, speed_hbm, cross_hbm, weight_hbm, dist_hbm,
                   mom_ref, table_ref, side_ref, speed_ref, cross_ref, weight_ref, dist_ref, sems):
    count = speed_ref.shape[1]
    chunk = count // chunks
    small = [(side_hbm, side_ref), (speed_hbm, speed_ref), (cross_hbm, cross_ref), (weight_hbm, weight_ref)]
    copies = [pltpu.make_async_copy(a, b, sems.at[chunks + i]) for i, (a, b) in enumerate(small)]
    parts = []
    for i in range(chunks):
        rows = pl.ds(i * chunk * nx, chunk * nx)
        parts.append(pltpu.make_async_copy(dist_hbm.at[rows, :], dist_ref.at[rows, :], sems.at[i]))
    for c in copies + parts:
        c.start()
    for c in copies:
        c.wait()
    speed = speed_ref[...]
    x = jnp.where(side_ref[...] == 1, speed, -speed)
    y = cross_ref[0:1, :]
    z = cross_ref[1:2, :]
    xx, yy, zz = x * x, y * y, z * z
    square = xx + yy + zz
    rows = [jnp.ones_like(x), x, y, z, xx, yy, zz, x * y, x * z, y * z, x * square, y * square, z * square]
    rows += [jnp.zeros_like(x)] * (ROWS - NMOM)
    full = jnp.concatenate(rows, axis=0) * (weight_ref[...] * (1.0 / total))
    high, low = split(full)
    table = jnp.concatenate([high, low], axis=0)
    table_ref[...] = table
    for c in range(chunks):
        parts[c].wait()
        tab = table[:, c * chunk : (c + 1) * chunk]
        for i in range(0, nx, 2):
            pair = range(min(2, nx - i))
            planes = [dist_ref[pl.ds(c * chunk * nx + i + k, chunk, stride=nx), :] for k in pair]
            lanes = planes[0].shape[1]
            got = project(tab, jnp.concatenate(planes, axis=1))
            for k in pair:
                part = got[:NMOM, k * lanes : (k + 1) * lanes]
                place = pl.ds(i + k, NMOM, stride=nx)
                if c == 0:
                    mom_ref[place, :] = part
                else:
                    mom_ref[place, :] += part


def old_moments(total, nx, side, speed, cross, weight, dist):
    count, lanes = speed.shape[1], dist.shape[1]
    chunks = max(1, count // 256)
    whole = pl.BlockSpec(memory_space=pltpu.VMEM)
    return pl.pallas_call(
        functools.partial(moments_kernel, total, nx, chunks),
        in_specs=[pl.BlockSpec(memory_space=pltpu.HBM)] * 5,
        out_specs=[whole] * 2,
        out_shape=[
            jax.ShapeDtypeStruct((NMOM * nx, lanes), jnp.float32),
            jax.ShapeDtypeStruct((2 * ROWS, count), jnp.bfloat16),
        ],
        scratch_shapes=[
            pltpu.VMEM(side.shape, jnp.int32),
            pltpu.VMEM(speed.shape, jnp.float32),
            pltpu.VMEM(cross.shape, jnp.float32),
            pltpu.VMEM(weight.shape, jnp.float32),
            pltpu.VMEM(dist.shape, jnp.float32),
            pltpu.SemaphoreType.DMA((chunks + 4,)),
        ],
        compiler_params=params(),
        cost_estimate=cost(2 * 48 * count * nx * lanes, 4 * count * nx * lanes),
        name="moments",
    )(*[pltpu.with_memory_space_constraint(a, pltpu.HBM) for a in (side, speed, cross, weight, dist)])


def slope_kernel(nx, side_ref, speed_ref, cross_ref, dist_ref, slope_ref, comp_ref):
    count = speed_ref.shape[1]
    lanes = dist_ref.shape[1]
    speed = speed_ref[...]
    x = jnp.where(side_ref[...] == 1, speed, -speed)
    stacked = jnp.concatenate([x, cross_ref[...], jnp.zeros((5, count), jnp.float32)], axis=0)
    columns = jnp.transpose(stacked)
    for k in range(3):
        comp_ref[k] = jnp.broadcast_to(columns[:, k : k + 1], (count, lanes))
    group = 32

    def one(g, carry):
        at = pl.multiple_of(g * group, group)
        y = comp_ref[1, pl.ds(at, group), :]
        z = comp_ref[2, pl.ds(at, group), :]
        lane = lax.broadcasted_iota(jnp.int32, (group, lanes), 1)
        from_y = jnp.where(y > 0, lane + (lanes - NZ), lane + NZ) & (lanes - 1)
        from_z = (lane & ~(NZ - 1)) | (jnp.where(z > 0, lane + (NZ - 1), lane + 1) & (NZ - 1))
        ay, az = KAPPA_CELL * jnp.abs(y), KAPPA_CELL * jnp.abs(z)
        both = ay + az
        for i in range(nx):
            d = dist_ref[pl.ds(at * nx + i, group, stride=nx), :]
            near_y = jnp.take_along_axis(d, from_y, axis=1)
            near_z = jnp.take_along_axis(d, from_z, axis=1)
            slope_ref[i, pl.ds(at, group), :] = both * d - ay * near_y - az * near_z
        return carry

    lax.fori_loop(0, count // group, one, 0)


def slopes(nx, half, halves, side, speed, cross, dist):
    count, lanes = speed.shape[1] // halves, dist.shape[1]
    chunk = min(count, 128)
    steps = count // chunk
    vec = lambda r: pl.BlockSpec((r, chunk), lambda i: (0, half * steps + i))
    return pl.pallas_call(
        functools.partial(slope_kernel, nx),
        grid=(steps,),
        in_specs=[vec(1), vec(1), vec(2), pl.BlockSpec((chunk * nx, lanes), lambda i: (half * steps + i, 0))],
        out_specs=[
            pl.BlockSpec((nx, chunk, lanes), lambda i: (0, i, 0)),
            pl.BlockSpec((3, chunk, lanes), lambda i: (0, i, 0)),
        ],
        out_shape=[
            jax.ShapeDtypeStruct((nx, count, lanes), jnp.float32),
            jax.ShapeDtypeStruct((3, count, lanes), jnp.float32),
        ],
        compiler_params=params(),
        cost_estimate=cost(20 * count * nx * lanes, 8 * count * nx * lanes),
        name="slope",
    )(side, speed, cross, dist)


def map_kernel(nx, halves, ma_ref, mb_ref, *refs):
    comps, slopes_in = refs[:halves], refs[halves : 2 * halves]
    inflow_ref, decay_ref, source_ref, face_ref, last_decay_ref, last_source_ref, place_ref, state = refs[2 * halves :]
    here, there = lax.axis_index("gx"), lax.axis_size("gx") - 1 - lax.axis_index("gx")
    place_ref[...] = jnp.where(comps[0][0, 0:8, :] > 0, here, there)
    lanes = inflow_ref.shape[1]
    count = inflow_ref.shape[0]
    m = [ma_ref[k * nx : (k + 1) * nx, :] + mb_ref[k * nx : (k + 1) * nx, :] for k in range(NMOM)]
    n = m[0]
    inv_n = 1.0 / n
    u = [m[1] * inv_n, m[2] * inv_n, m[3] * inv_n]
    energy = m[4] + m[5] + m[6]
    uu = u[0] * u[0] + u[1] * u[1] + u[2] * u[2]
    temp = (energy * inv_n - uu) * (1.0 / 3.0)
    second = ((m[4], m[7], m[8]), (m[7], m[5], m[9]), (m[8], m[9], m[6]))
    inv_t = 1.0 / temp
    flux_scale = inv_n * inv_t * inv_t * (1.0 / 15.0)
    nu = KAPPA_CELL * n * jnp.exp(SHEAR * jnp.log(temp))
    for k in range(3):
        inner = u[0] * second[k][0] + u[1] * second[k][1] + u[2] * second[k][2]
        q = 0.5 * (m[10 + k] - 2.0 * inner - u[k] * energy + 2.0 * n * u[k] * uu)
        state[k] = u[k]
        state[3 + k] = q * flux_scale
    state[6] = inv_t
    state[7] = inv_t * (-0.5 * LOG2E)
    state[8] = nu * n * inv_t * jnp.sqrt(inv_t)
    state[9] = nu
    forward = comps[0][0, 0:1, 0:1][0, 0] > 0
    group = 32
    part = count // halves

    for j in range(nx):
        at_x = jnp.where(forward, j, nx - 1 - j)
        before = jnp.where(forward, j - 1, nx - j)
        s = [jnp.broadcast_to(state[k, pl.ds(at_x, 1), :], (8, lanes)) for k in range(10)]
        s = [jnp.concatenate([a] * (group // 8), axis=0) for a in s]

        for h in range(halves):
            comp_ref, slope_ref = comps[h], slopes_in[h]

            def one(g, carry):
                at = pl.multiple_of(g * group, group)
                own = pl.ds(at, group)
                rows = pl.ds(h * part + at, group)
                cx = comp_ref[0, own, :]
                wx = cx - s[0]
                wy = comp_ref[1, own, :] - s[1]
                wz = comp_ref[2, own, :] - s[2]
                ww = wx * wx + wy * wy + wz * wz
                wq = wx * s[3] + wy * s[4] + wz * s[5]
                shape = 1.0 + wq * (ww * s[6] - 5.0)
                target = s[8] * jnp.exp2(ww * s[7]) * shape
                speed = jnp.abs(cx)
                inv = 1.0 / (speed + s[9])
                decay = speed * inv
                source = (target - slope_ref[at_x, own, :]) * inv
                if j > 0:
                    source = decay * source_ref[before, rows, :] + source
                    decay = decay * decay_ref[before, rows, :]
                decay_ref[at_x, rows, :] = decay
                source_ref[at_x, rows, :] = source
                if j == nx - 1:
                    last_decay_ref[rows, :] = decay
                    last_source_ref[rows, :] = source
                    face_ref[rows, :] = decay * inflow_ref[rows, :] + source
                return carry

            lax.fori_loop(0, part // group, one, 0)


def maps(nx, ma, mb, comps, slopes_in, inflow):
    count, lanes = inflow.shape
    halves = len(comps)
    whole = pl.BlockSpec(memory_space=pltpu.VMEM)
    field = pltpu.VMEM((nx, count, lanes), jnp.float32)
    face = pltpu.VMEM((count, lanes), jnp.float32)
    return pl.pallas_call(
        functools.partial(map_kernel, nx, halves),
        in_specs=[whole] * (3 + 2 * halves),
        out_specs=[whole] * 6,
        out_shape=[field, field, face, face, face, pltpu.VMEM((8, lanes), jnp.int32)],
        scratch_shapes=[pltpu.VMEM((10, nx, lanes), jnp.float32)],
        compiler_params=params(),
        cost_estimate=cost(40 * count * nx * lanes, 12 * count * nx * lanes),
        name="maps",
    )(ma, mb, *comps, *slopes_in, inflow)


def entry_of(step, place_ref, got_ref, entry_ref):
    return jnp.where(place_ref[0:1, :] == step, got_ref[...], entry_ref[...])


def face_kernel(step, place_ref, got_ref, entry_ref, decay_ref, source_ref, next_ref, face_ref):
    entry = entry_of(step, place_ref, got_ref, entry_ref)
    next_ref[...] = entry
    face_ref[...] = decay_ref[...] * entry + source_ref[...]


def pass_face(step, place, got, entry, decay, source):
    whole = pl.BlockSpec(memory_space=pltpu.VMEM)
    out = pltpu.VMEM(entry.shape, jnp.float32)
    return pl.pallas_call(
        functools.partial(face_kernel, step),
        in_specs=[whole] * 5,
        out_specs=[whole] * 2,
        out_shape=[out, out],
        compiler_params=params(),
        cost_estimate=cost(2 * entry.size, 20 * entry.size),
        name="face",
    )(place, got, entry, decay, source)


def new_moments_kernel(nx, step, place_ref, got_ref, entry_ref, table_ref, decay_ref, source_ref, mom_ref):
    entry = entry_of(step, place_ref, got_ref, entry_ref)
    lanes = entry.shape[1]
    table = table_ref[...]
    for i in range(0, nx, 2):
        pair = range(min(2, nx - i))
        planes = [decay_ref[i + k] * entry + source_ref[i + k] for k in pair]
        got = project(table, jnp.concatenate(planes, axis=1))
        for k in pair:
            mom_ref[pl.ds(i + k, NMOM, stride=nx), :] = got[:NMOM, k * lanes : (k + 1) * lanes]


def new_moments(nx, step, face_in, table, decay, source):
    count, lanes = decay.shape[1:]
    whole = pl.BlockSpec(memory_space=pltpu.VMEM)
    return pl.pallas_call(
        functools.partial(new_moments_kernel, nx, step),
        in_specs=[whole] * 6,
        out_specs=whole,
        out_shape=jax.ShapeDtypeStruct((NMOM * nx, lanes), jnp.float32),
        compiler_params=params(),
        cost_estimate=cost(2 * 48 * count * nx * lanes, 8 * count * nx * lanes),
        name="new_moments",
    )(*face_in, table, decay, source)


def write_kernel(nx, step, place_ref, got_ref, entry_ref, decay_ref, source_ref, dist_ref):
    entry = entry_of(step, place_ref, got_ref, entry_ref)
    count = entry.shape[0]
    for i in range(nx):
        dist_ref[pl.ds(i, count, stride=nx), :] = decay_ref[i] * entry + source_ref[i]


def write_dist(nx, step, place, got, entry, decay, source):
    count, lanes = entry.shape
    chunk = min(count, 128)
    field = pl.BlockSpec((nx, chunk, lanes), lambda i: (0, i, 0))
    face = pl.BlockSpec((chunk, lanes), lambda i: (i, 0))
    return pl.pallas_call(
        functools.partial(write_kernel, nx, step),
        grid=(count // chunk,),
        in_specs=[pl.BlockSpec((8, lanes), lambda i: (0, 0)), face, face, field, field],
        out_specs=pl.BlockSpec((chunk * nx, lanes), lambda i: (i, 0)),
        out_shape=jax.ShapeDtypeStruct((count * nx, lanes), jnp.float32),
        compiler_params=params(),
        cost_estimate=cost(2 * count * nx * lanes, 12 * count * nx * lanes),
        name="write_dist",
    )(place, got, entry, decay, source)


def stages_of(n):
    out, bit = [], 1
    while bit < n:
        if bit * 4 <= n:
            out.append((bit, 2 * bit, 3 * bit))
            bit *= 4
        else:
            out.append((bit,))
            bit *= 2
    return out


def exchange(a, axis, mask):
    n = lax.axis_size(axis)
    return lax.ppermute(a, axis, [(i, i ^ mask) for i in range(n)])


def partial_sums(a, axis, beside=()):
    n = lax.axis_size(axis)
    beside = list(beside)
    if n & (n - 1) or n == 1:
        total = lax.psum(a, axis)
        return (total, jnp.zeros_like(total)), [f(a) for f in beside]
    stages = stages_of(n)
    done = []
    for i, masks in enumerate(stages):
        got = [exchange(a, axis, m) for m in masks]
        take = beside if i == len(stages) - 1 else beside[:1]
        beside = beside[len(take) :]
        made = [f(a) for f in take]
        got, made = lax.optimization_barrier((got, made))
        done += made
        other = functools.reduce(jnp.add, got)
        if i == len(stages) - 1:
            return (a, other), done
        a = a + other


def hop(face, side, step):
    n = lax.axis_size("gx")
    up = [(step, step + 1)]
    down = [(n - 1 - step, n - 2 - step)]
    if n % 2 == 0:
        return lax.ppermute(face, "gx", up + down)
    return jnp.where(side[0] == 1, lax.ppermute(face, "gx", up), lax.ppermute(face, "gx", down))


def local(total, dist, inflow, speed_x, transverse, quad_weight, side):
    count, nx, lanes = dist.shape
    flat = dist.reshape(count * nx, lanes)
    side_row = side.reshape(1, count)
    speed = speed_x.reshape(1, count)
    weight = quad_weight.reshape(1, count)
    partial, table = old_moments(total, nx, side_row, speed, transverse, weight, flat)

    def slope_part(half, halves):
        def make(sent):
            args = lax.optimization_barrier((side_row, speed, transverse, flat, sent))[:4]
            return slopes(nx, half, halves, *args)

        return make

    n = lax.axis_size("gx")
    halves = 2 if count % 256 == 0 else 1
    parts = [slope_part(h, halves) for h in range(halves)]
    (ma, mb), made = partial_sums(partial, "vert", parts)
    decay, source, face, last_decay, last_source, place = maps(
        nx, ma, mb, [m[1] for m in made], [m[0] for m in made], inflow
    )
    got, entry = inflow, inflow
    for step in range(n - 1):
        if step > 0:
            entry, face = pass_face(step, place, got, entry, last_decay, last_source)
        got = hop(face, side, step)
    new_partial = new_moments(nx, n - 1, (place, got, entry), table, decay, source)

    def write(sent):
        args = lax.optimization_barrier((place, got, entry, decay, source, sent))[:5]
        return write_dist(nx, n - 1, *args)

    (na, nb), (new_flat,) = partial_sums(new_partial, "vert", [write])
    return new_flat.reshape(count, nx, lanes), (na + nb).reshape(NMOM, nx, lanes)


def solution(mesh):
    def whole(dist, inflow, speed_x, transverse, quad_weight, side):
        body = functools.partial(local, dist.shape[0])
        return jax.shard_map(
            body,
            mesh=mesh,
            in_specs=(P("vert", "gx", None), P("vert", None), P("vert"), P(None, "vert"), P("vert"), P("vert")),
            out_specs=(P("vert", "gx", None), P(None, "gx", None)),
            check_vma=False,
        )(dist, inflow, speed_x, transverse, quad_weight, side)

    return whole
```

time: 60 us -> 46.3 us (0.77)
  local copies, waits for them, and re-layouts: 8.27 us -> 0.02 us
  waiting for transfers between devices: 20.1 us -> 14.3 us
  other arithmetic: 2.92 us -> 0.67 us
  starting transfers between devices: 14.5 us -> 16.6 us
  Pallas kernels: 12.4 us -> 13.7 us
  between operations: 1.45 us -> 0.78 us
    unnamed x22 -> x10, local copies, waits for them, and re-layouts: 7.24 us -> 0.02 us
    ppermute x8, waiting for transfers between devices: 11.3 us -> 4.27 us  [exchange(): return lax.ppermute(a, axis, [(i, i ^ mask) for i in range(n)])]
    add x4 -> x2, other arithmetic: 2.25 us -> 0.04 us  [partial_sums(): a = a + other]
    ppermute x8, starting transfers between devices: 11.2 us -> 13.3 us  [exchange(): return lax.ppermute(a, axis, [(i, i ^ mask) for i in range(n)])]
    pallas_call x4 -> x8, Pallas kernels: 12.4 us -> 13.7 us  [the longest x2 5.24 us: slopes(): pl.pallas_call(functools.partial(slope_kernel, nx), grid=(steps,), in_spe...]
    ppermute x3, waiting for transfers between devices: 8.82 us -> 10 us  [hop(): return lax.ppermute(face, 'gx', up + down)]
    slice x2 -> x0, local copies, waits for them, and re-layouts: 1.02 us -> none  [the longest x1 0.51 us: local(): forward = side[0] == 1]
  transfers between devices with their start and end apart: 11 -> 11, of which waited for: 8 -> 6; matrix products, arithmetic and copies ran while one was open for 2% -> 0% of each run, Pallas kernels for 9% -> 16%
where the time goes in v1:
time: 46.3 us; the launch traced here: 46.1 us
  starting transfers between devices  16.6 us (36%)
  waiting for transfers between devices  14.3 us (31%)
  Pallas kernels  13.7 us (30%)
  between operations  0.78 us (2%)
  other arithmetic  0.67 us (1%)
    ppermute x8, starting transfers between devices, exchange(): return lax.ppermute(a, axis, [(i, i ^ mask) for i in range(n)])  13.3 us
    ppermute x3, waiting for transfers between devices, hop(): return lax.ppermute(face, 'gx', up + down)  10 us
    pallas_call x2, Pallas kernels, slopes(): pl.pallas_call(functools.partial(slope_kernel, nx), grid=(steps,), in_spe...  5.24 us
    ppermute x8, waiting for transfers between devices, exchange(): return lax.ppermute(a, axis, [(i, i ^ mask) for i in range(n)])  4.27 us
    ppermute x3, starting transfers between devices, hop(): return lax.ppermute(face, 'gx', up + down)  3.28 us
    pallas_call x1, Pallas kernels, maps(): pl.pallas_call(functools.partial(map_kernel, nx, halves), in_specs=[whole...  3.15 us
    pallas_call x1, Pallas kernels, write_dist(): pl.pallas_call(functools.partial(write_kernel, nx, step), grid=(count //...  2.28 us
    pallas_call x1, Pallas kernels, old_moments(): pl.pallas_call(functools.partial(moments_kernel, total, nx, chunks), in_s...  2.22 us
  transfers between devices with their start and end apart: 11, of which 6 were waited for; matrix products, arithmetic and copies ran while one was open for 0% of the time, Pallas kernels for 16%

profile of v1, /device:TPU:0, one launch (start us, length us, event | category | flops | bytes accessed | tf_op | source)
XLA Modules:
  0.0 46.1 jit_solution(15259495068617450442)
XLA Ops:
  0.6 0.0 copy-start.2
  0.6 0.0 copy-start.3
  0.7 0.0 copy-start.4
  0.7 0.0 copy-start
  0.7 2.2 %moments.1 = (f32[104,128]{1,0:T(8,128)S(1)}, bf16[32,512]{1,0:T(8,128)(2,1)S(1)}) custom-call(s32[1,512]{1,0:T(1,128)} %bitcast.10, f32[1,512]{1,0:T(1,128)} %bitcast.13, f32[2,512]{1,0:T(2,128)} %cross_ref.1, f32[1,512]{1,0:T(1,128)} %bitcast.17, f32[4096,128]{1,0:T(8,128)} %bitcast.7), custom_call_target="tpu_custom_call" | custom-call | flops 50331648 | bytes 2097152 | tf_op jit(solution)/shard_map/moments/pallas_call | solution.py:86
  2.9 0.0 copy-start.1
  2.9 4.0 %collective-permute-start.2 = (f32[104,128]{1,0:T(8,128)S(1)}, f32[104,128]{1,0:T(8,128)S(1)}, u32[]{:S(2)}, u32[]{:S(2)}) collective-permute-start(f32[104,128]{1,0:T(8,128)S(1)} %get-tuple-element.43), channel_id=1, source_target_pairs={{0,3},{1,2},{2,1},{3,0},{4,7},{5,6},{6,5},{7,4},{8,11},{9,10},{10,... | collective-permute-start | bytes 159752 | tf_op jit(solution)/shard_map/ppermute | solution.py:337
  6.9 0.4 collective-permute-start.1
  7.4 0.2 collective-permute-start
  7.6 0.0 copy-done.2
  7.6 0.0 copy-done.3
  7.6 0.0 copy-done.4
  7.6 0.0 copy-done
  7.6 2.6 %slope.2 = (f32[8,256,128]{2,1,0:T(8,128)S(1)}, f32[3,256,128]{2,1,0:T(8,128)S(1)}) custom-call(s32[1,512]{1,0:T(1,128)S(1)} %bitcast.11, f32[1,512]{1,0:T(1,128)S(1)} %bitcast.14, f32[2,512]{1,0:T(2,128)S(1)} %copy-done.2, f32[4096,128]{1,0:T(8,128)S(1)} %bitcast.8), custom_call_target="tpu_custom_call" | custom-call | flops 5242880 | bytes 2097152 | tf_op jit(solution)/shard_map/slope/pallas_call | solution.py:143
  10.2 0.0 collective-permute-done.2
  10.2 0.8 %collective-permute-done.1 = f32[104,128]{1,0:T(8,128)S(1)} collective-permute-done((f32[104,128]{1,0:T(8,128)S(1)}, f32[104,128]{1,0:T(8,128)S(1)}, u32[]{:S(2)}, u32[]{:S(2)}) %collective-permute-start.1) | collective-permute-done | bytes 53280 | tf_op jit(solution)/shard_map/ppermute | solution.py:337
  11.1 0.4 collective-permute-done
  11.5 2.7 %collective-permute-start.3 = (f32[104,128]{1,0:T(8,128)S(1)}, f32[104,128]{1,0:T(8,128)S(1)}, u32[]{:S(2)}, u32[]{:S(2)}) collective-permute-start(f32[104,128]{1,0:T(8,128)S(1)} %add_add_fusion.1.ma_ref), channel_id=1, source_target_pairs={{0,4},{1,5},{2,6},{3,7},{4,0},{5,1},{6,2},{7,3},{8,12},{9,13},{10,... | collective-permute-start | bytes 159752 | tf_op jit(solution)/shard_map/ppermute | solution.py:337
  14.2 2.6 %slope.3 = (f32[8,256,128]{2,1,0:T(8,128)S(1)}, f32[3,256,128]{2,1,0:T(8,128)S(1)}) custom-call(s32[1,512]{1,0:T(1,128)S(1)} %bitcast.12, f32[1,512]{1,0:T(1,128)S(1)} %bitcast.15, f32[2,512]{1,0:T(2,128)S(1)} %copy-done.2, f32[4096,128]{1,0:T(8,128)S(1)} %bitcast.9), custom_call_target="tpu_custom_call" | custom-call | flops 5242880 | bytes 2097152 | tf_op jit(solution)/shard_map/slope/pallas_call | solution.py:143
  16.8 0.0 collective-permute-done.3.mb_ref
  16.8 0.0 copy-done.1
  16.8 3.1 %maps.1 = (f32[8,512,128]{2,1,0:T(8,128)S(1)}, f32[8,512,128]{2,1,0:T(8,128)S(1)}, f32[512,128]{1,0:T(8,128)S(1)}, f32[512,128]{1,0:T(8,128)S(1)}, f32[512,128]{1,0:T(8,128)S(1)}, /*index=5*/s32[8,128]{1,0:T(8,128)S(1)}) custom-call(f32[104,128]{1,0:T(8,128)S(1)} %add_add_fusion.1.ma_ref, f32[104,128]{1,0:T(8,128)S(1)} %collective-permute-done.3.mb_ref, ...), custom_call_target="tpu_custom_call" | custom-call | flops 20971520 | bytes 6291456 | tf_op jit(solution)/shard_map/maps/pallas_call | solution.py:237
  20.0 1.3 %collective-permute-start.4 = (f32[512,128]{1,0:T(8,128)S(1)}, f32[512,128]{1,0:T(8,128)S(1)}, u32[]{:S(2)}, u32[]{:S(2)}) collective-permute-start(f32[512,128]{1,0:T(8,128)S(1)} %get-tuple-element.65), channel_id=1, source_target_pairs={{0,8},{24,16},{1,9},{25,17},{2,10},{26,18},{3,11},{27,19},{4,12},{... | collective-permute-start | bytes 786440 | tf_op jit(solution)/shard_map/ppermute | solution.py:366
  21.3 1.1 %collective-permute-done.4.got_ref = f32[512,128]{1,0:T(8,128)S(1)} collective-permute-done((f32[512,128]{1,0:T(8,128)S(1)}, f32[512,128]{1,0:T(8,128)S(1)}, u32[]{:S(2)}, u32[]{:S(2)}) %collective-permute-start.4) | collective-permute-done | bytes 262176 | tf_op jit(solution)/shard_map/ppermute | solution.py:366
  22.4 0.1 face.2
  22.5 0.7 %collective-permute-start.5 = (f32[512,128]{1,0:T(8,128)S(1)}, f32[512,128]{1,0:T(8,128)S(1)}, u32[]{:S(2)}, u32[]{:S(2)}) collective-permute-start(f32[512,128]{1,0:T(8,128)S(1)} %get-tuple-element.68), channel_id=1, source_target_pairs={{8,16},{16,8},{9,17},{17,9},{10,18},{18,10},{11,19},{19,11},{12,20... | collective-permute-start | bytes 786440 | tf_op jit(solution)/shard_map/ppermute | solution.py:366
  23.2 0.0 collective-permute-done.5.got_ref
  23.2 0.1 face.3
  23.3 1.3 %collective-permute-start.6 = (f32[512,128]{1,0:T(8,128)S(1)}, f32[512,128]{1,0:T(8,128)S(1)}, u32[]{:S(2)}, u32[]{:S(2)}) collective-permute-start(f32[512,128]{1,0:T(8,128)S(1)} %get-tuple-element.70), channel_id=1, source_target_pairs={{16,24},{8,0},{17,25},{9,1},{18,26},{10,2},{19,27},{11,3},{20,28},... | collective-permute-start | bytes 786440 | tf_op jit(solution)/shard_map/ppermute | solution.py:366
  24.6 8.9 %collective-permute-done.6.got_ref = f32[512,128]{1,0:T(8,128)S(1)} collective-permute-done((f32[512,128]{1,0:T(8,128)S(1)}, f32[512,128]{1,0:T(8,128)S(1)}, u32[]{:S(2)}, u32[]{:S(2)}) %collective-permute-start.6) | collective-permute-done | bytes 262176 | tf_op jit(solution)/shard_map/ppermute | solution.py:366
  33.5 0.7 %new_moments.1 = f32[104,128]{1,0:T(8,128)S(1)} custom-call(s32[8,128]{1,0:T(8,128)S(1)} %get-tuple-element.75.place_ref, f32[512,128]{1,0:T(8,128)S(1)} %collective-permute-done.6.got_ref, f32[512,128]{1,0:T(8,128)S(1)} %get-tuple-element.77.entry_ref, bf16[32,512]{1,0:T(8,128)(2,1)S(1)} %get-tuple-element.72.table_ref, ...), custom_call_target="tpu_custom_call" | custom-call | flops 50331648 | bytes 4194304 | tf_op jit(solution)/shard_map/new_moments/pallas_call | solution.py:288
  34.1 1.6 %collective-permute-start.9 = (f32[104,128]{1,0:T(8,128)S(1)}, f32[104,128]{1,0:T(8,128)S(1)}, u32[]{:S(2)}, u32[]{:S(2)}) collective-permute-start(f32[104,128]{1,0:T(8,128)S(1)} %new_moments.1), channel_id=1, source_target_pairs={{0,3},{1,2},{2,1},{3,0},{4,7},{5,6},{6,5},{7,4},{8,11},{9,10},{10,... | collective-permute-start | bytes 159752 | tf_op jit(solution)/shard_map/ppermute | solution.py:337
  35.7 0.4 collective-permute-start.8
  36.2 1.4 %collective-permute-start.7 = (f32[104,128]{1,0:T(8,128)S(1)}, f32[104,128]{1,0:T(8,128)S(1)}, u32[]{:S(2)}, u32[]{:S(2)}) collective-permute-start(f32[104,128]{1,0:T(8,128)S(1)} %new_moments.1), channel_id=1, source_target_pairs={{0,1},{1,0},{2,3},{3,2},{4,5},{5,4},{6,7},{7,6},{8,9},{9,8},{10,11... | collective-permute-start | bytes 159752 | tf_op jit(solution)/shard_map/ppermute | solution.py:337
  37.6 2.3 %write_dist.1 = f32[4096,128]{1,0:T(8,128)} custom-call(s32[8,128]{1,0:T(8,128)S(1)} %get-tuple-element.75.place_ref, f32[512,128]{1,0:T(8,128)S(1)} %collective-permute-done.6.got_ref, f32[512,128]{1,0:T(8,128)S(1)} %get-tuple-element.77.entry_ref, f32[8,512,128]{2,1,0:T(8,128)S(1)} %get-tuple-element.78.decay_ref, ...), custom_call_target="tpu_custom_call" | custom-call | flops 1048576 | bytes 6291456 | tf_op jit(solution)/shard_map/write_dist/pallas_call | solution.py:311
  39.9 0.0 collective-permute-done.9
  39.9 0.0 collective-permute-done.8
  39.9 0.4 collective-permute-done.7
  40.3 2.5 %collective-permute-start.10 = (f32[104,128]{1,0:T(8,128)S(1)}, f32[104,128]{1,0:T(8,128)S(1)}, u32[]{:S(2)}, u32[]{:S(2)}) collective-permute-start(f32[104,128]{1,0:T(8,128)S(1)} %add_add_fusion), channel_id=1, source_target_pairs={{0,4},{1,5},{2,6},{3,7},{4,0},{5,1},{6,2},{7,3},{8,12},{9,13},{10,... | collective-permute-start | bytes 159752 | tf_op jit(solution)/shard_map/ppermute | solution.py:337
  42.9 2.6 %collective-permute-done.10 = f32[104,128]{1,0:T(8,128)S(1)} collective-permute-done((f32[104,128]{1,0:T(8,128)S(1)}, f32[104,128]{1,0:T(8,128)S(1)}, u32[]{:S(2)}, u32[]{:S(2)}) %collective-permute-start.10) | collective-permute-done | bytes 53280 | tf_op jit(solution)/shard_map/ppermute | solution.py:337
  45.4 0.6 %add_bitcast_fusion = f32[13,8,128]{2,1,0:T(8,128)} fusion(f32[104,128]{1,0:T(8,128)S(1)} %add_add_fusion, f32[104,128]{1,0:T(8,128)S(1)} %collective-permute-done.10), kind=kLoop, calls=%fused_computation | loop fusion | flops 13312 | bytes 159744 | tf_op jit(solution)/shard_map/reshape | solution.py:404
  (2 shorter events, 0.0 us)
Async XLA Ops:
  0.6 6.9 %copy-start.2 = (f32[2,512]{1,0:T(2,128)S(1)}, f32[2,512]{1,0:T(2,128)}, u32[]{:S(2)}) copy-start(f32[2,512]{1,0:T(2,128)} %cross_ref.1) | copy-start | bytes 12292
  0.6 6.9 %copy-start.3 = (s32[512]{0:T(512)S(1)}, s32[512]{0:T(512)}, u32[]{:S(2)}) copy-start(s32[512]{0:T(512)} %param.11) | copy-start | bytes 6148
  0.7 6.9 %copy-start.4 = (f32[512]{0:T(512)S(1)}, f32[512]{0:T(512)}, u32[]{:S(2)}) copy-start(f32[512]{0:T(512)} %param.8) | copy-start | bytes 6148
  0.7 6.9 %copy-start = (f32[512,8,128]{2,1,0:T(8,128)S(1)}, f32[512,8,128]{2,1,0:T(8,128)}, u32[]{:S(2)}) copy-start(f32[512,8,128]{2,1,0:T(8,128)} %param.6) | copy-start | bytes 6291460
  2.9 13.9 %copy-start.1 = (f32[512,128]{1,0:T(8,128)S(1)}, f32[512,128]{1,0:T(8,128)}, u32[]{:S(2)}) copy-start(f32[512,128]{1,0:T(8,128)} %entry_ref.1) | copy-start | bytes 786436
  2.9 7.3 %collective-permute-start.2 = (f32[104,128]{1,0:T(8,128)S(1)}, f32[104,128]{1,0:T(8,128)S(1)}, u32[]{:S(2)}, u32[]{:S(2)}) collective-permute-start(f32[104,128]{1,0:T(8,128)S(1)} %get-tuple-element.43), channel_id=1, source_target_pairs={{0,3},{1,2},{2,1},{3,0},{4,7},{5,6},{6,5},{7,4},{8,11},{9,10},{10,... | collective-permute-start | bytes 159752 | tf_op jit(solution)/shard_map/ppermute | solution.py:337
  6.9 4.1 %collective-permute-start.1 = (f32[104,128]{1,0:T(8,128)S(1)}, f32[104,128]{1,0:T(8,128)S(1)}, u32[]{:S(2)}, u32[]{:S(2)}) collective-permute-start(f32[104,128]{1,0:T(8,128)S(1)} %get-tuple-element.43), channel_id=1, source_target_pairs={{0,2},{1,3},{2,0},{3,1},{4,6},{5,7},{6,4},{7,5},{8,10},{9,11},{10,... | collective-permute-start | bytes 159752 | tf_op jit(solution)/shard_map/ppermute | solution.py:337
  7.4 4.1 %collective-permute-start = (f32[104,128]{1,0:T(8,128)S(1)}, f32[104,128]{1,0:T(8,128)S(1)}, u32[]{:S(2)}, u32[]{:S(2)}) collective-permute-start(f32[104,128]{1,0:T(8,128)S(1)} %get-tuple-element.43), channel_id=1, source_target_pairs={{0,1},{1,0},{2,3},{3,2},{4,5},{5,4},{6,7},{7,6},{8,9},{9,8},{10,11... | collective-permute-start | bytes 159752 | tf_op jit(solution)/shard_map/ppermute | solution.py:337
  11.5 5.3 %collective-permute-start.3 = (f32[104,128]{1,0:T(8,128)S(1)}, f32[104,128]{1,0:T(8,128)S(1)}, u32[]{:S(2)}, u32[]{:S(2)}) collective-permute-start(f32[104,128]{1,0:T(8,128)S(1)} %add_add_fusion.1.ma_ref), channel_id=1, source_target_pairs={{0,4},{1,5},{2,6},{3,7},{4,0},{5,1},{6,2},{7,3},{8,12},{9,13},{10,... | collective-permute-start | bytes 159752 | tf_op jit(solution)/shard_map/ppermute | solution.py:337
  20.0 2.4 %collective-permute-start.4 = (f32[512,128]{1,0:T(8,128)S(1)}, f32[512,128]{1,0:T(8,128)S(1)}, u32[]{:S(2)}, u32[]{:S(2)}) collective-permute-start(f32[512,128]{1,0:T(8,128)S(1)} %get-tuple-element.65), channel_id=1, source_target_pairs={{0,8},{24,16},{1,9},{25,17},{2,10},{26,18},{3,11},{27,19},{4,12},{... | collective-permute-start | bytes 786440 | tf_op jit(solution)/shard_map/ppermute | solution.py:366
  22.5 0.7 %collective-permute-start.5 = (f32[512,128]{1,0:T(8,128)S(1)}, f32[512,128]{1,0:T(8,128)S(1)}, u32[]{:S(2)}, u32[]{:S(2)}) collective-permute-start(f32[512,128]{1,0:T(8,128)S(1)} %get-tuple-element.68), channel_id=1, source_target_pairs={{8,16},{16,8},{9,17},{17,9},{10,18},{18,10},{11,19},{19,11},{12,20... | collective-permute-start | bytes 786440 | tf_op jit(solution)/shard_map/ppermute | solution.py:366
  23.3 10.2 %collective-permute-start.6 = (f32[512,128]{1,0:T(8,128)S(1)}, f32[512,128]{1,0:T(8,128)S(1)}, u32[]{:S(2)}, u32[]{:S(2)}) collective-permute-start(f32[512,128]{1,0:T(8,128)S(1)} %get-tuple-element.70), channel_id=1, source_target_pairs={{16,24},{8,0},{17,25},{9,1},{18,26},{10,2},{19,27},{11,3},{20,28},... | collective-permute-start | bytes 786440 | tf_op jit(solution)/shard_map/ppermute | solution.py:366
  34.1 5.8 %collective-permute-start.9 = (f32[104,128]{1,0:T(8,128)S(1)}, f32[104,128]{1,0:T(8,128)S(1)}, u32[]{:S(2)}, u32[]{:S(2)}) collective-permute-start(f32[104,128]{1,0:T(8,128)S(1)} %new_moments.1), channel_id=1, source_target_pairs={{0,3},{1,2},{2,1},{3,0},{4,7},{5,6},{6,5},{7,4},{8,11},{9,10},{10,... | collective-permute-start | bytes 159752 | tf_op jit(solution)/shard_map/ppermute | solution.py:337
  35.7 4.2 %collective-permute-start.8 = (f32[104,128]{1,0:T(8,128)S(1)}, f32[104,128]{1,0:T(8,128)S(1)}, u32[]{:S(2)}, u32[]{:S(2)}) collective-permute-start(f32[104,128]{1,0:T(8,128)S(1)} %new_moments.1), channel_id=1, source_target_pairs={{0,2},{1,3},{2,0},{3,1},{4,6},{5,7},{6,4},{7,5},{8,10},{9,11},{10,... | collective-permute-start | bytes 159752 | tf_op jit(solution)/shard_map/ppermute | solution.py:337
  36.2 4.1 %collective-permute-start.7 = (f32[104,128]{1,0:T(8,128)S(1)}, f32[104,128]{1,0:T(8,128)S(1)}, u32[]{:S(2)}, u32[]{:S(2)}) collective-permute-start(f32[104,128]{1,0:T(8,128)S(1)} %new_moments.1), channel_id=1, source_target_pairs={{0,1},{1,0},{2,3},{3,2},{4,5},{5,4},{6,7},{7,6},{8,9},{9,8},{10,11... | collective-permute-start | bytes 159752 | tf_op jit(solution)/shard_map/ppermute | solution.py:337
  40.3 5.1 %collective-permute-start.10 = (f32[104,128]{1,0:T(8,128)S(1)}, f32[104,128]{1,0:T(8,128)S(1)}, u32[]{:S(2)}, u32[]{:S(2)}) collective-permute-start(f32[104,128]{1,0:T(8,128)S(1)} %add_add_fusion), channel_id=1, source_target_pairs={{0,4},{1,5},{2,6},{3,7},{4,0},{5,1},{6,2},{7,3},{8,12},{9,13},{10,... | collective-permute-start | bytes 159752 | tf_op jit(solution)/shard_map/ppermute | solution.py:337

commit v2 on v1

--- a/solution.py
+++ b/solution.py
@@ -37,7 +37,7 @@
 
 
 def moments_kernel(total, nx, chunks, side_hbm, speed_hbm, cross_hbm, weight_hbm, dist_hbm,
-                   mom_ref, table_ref, side_ref, speed_ref, cross_ref, weight_ref, dist_ref, sems):
+                   mom_ref, table_ref, rows_ref, dist_ref, side_ref, speed_ref, cross_ref, weight_ref, sems):
     count = speed_ref.shape[1]
     chunk = count // chunks
     small = [(side_hbm, side_ref), (speed_hbm, speed_ref), (cross_hbm, cross_ref), (weight_hbm, weight_ref)]
@@ -56,6 +56,7 @@
     z = cross_ref[1:2, :]
     xx, yy, zz = x * x, y * y, z * z
     square = xx + yy + zz
+    rows_ref[...] = jnp.concatenate([x, y, z] + [jnp.zeros_like(x)] * 5, axis=0)
     rows = [jnp.ones_like(x), x, y, z, xx, yy, zz, x * y, x * z, y * z, x * square, y * square, z * square]
     rows += [jnp.zeros_like(x)] * (ROWS - NMOM)
     full = jnp.concatenate(rows, axis=0) * (weight_ref[...] * (1.0 / total))
@@ -81,22 +82,23 @@
 
 def old_moments(total, nx, side, speed, cross, weight, dist):
     count, lanes = speed.shape[1], dist.shape[1]
-    chunks = max(1, count // 256)
+    chunks = max(1, count // 128)
     whole = pl.BlockSpec(memory_space=pltpu.VMEM)
     return pl.pallas_call(
         functools.partial(moments_kernel, total, nx, chunks),
         in_specs=[pl.BlockSpec(memory_space=pltpu.HBM)] * 5,
-        out_specs=[whole] * 2,
+        out_specs=[whole] * 4,
         out_shape=[
-            jax.ShapeDtypeStruct((NMOM * nx, lanes), jnp.float32),
-            jax.ShapeDtypeStruct((2 * ROWS, count), jnp.bfloat16),
+            pltpu.VMEM((NMOM * nx, lanes), jnp.float32),
+            pltpu.VMEM((2 * ROWS, count), jnp.bfloat16),
+            pltpu.VMEM((8, count), jnp.float32),
+            pltpu.VMEM(dist.shape, jnp.float32),
         ],
         scratch_shapes=[
             pltpu.VMEM(side.shape, jnp.int32),
             pltpu.VMEM(speed.shape, jnp.float32),
             pltpu.VMEM(cross.shape, jnp.float32),
             pltpu.VMEM(weight.shape, jnp.float32),
-            pltpu.VMEM(dist.shape, jnp.float32),
             pltpu.SemaphoreType.DMA((chunks + 4,)),
         ],
         compiler_params=params(),
@@ -105,13 +107,10 @@
     )(*[pltpu.with_memory_space_constraint(a, pltpu.HBM) for a in (side, speed, cross, weight, dist)])
 
 
-def slope_kernel(nx, side_ref, speed_ref, cross_ref, dist_ref, slope_ref, comp_ref):
-    count = speed_ref.shape[1]
+def slope_kernel(nx, start, rows_ref, dist_ref, slope_ref, comp_ref):
+    count = slope_ref.shape[1]
     lanes = dist_ref.shape[1]
-    speed = speed_ref[...]
-    x = jnp.where(side_ref[...] == 1, speed, -speed)
-    stacked = jnp.concatenate([x, cross_ref[...], jnp.zeros((5, count), jnp.float32)], axis=0)
-    columns = jnp.transpose(stacked)
+    columns = jnp.transpose(rows_ref[:, start : start + count])
     for k in range(3):
         comp_ref[k] = jnp.broadcast_to(columns[:, k : k + 1], (count, lanes))
     group = 32
@@ -126,7 +125,7 @@
         ay, az = KAPPA_CELL * jnp.abs(y), KAPPA_CELL * jnp.abs(z)
         both = ay + az
         for i in range(nx):
-            d = dist_ref[pl.ds(at * nx + i, group, stride=nx), :]
+            d = dist_ref[pl.ds((start + at) * nx + i, group, stride=nx), :]
             near_y = jnp.take_along_axis(d, from_y, axis=1)
             near_z = jnp.take_along_axis(d, from_z, axis=1)
             slope_ref[i, pl.ds(at, group), :] = both * d - ay * near_y - az * near_z
@@ -135,36 +134,28 @@
     lax.fori_loop(0, count // group, one, 0)
 
 
-def slopes(nx, half, halves, side, speed, cross, dist):
-    count, lanes = speed.shape[1] // halves, dist.shape[1]
-    chunk = min(count, 128)
-    steps = count // chunk
-    vec = lambda r: pl.BlockSpec((r, chunk), lambda i: (0, half * steps + i))
-    return pl.pallas_call(
-        functools.partial(slope_kernel, nx),
-        grid=(steps,),
-        in_specs=[vec(1), vec(1), vec(2), pl.BlockSpec((chunk * nx, lanes), lambda i: (half * steps + i, 0))],
-        out_specs=[
-            pl.BlockSpec((nx, chunk, lanes), lambda i: (0, i, 0)),
-            pl.BlockSpec((3, chunk, lanes), lambda i: (0, i, 0)),
-        ],
+def slopes(nx, half, halves, rows, dist):
+    count, lanes = rows.shape[1] // halves, dist.shape[1]
+    whole = pl.BlockSpec(memory_space=pltpu.VMEM)
+    return pl.pallas_call(
+        functools.partial(slope_kernel, nx, half * count),
+        in_specs=[whole] * 2,
+        out_specs=[whole] * 2,
         out_shape=[
-            jax.ShapeDtypeStruct((nx, count, lanes), jnp.float32),
-            jax.ShapeDtypeStruct((3, count, lanes), jnp.float32),
+            pltpu.VMEM((nx, count, lanes), jnp.float32),
+            pltpu.VMEM((3, count, lanes), jnp.float32),
         ],
         compiler_params=params(),
         cost_estimate=cost(20 * count * nx * lanes, 8 * count * nx * lanes),
         name="slope",
-    )(side, speed, cross, dist)
+    )(rows, dist)
 
 
 def map_kernel(nx, halves, ma_ref, mb_ref, *refs):
     comps, slopes_in = refs[:halves], refs[halves : 2 * halves]
-    inflow_ref, decay_ref, source_ref, face_ref, last_decay_ref, last_source_ref, place_ref, state = refs[2 * halves :]
-    here, there = lax.axis_index("gx"), lax.axis_size("gx") - 1 - lax.axis_index("gx")
-    place_ref[...] = jnp.where(comps[0][0, 0:8, :] > 0, here, there)
-    lanes = inflow_ref.shape[1]
-    count = inflow_ref.shape[0]
+    decay_ref, source_ref, send_ref, sign_ref, state = refs[2 * halves :]
+    count, lanes = decay_ref.shape[1:]
+    sign_ref[...] = comps[0][0, 0:8, :]
     m = [ma_ref[k * nx : (k + 1) * nx, :] + mb_ref[k * nx : (k + 1) * nx, :] for k in range(NMOM)]
     n = m[0]
     inv_n = 1.0 / n
@@ -219,59 +210,170 @@
                     decay = decay * decay_ref[before, rows, :]
                 decay_ref[at_x, rows, :] = decay
                 source_ref[at_x, rows, :] = source
-                if j == nx - 1:
-                    last_decay_ref[rows, :] = decay
-                    last_source_ref[rows, :] = source
-                    face_ref[rows, :] = decay * inflow_ref[rows, :] + source
                 return carry
 
             lax.fori_loop(0, part // group, one, 0)
 
-
-def maps(nx, ma, mb, comps, slopes_in, inflow):
-    count, lanes = inflow.shape
+    last = jnp.where(forward, nx - 1, 0)
+    theirs = pl.ds(pl.multiple_of((1 - lax.axis_index("gx") % 2) * (count // 2), count // 2), count // 2)
+    send_ref[0] = decay_ref[last, theirs, :]
+    send_ref[1] = source_ref[last, theirs, :]
+
+
+def maps(nx, ma, mb, comps, slopes_in):
+    lanes = ma.shape[1]
     halves = len(comps)
+    count = halves * comps[0].shape[1]
     whole = pl.BlockSpec(memory_space=pltpu.VMEM)
     field = pltpu.VMEM((nx, count, lanes), jnp.float32)
-    face = pltpu.VMEM((count, lanes), jnp.float32)
     return pl.pallas_call(
         functools.partial(map_kernel, nx, halves),
-        in_specs=[whole] * (3 + 2 * halves),
-        out_specs=[whole] * 6,
-        out_shape=[field, field, face, face, face, pltpu.VMEM((8, lanes), jnp.int32)],
+        in_specs=[whole] * (2 + 2 * halves),
+        out_specs=[whole] * 4,
+        out_shape=[
+            field,
+            field,
+            pltpu.VMEM((2, count // 2, lanes), jnp.float32),
+            pltpu.VMEM((8, lanes), jnp.float32),
+        ],
         scratch_shapes=[pltpu.VMEM((10, nx, lanes), jnp.float32)],
         compiler_params=params(),
         cost_estimate=cost(40 * count * nx * lanes, 12 * count * nx * lanes),
         name="maps",
-    )(ma, mb, *comps, *slopes_in, inflow)
-
-
-def entry_of(step, place_ref, got_ref, entry_ref):
-    return jnp.where(place_ref[0:1, :] == step, got_ref[...], entry_ref[...])
-
-
-def face_kernel(step, place_ref, got_ref, entry_ref, decay_ref, source_ref, next_ref, face_ref):
-    entry = entry_of(step, place_ref, got_ref, entry_ref)
+    )(ma, mb, *comps, *slopes_in)
+
+
+def standing(sign_ref):
+    place, chips = lax.axis_index("gx"), lax.axis_size("gx") // 2
+    chip, core = place // 2, place % 2
+    forward = sign_ref[0:1, :] > 0
+    return jnp.where(forward, core, 1 - core) == 0, jnp.where(forward, chip, chips - 1 - chip)
+
+
+def half_of(ref_rows, which):
+    half = ref_rows // 2
+    return pl.ds(pl.multiple_of(which * half, half), half)
+
+
+def compose_kernel(nx, sign_ref, got_ref, decay_ref, source_ref, inflow_ref, near_ref, face_ref, entry_ref, *chip_ref):
+    first, _ = standing(sign_ref)
+    core = lax.axis_index("gx") % 2
+    mine = half_of(inflow_ref.shape[0], core)
+    last = jnp.where(sign_ref[0:1, 0:1][0, 0] > 0, nx - 1, 0)
+    decay, source = decay_ref[last, mine, :], source_ref[last, mine, :]
+    got_decay, got_source = got_ref[0], got_ref[1]
+    near_decay = jnp.where(first, decay, got_decay)
+    near_source = jnp.where(first, source, got_source)
+    far_decay = jnp.where(first, got_decay, decay)
+    far_source = jnp.where(first, got_source, source)
+    chip_decay, chip_source = far_decay * near_decay, far_decay * near_source + far_source
+    near_ref[0], near_ref[1] = near_decay, near_source
+    if chip_ref:
+        chip_ref[0][0], chip_ref[0][1] = chip_decay, chip_source
+    entry = inflow_ref[mine, :]
+    entry_ref[...] = entry
+    face_ref[...] = chip_decay * entry + chip_source
+
+
+def compose_chip(nx, sign, got, decay, source, inflow):
+    _, half, lanes = got.shape
+    whole = pl.BlockSpec(memory_space=pltpu.VMEM)
+    pair = pltpu.VMEM((2, half, lanes), jnp.float32)
+    outs = [pair] + [pltpu.VMEM((half, lanes), jnp.float32)] * 2
+    if lax.axis_size("gx") > 4:
+        outs.append(pair)
+    return pl.pallas_call(
+        functools.partial(compose_kernel, nx),
+        in_specs=[whole] * 5,
+        out_specs=[whole] * len(outs),
+        out_shape=outs,
+        compiler_params=params(),
+        cost_estimate=cost(10 * half * lanes, 40 * half * lanes),
+        name="compose",
+    )(sign, got, decay, source, inflow)
+
+
+def pass_kernel(step, sign_ref, got_ref, entry_ref, chip_ref, next_ref, face_ref):
+    _, before = standing(sign_ref)
+    entry = jnp.where(before == step, got_ref[...], entry_ref[...])
     next_ref[...] = entry
-    face_ref[...] = decay_ref[...] * entry + source_ref[...]
-
-
-def pass_face(step, place, got, entry, decay, source):
+    face_ref[...] = chip_ref[0] * entry + chip_ref[1]
+
+
+def pass_face(step, sign, got, entry, chip):
     whole = pl.BlockSpec(memory_space=pltpu.VMEM)
     out = pltpu.VMEM(entry.shape, jnp.float32)
     return pl.pallas_call(
-        functools.partial(face_kernel, step),
-        in_specs=[whole] * 5,
+        functools.partial(pass_kernel, step),
+        in_specs=[whole] * 4,
         out_specs=[whole] * 2,
         out_shape=[out, out],
         compiler_params=params(),
-        cost_estimate=cost(2 * entry.size, 20 * entry.size),
+        cost_estimate=cost(3 * entry.size, 20 * entry.size),
         name="face",
-    )(place, got, entry, decay, source)
-
-
-def new_moments_kernel(nx, step, place_ref, got_ref, entry_ref, table_ref, decay_ref, source_ref, mom_ref):
-    entry = entry_of(step, place_ref, got_ref, entry_ref)
+    )(sign, got, entry, chip)
+
+
+def share_kernel(step, sign_ref, got_ref, entry_ref, near_ref, keep_ref, send_ref):
+    first, before = standing(sign_ref)
+    entry = jnp.where(before == step, got_ref[...], entry_ref[...])
+    middle = near_ref[0] * entry + near_ref[1]
+    keep_ref[...] = jnp.where(first, entry, middle)
+    send_ref[...] = jnp.where(first, middle, entry)
+
+
+def share_entry(step, sign, got, entry, near):
+    whole = pl.BlockSpec(memory_space=pltpu.VMEM)
+    out = pltpu.VMEM(entry.shape, jnp.float32)
+    return pl.pallas_call(
+        functools.partial(share_kernel, step),
+        in_specs=[whole] * 4,
+        out_specs=[whole] * 2,
+        out_shape=[out, out],
+        compiler_params=params(),
+        cost_estimate=cost(3 * entry.size, 20 * entry.size),
+        name="share",
+    )(sign, got, entry, near)
+
+
+def chip_exchange(a):
+    n = lax.axis_size("gx")
+    return lax.ppermute(a, "gx", [(i, i ^ 1) for i in range(n)])
+
+
+def chip_hop(face, step):
+    chips = lax.axis_size("gx") // 2
+    up, down = (step, step + 1), (chips - 1 - step, chips - 2 - step)
+    pairs = [(2 * a + c, 2 * b + c) for a, b in (up, down) for c in range(2)]
+    if chips % 2 == 0:
+        got = lax.ppermute(face, "gx", pairs)
+        return got, got
+    return lax.ppermute(face, "gx", pairs[:2]), lax.ppermute(face, "gx", pairs[2:])
+
+
+def entries(nx, sign, decay, source, send, inflow, side):
+    near, face, entry, *chip = compose_chip(nx, sign, chip_exchange(send), decay, source, inflow)
+    got = entry
+    chips = lax.axis_size("gx") // 2
+    for step in range(chips - 1):
+        if step > 0:
+            entry, face = pass_face(step, sign, got, entry, chip[0])
+        low, high = chip_hop(face, step)
+        got = low if low is high else jnp.where(side[0] == 1, low, high)
+    keep, share = share_entry(chips - 1, sign, got, entry, near)
+    return keep, chip_exchange(share)
+
+
+def whole_entry(keep_ref, got_ref, entry_ref):
+    count = entry_ref.shape[0]
+    core = lax.axis_index("gx") % 2
+    entry_ref[half_of(count, core), :] = keep_ref[...]
+    entry_ref[half_of(count, 1 - core), :] = got_ref[...]
+
+
+def new_moments_kernel(nx, keep_ref, got_ref, table_ref, decay_ref, source_ref, mom_ref, entry_ref):
+    whole_entry(keep_ref, got_ref, entry_ref)
+    entry = entry_ref[...]
     lanes = entry.shape[1]
     table = table_ref[...]
     for i in range(0, nx, 2):
@@ -282,42 +384,41 @@
             mom_ref[pl.ds(i + k, NMOM, stride=nx), :] = got[:NMOM, k * lanes : (k + 1) * lanes]
 
 
-def new_moments(nx, step, face_in, table, decay, source):
+def new_moments(nx, keep, got, table, decay, source):
     count, lanes = decay.shape[1:]
     whole = pl.BlockSpec(memory_space=pltpu.VMEM)
     return pl.pallas_call(
-        functools.partial(new_moments_kernel, nx, step),
-        in_specs=[whole] * 6,
-        out_specs=whole,
-        out_shape=jax.ShapeDtypeStruct((NMOM * nx, lanes), jnp.float32),
+        functools.partial(new_moments_kernel, nx),
+        in_specs=[whole] * 5,
+        out_specs=[whole] * 2,
+        out_shape=[pltpu.VMEM((NMOM * nx, lanes), jnp.float32), pltpu.VMEM((count, lanes), jnp.float32)],
         compiler_params=params(),
         cost_estimate=cost(2 * 48 * count * nx * lanes, 8 * count * nx * lanes),
         name="new_moments",
-    )(*face_in, table, decay, source)
-
-
-def write_kernel(nx, step, place_ref, got_ref, entry_ref, decay_ref, source_ref, dist_ref):
-    entry = entry_of(step, place_ref, got_ref, entry_ref)
+    )(keep, got, table, decay, source)
+
+
+def write_kernel(nx, entry_ref, decay_ref, source_ref, dist_ref):
+    entry = entry_ref[...]
     count = entry.shape[0]
     for i in range(nx):
         dist_ref[pl.ds(i, count, stride=nx), :] = decay_ref[i] * entry + source_ref[i]
 
 
-def write_dist(nx, step, place, got, entry, decay, source):
+def write_dist(nx, entry, decay, source):
     count, lanes = entry.shape
     chunk = min(count, 128)
     field = pl.BlockSpec((nx, chunk, lanes), lambda i: (0, i, 0))
-    face = pl.BlockSpec((chunk, lanes), lambda i: (i, 0))
-    return pl.pallas_call(
-        functools.partial(write_kernel, nx, step),
+    return pl.pallas_call(
+        functools.partial(write_kernel, nx),
         grid=(count // chunk,),
-        in_specs=[pl.BlockSpec((8, lanes), lambda i: (0, 0)), face, face, field, field],
+        in_specs=[pl.BlockSpec((chunk, lanes), lambda i: (i, 0)), field, field],
         out_specs=pl.BlockSpec((chunk * nx, lanes), lambda i: (i, 0)),
         out_shape=jax.ShapeDtypeStruct((count * nx, lanes), jnp.float32),
         compiler_params=params(),
         cost_estimate=cost(2 * count * nx * lanes, 12 * count * nx * lanes),
         name="write_dist",
-    )(place, got, entry, decay, source)
+    )(entry, decay, source)
 
 
 def stages_of(n):
@@ -358,47 +459,23 @@
         a = a + other
 
 
-def hop(face, side, step):
-    n = lax.axis_size("gx")
-    up = [(step, step + 1)]
-    down = [(n - 1 - step, n - 2 - step)]
-    if n % 2 == 0:
-        return lax.ppermute(face, "gx", up + down)
-    return jnp.where(side[0] == 1, lax.ppermute(face, "gx", up), lax.ppermute(face, "gx", down))
-
-
 def local(total, dist, inflow, speed_x, transverse, quad_weight, side):
     count, nx, lanes = dist.shape
     flat = dist.reshape(count * nx, lanes)
-    side_row = side.reshape(1, count)
-    speed = speed_x.reshape(1, count)
-    weight = quad_weight.reshape(1, count)
-    partial, table = old_moments(total, nx, side_row, speed, transverse, weight, flat)
-
-    def slope_part(half, halves):
-        def make(sent):
-            args = lax.optimization_barrier((side_row, speed, transverse, flat, sent))[:4]
-            return slopes(nx, half, halves, *args)
-
-        return make
-
-    n = lax.axis_size("gx")
+    row = lambda a: a.reshape(1, count)
+    partial, table, rows, held = old_moments(total, nx, row(side), row(speed_x), transverse, row(quad_weight), flat)
     halves = 2 if count % 256 == 0 else 1
-    parts = [slope_part(h, halves) for h in range(halves)]
-    (ma, mb), made = partial_sums(partial, "vert", parts)
-    decay, source, face, last_decay, last_source, place = maps(
-        nx, ma, mb, [m[1] for m in made], [m[0] for m in made], inflow
-    )
-    got, entry = inflow, inflow
-    for step in range(n - 1):
-        if step > 0:
-            entry, face = pass_face(step, place, got, entry, last_decay, last_source)
-        got = hop(face, side, step)
-    new_partial = new_moments(nx, n - 1, (place, got, entry), table, decay, source)
+
+    def slope_part(h):
+        return lambda sent: slopes(nx, h, halves, *lax.optimization_barrier((rows, held, sent))[:2])
+
+    (ma, mb), made = partial_sums(partial, "vert", [slope_part(h) for h in range(halves)])
+    decay, source, send, sign = maps(nx, ma, mb, [m[1] for m in made], [m[0] for m in made])
+    keep, got = entries(nx, sign, decay, source, send, inflow, side)
+    new_partial, entry = new_moments(nx, keep, got, table, decay, source)
 
     def write(sent):
-        args = lax.optimization_barrier((place, got, entry, decay, source, sent))[:5]
-        return write_dist(nx, n - 1, *args)
+        return write_dist(nx, *lax.optimization_barrier((entry, decay, source, sent))[:3])
 
     (na, nb), (new_flat,) = partial_sums(new_partial, "vert", [write])
     return new_flat.reshape(count, nx, lanes), (na + nb).reshape(NMOM, nx, lanes)

time: 46.3 us -> 41.3 us (0.89)
  waiting for transfers between devices: 14.3 us -> 11.3 us
  starting transfers between devices: 16.6 us -> 15.4 us
  Pallas kernels: 13.7 us -> 13.1 us
    ppermute x3, waiting for transfers between devices: 10 us -> 6.88 us  [the longest x1 4.02 us: chip_hop(): got = lax.ppermute(face, 'gx', pairs)]
    ppermute x3, starting transfers between devices: 3.28 us -> 1.73 us  [the longest x1 1.58 us: chip_hop(): got = lax.ppermute(face, 'gx', pairs)]
    pallas_call x6, Pallas kernels: 8.35 us -> 7.77 us  [the longest x2 4.68 us: slopes(): pl.pallas_call(functools.partial(slope_kernel, nx, half * count), in_spec...]
  transfers between devices with their start and end apart: 11 -> 11, of which waited for: 6 -> 8; matrix products, arithmetic and copies ran while one was open for 0% -> 0% of each run, Pallas kernels for 16% -> 17%
where the time goes in v2:
time: 41.3 us; the launch traced here: 41.2 us
  starting transfers between devices  15.4 us (37%)
  Pallas kernels  13.1 us (32%)
  waiting for transfers between devices  11.3 us (27%)
  between operations  0.71 us (2%)
  other arithmetic  0.67 us (2%)
    ppermute x8, starting transfers between devices, exchange(): return lax.ppermute(a, axis, [(i, i ^ mask) for i in range(n)])  13.7 us
    pallas_call x2, Pallas kernels, slopes(): pl.pallas_call(functools.partial(slope_kernel, nx, half * count), in_spec...  4.68 us
    ppermute x8, waiting for transfers between devices, exchange(): return lax.ppermute(a, axis, [(i, i ^ mask) for i in range(n)])  4.42 us
    ppermute x1, waiting for transfers between devices, chip_hop(): got = lax.ppermute(face, 'gx', pairs)  4.02 us
    pallas_call x1, Pallas kernels, maps(): pl.pallas_call(functools.partial(map_kernel, nx, halves), in_specs=[whole...  3.18 us
    ppermute x2, waiting for transfers between devices, chip_exchange(): return lax.ppermute(a, 'gx', [(i, i ^ 1) for i in range(n)])  2.86 us
    pallas_call x1, Pallas kernels, write_dist(): pl.pallas_call(functools.partial(write_kernel, nx), grid=(count // chunk,...  2.29 us
    pallas_call x1, Pallas kernels, old_moments(): pl.pallas_call(functools.partial(moments_kernel, total, nx, chunks), in_s...  2.15 us
  transfers between devices with their start and end apart: 11, of which 8 were waited for; matrix products, arithmetic and copies ran while one was open for 0% of the time, Pallas kernels for 17%

profile of v2, /device:TPU:0, one launch (start us, length us, event | category | flops | bytes accessed | tf_op | source)
XLA Modules:
  0.0 41.2 jit_solution(15789238451026874607)
XLA Ops:
  0.6 2.1 %moments.1 = (f32[104,128]{1,0:T(8,128)S(1)}, bf16[32,512]{1,0:T(8,128)(2,1)S(1)}, f32[8,512]{1,0:T(8,128)S(1)}, f32[4096,128]{1,0:T(8,128)S(1)}) custom-call(s32[1,512]{1,0:T(1,128)} %bitcast.9, f32[1,512]{1,0:T(1,128)} %bitcast.10, f32[2,512]{1,0:T(2,128)} %cross_hbm.1, f32[1,512]{1,0:T(1,128)} %bitcast.11, f32[4096,128]{1,0:T(8,128)} %bitcast.8), custom_call_target="tpu_custom_call" | custom-call | flops 50331648 | bytes 2097152 | tf_op jit(solution)/shard_map/moments/pallas_call | solution.py:87
  2.8 4.0 %collective-permute-start.2 = (f32[104,128]{1,0:T(8,128)S(1)}, f32[104,128]{1,0:T(8,128)S(1)}, u32[]{:S(2)}, u32[]{:S(2)}) collective-permute-start(f32[104,128]{1,0:T(8,128)S(1)} %get-tuple-element.40), channel_id=1, source_target_pairs={{0,3},{1,2},{2,1},{3,0},{4,7},{5,6},{6,5},{7,4},{8,11},{9,10},{10,... | collective-permute-start | bytes 159752 | tf_op jit(solution)/shard_map/ppermute | solution.py:438
  6.8 0.4 %collective-permute-start.1 = (f32[104,128]{1,0:T(8,128)S(1)}, f32[104,128]{1,0:T(8,128)S(1)}, u32[]{:S(2)}, u32[]{:S(2)}) collective-permute-start(f32[104,128]{1,0:T(8,128)S(1)} %get-tuple-element.40), channel_id=1, source_target_pairs={{0,2},{1,3},{2,0},{3,1},{4,6},{5,7},{6,4},{7,5},{8,10},{9,11},{10,... | collective-permute-start | bytes 159752 | tf_op jit(solution)/shard_map/ppermute | solution.py:438
  7.3 0.2 collective-permute-start
  7.4 2.3 %slope.2 = (f32[8,256,128]{2,1,0:T(8,128)S(1)}, f32[3,256,128]{2,1,0:T(8,128)S(1)}) custom-call(f32[8,512]{1,0:T(8,128)S(1)} %get-tuple-element.50.rows_ref, f32[4096,128]{1,0:T(8,128)S(1)} %get-tuple-element.51.dist_ref), custom_call_target="tpu_custom_call" | custom-call | flops 5242880 | bytes 2097152 | tf_op jit(solution)/shard_map/slope/pallas_call | solution.py:140
  9.8 0.0 collective-permute-done.2
  9.8 1.1 %collective-permute-done.1 = f32[104,128]{1,0:T(8,128)S(1)} collective-permute-done((f32[104,128]{1,0:T(8,128)S(1)}, f32[104,128]{1,0:T(8,128)S(1)}, u32[]{:S(2)}, u32[]{:S(2)}) %collective-permute-start.1) | collective-permute-done | bytes 53280 | tf_op jit(solution)/shard_map/ppermute | solution.py:438
  10.9 0.4 %collective-permute-done = f32[104,128]{1,0:T(8,128)S(1)} collective-permute-done((f32[104,128]{1,0:T(8,128)S(1)}, f32[104,128]{1,0:T(8,128)S(1)}, u32[]{:S(2)}, u32[]{:S(2)}) %collective-permute-start) | collective-permute-done | bytes 53280 | tf_op jit(solution)/shard_map/ppermute | solution.py:438
  11.4 0.0 copy-start
  11.4 2.7 %collective-permute-start.3 = (f32[104,128]{1,0:T(8,128)S(1)}, f32[104,128]{1,0:T(8,128)S(1)}, u32[]{:S(2)}, u32[]{:S(2)}) collective-permute-start(f32[104,128]{1,0:T(8,128)S(1)} %add_add_fusion.1.ma_ref), channel_id=1, source_target_pairs={{0,4},{1,5},{2,6},{3,7},{4,0},{5,1},{6,2},{7,3},{8,12},{9,13},{10,... | collective-permute-start | bytes 159752 | tf_op jit(solution)/shard_map/ppermute | solution.py:438
  14.1 2.3 %slope.3 = (f32[8,256,128]{2,1,0:T(8,128)S(1)}, f32[3,256,128]{2,1,0:T(8,128)S(1)}) custom-call(f32[8,512]{1,0:T(8,128)S(1)} %get-tuple-element.50.rows_ref, f32[4096,128]{1,0:T(8,128)S(1)} %get-tuple-element.51.dist_ref), custom_call_target="tpu_custom_call" | custom-call | flops 5242880 | bytes 2097152 | tf_op jit(solution)/shard_map/slope/pallas_call | solution.py:140
  16.4 0.1 collective-permute-done.3.mb_ref
  16.5 3.2 %maps.1 = (f32[8,512,128]{2,1,0:T(8,128)S(1)}, f32[8,512,128]{2,1,0:T(8,128)S(1)}, f32[2,256,128]{2,1,0:T(8,128)S(1)}, f32[8,128]{1,0:T(8,128)S(1)}) custom-call(f32[104,128]{1,0:T(8,128)S(1)} %add_add_fusion.1.ma_ref, f32[104,128]{1,0:T(8,128)S(1)} %collective-permute-done.3.mb_ref, f32[3,256,128]{2,1,0:T(8,128)S(1)} %get-tuple-element.55.refs_0_, ...), custom_call_target="tpu_custom_call" | custom-call | flops 20971520 | bytes 6291456 | tf_op jit(solution)/shard_map/maps/pallas_call | solution.py:229
  19.7 0.1 collective-permute-start.4
  19.8 1.5 %collective-permute-done.4.got_ref = f32[2,256,128]{2,1,0:T(8,128)S(1)} collective-permute-done((f32[2,256,128]{2,1,0:T(8,128)S(1)}, f32[2,256,128]{2,1,0:T(8,128)S(1)}, u32[]{:S(2)}, u32[]{:S(2)}) %collective-permute-start.4) | collective-permute-done | bytes 262176 | tf_op jit(solution)/shard_map/ppermute | solution.py:341
  21.3 0.0 copy-done
  21.3 0.2 compose.1
  21.5 1.6 %collective-permute-start.5 = (f32[256,128]{1,0:T(8,128)S(1)}, f32[256,128]{1,0:T(8,128)S(1)}, u32[]{:S(2)}, u32[]{:S(2)}) collective-permute-start(f32[256,128]{1,0:T(8,128)S(1)} %get-tuple-element.63), channel_id=1, source_target_pairs={{0,16},{8,24},{16,0},{24,8},{1,17},{9,25},{17,1},{25,9},{2,18},{10... | collective-permute-start | bytes 393224 | tf_op jit(solution)/shard_map/ppermute | solution.py:349
  23.1 4.0 %collective-permute-done.5.got_ref = f32[256,128]{1,0:T(8,128)S(1)} collective-permute-done((f32[256,128]{1,0:T(8,128)S(1)}, f32[256,128]{1,0:T(8,128)S(1)}, u32[]{:S(2)}, u32[]{:S(2)}) %collective-permute-start.5) | collective-permute-done | bytes 131104 | tf_op jit(solution)/shard_map/ppermute | solution.py:349
  27.1 0.1 collective-permute-start.6
  27.2 1.3 %collective-permute-done.6.got_ref = f32[256,128]{1,0:T(8,128)S(1)} collective-permute-done((f32[256,128]{1,0:T(8,128)S(1)}, f32[256,128]{1,0:T(8,128)S(1)}, u32[]{:S(2)}, u32[]{:S(2)}) %collective-permute-start.6) | collective-permute-done | bytes 131104 | tf_op jit(solution)/shard_map/ppermute | solution.py:341
  28.5 0.6 %new_moments.1 = (f32[104,128]{1,0:T(8,128)S(1)}, f32[512,128]{1,0:T(8,128)S(1)}) custom-call(f32[256,128]{1,0:T(8,128)S(1)} %get-tuple-element.66.keep_ref, f32[256,128]{1,0:T(8,128)S(1)} %collective-permute-done.6.got_ref, bf16[32,512]{1,0:T(8,128)(2,1)S(1)} %get-tuple-element.68.table_ref, f32[8,512,128]{2,1,0:T(8,128)S(1)} %get-tuple-element.72.decay_ref, ...), custom_call_target="tpu_custom_call" | custom-call | flops 50331648 | bytes 4194304 | tf_op jit(solution)/shard_map/new_moments/pallas_call | solution.py:390
  29.1 1.6 %collective-permute-start.9 = (f32[104,128]{1,0:T(8,128)S(1)}, f32[104,128]{1,0:T(8,128)S(1)}, u32[]{:S(2)}, u32[]{:S(2)}) collective-permute-start(f32[104,128]{1,0:T(8,128)S(1)} %get-tuple-element.69), channel_id=1, source_target_pairs={{0,3},{1,2},{2,1},{3,0},{4,7},{5,6},{6,5},{7,4},{8,11},{9,10},{10,... | collective-permute-start | bytes 159752 | tf_op jit(solution)/shard_map/ppermute | solution.py:438
  30.7 0.4 collective-permute-start.8
  31.1 1.6 %collective-permute-start.7 = (f32[104,128]{1,0:T(8,128)S(1)}, f32[104,128]{1,0:T(8,128)S(1)}, u32[]{:S(2)}, u32[]{:S(2)}) collective-permute-start(f32[104,128]{1,0:T(8,128)S(1)} %get-tuple-element.69), channel_id=1, source_target_pairs={{0,1},{1,0},{2,3},{3,2},{4,5},{5,4},{6,7},{7,6},{8,9},{9,8},{10,11... | collective-permute-start | bytes 159752 | tf_op jit(solution)/shard_map/ppermute | solution.py:438
  32.6 2.3 %write_dist.1 = f32[4096,128]{1,0:T(8,128)} custom-call(f32[512,128]{1,0:T(8,128)S(1)} %get-tuple-element.71.entry_ref, f32[8,512,128]{2,1,0:T(8,128)S(1)} %get-tuple-element.72.decay_ref, f32[8,512,128]{2,1,0:T(8,128)S(1)} %get-tuple-element.73.source_ref), custom_call_target="tpu_custom_call" | custom-call | flops 1048576 | bytes 6291456 | tf_op jit(solution)/shard_map/write_dist/pallas_call | solution.py:412
  34.9 0.0 collective-permute-done.9
  34.9 0.0 collective-permute-done.8
  34.9 0.3 collective-permute-done.7
  35.2 2.8 %collective-permute-start.10 = (f32[104,128]{1,0:T(8,128)S(1)}, f32[104,128]{1,0:T(8,128)S(1)}, u32[]{:S(2)}, u32[]{:S(2)}) collective-permute-start(f32[104,128]{1,0:T(8,128)S(1)} %add_add_fusion), channel_id=1, source_target_pairs={{0,4},{1,5},{2,6},{3,7},{4,0},{5,1},{6,2},{7,3},{8,12},{9,13},{10,... | collective-permute-start | bytes 159752 | tf_op jit(solution)/shard_map/ppermute | solution.py:438
  38.1 2.5 %collective-permute-done.10 = f32[104,128]{1,0:T(8,128)S(1)} collective-permute-done((f32[104,128]{1,0:T(8,128)S(1)}, f32[104,128]{1,0:T(8,128)S(1)}, u32[]{:S(2)}, u32[]{:S(2)}) %collective-permute-start.10) | collective-permute-done | bytes 53280 | tf_op jit(solution)/shard_map/ppermute | solution.py:438
  40.5 0.6 %add_bitcast_fusion = f32[13,8,128]{2,1,0:T(8,128)} fusion(f32[104,128]{1,0:T(8,128)S(1)} %add_add_fusion, f32[104,128]{1,0:T(8,128)S(1)} %collective-permute-done.10), kind=kLoop, calls=%fused_computation | loop fusion | flops 13312 | bytes 159744 | tf_op jit(solution)/shard_map/reshape | solution.py:481
  (3 shorter events, 0.1 us)
Async XLA Ops:
  2.8 7.0 %collective-permute-start.2 = (f32[104,128]{1,0:T(8,128)S(1)}, f32[104,128]{1,0:T(8,128)S(1)}, u32[]{:S(2)}, u32[]{:S(2)}) collective-permute-start(f32[104,128]{1,0:T(8,128)S(1)} %get-tuple-element.40), channel_id=1, source_target_pairs={{0,3},{1,2},{2,1},{3,0},{4,7},{5,6},{6,5},{7,4},{8,11},{9,10},{10,... | collective-permute-start | bytes 159752 | tf_op jit(solution)/shard_map/ppermute | solution.py:438
  6.8 4.1 %collective-permute-start.1 = (f32[104,128]{1,0:T(8,128)S(1)}, f32[104,128]{1,0:T(8,128)S(1)}, u32[]{:S(2)}, u32[]{:S(2)}) collective-permute-start(f32[104,128]{1,0:T(8,128)S(1)} %get-tuple-element.40), channel_id=1, source_target_pairs={{0,2},{1,3},{2,0},{3,1},{4,6},{5,7},{6,4},{7,5},{8,10},{9,11},{10,... | collective-permute-start | bytes 159752 | tf_op jit(solution)/shard_map/ppermute | solution.py:438
  7.3 4.1 %collective-permute-start = (f32[104,128]{1,0:T(8,128)S(1)}, f32[104,128]{1,0:T(8,128)S(1)}, u32[]{:S(2)}, u32[]{:S(2)}) collective-permute-start(f32[104,128]{1,0:T(8,128)S(1)} %get-tuple-element.40), channel_id=1, source_target_pairs={{0,1},{1,0},{2,3},{3,2},{4,5},{5,4},{6,7},{7,6},{8,9},{9,8},{10,11... | collective-permute-start | bytes 159752 | tf_op jit(solution)/shard_map/ppermute | solution.py:438
  11.4 9.9 %copy-start = (f32[512,128]{1,0:T(8,128)S(1)}, f32[512,128]{1,0:T(8,128)}, u32[]{:S(2)}) copy-start(f32[512,128]{1,0:T(8,128)} %inflow_ref.1) | copy-start | bytes 786436
  11.4 5.1 %collective-permute-start.3 = (f32[104,128]{1,0:T(8,128)S(1)}, f32[104,128]{1,0:T(8,128)S(1)}, u32[]{:S(2)}, u32[]{:S(2)}) collective-permute-start(f32[104,128]{1,0:T(8,128)S(1)} %add_add_fusion.1.ma_ref), channel_id=1, source_target_pairs={{0,4},{1,5},{2,6},{3,7},{4,0},{5,1},{6,2},{7,3},{8,12},{9,13},{10,... | collective-permute-start | bytes 159752 | tf_op jit(solution)/shard_map/ppermute | solution.py:438
  19.7 1.6 %collective-permute-start.4 = (f32[2,256,128]{2,1,0:T(8,128)S(1)}, f32[2,256,128]{2,1,0:T(8,128)S(1)}, u32[]{:S(2)}, u32[]{:S(2)}) collective-permute-start(f32[2,256,128]{2,1,0:T(8,128)S(1)} %get-tuple-element.60), channel_id=1, source_target_pairs={{0,8},{8,0},{16,24},{24,16},{1,9},{9,1},{17,25},{25,17},{2,10},{10... | collective-permute-start | bytes 786440 | tf_op jit(solution)/shard_map/ppermute | solution.py:341
  21.5 5.6 %collective-permute-start.5 = (f32[256,128]{1,0:T(8,128)S(1)}, f32[256,128]{1,0:T(8,128)S(1)}, u32[]{:S(2)}, u32[]{:S(2)}) collective-permute-start(f32[256,128]{1,0:T(8,128)S(1)} %get-tuple-element.63), channel_id=1, source_target_pairs={{0,16},{8,24},{16,0},{24,8},{1,17},{9,25},{17,1},{25,9},{2,18},{10... | collective-permute-start | bytes 393224 | tf_op jit(solution)/shard_map/ppermute | solution.py:349
  27.1 1.4 %collective-permute-start.6 = (f32[256,128]{1,0:T(8,128)S(1)}, f32[256,128]{1,0:T(8,128)S(1)}, u32[]{:S(2)}, u32[]{:S(2)}) collective-permute-start(f32[256,128]{1,0:T(8,128)S(1)} %get-tuple-element.67), channel_id=1, source_target_pairs={{0,8},{8,0},{16,24},{24,16},{1,9},{9,1},{17,25},{25,17},{2,10},{10... | collective-permute-start | bytes 393224 | tf_op jit(solution)/shard_map/ppermute | solution.py:341
  29.1 5.8 %collective-permute-start.9 = (f32[104,128]{1,0:T(8,128)S(1)}, f32[104,128]{1,0:T(8,128)S(1)}, u32[]{:S(2)}, u32[]{:S(2)}) collective-permute-start(f32[104,128]{1,0:T(8,128)S(1)} %get-tuple-element.69), channel_id=1, source_target_pairs={{0,3},{1,2},{2,1},{3,0},{4,7},{5,6},{6,5},{7,4},{8,11},{9,10},{10,... | collective-permute-start | bytes 159752 | tf_op jit(solution)/shard_map/ppermute | solution.py:438
  30.7 4.2 %collective-permute-start.8 = (f32[104,128]{1,0:T(8,128)S(1)}, f32[104,128]{1,0:T(8,128)S(1)}, u32[]{:S(2)}, u32[]{:S(2)}) collective-permute-start(f32[104,128]{1,0:T(8,128)S(1)} %get-tuple-element.69), channel_id=1, source_target_pairs={{0,2},{1,3},{2,0},{3,1},{4,6},{5,7},{6,4},{7,5},{8,10},{9,11},{10,... | collective-permute-start | bytes 159752 | tf_op jit(solution)/shard_map/ppermute | solution.py:438
  31.1 4.1 %collective-permute-start.7 = (f32[104,128]{1,0:T(8,128)S(1)}, f32[104,128]{1,0:T(8,128)S(1)}, u32[]{:S(2)}, u32[]{:S(2)}) collective-permute-start(f32[104,128]{1,0:T(8,128)S(1)} %get-tuple-element.69), channel_id=1, source_target_pairs={{0,1},{1,0},{2,3},{3,2},{4,5},{5,4},{6,7},{7,6},{8,9},{9,8},{10,11... | collective-permute-start | bytes 159752 | tf_op jit(solution)/shard_map/ppermute | solution.py:438
  35.2 5.3 %collective-permute-start.10 = (f32[104,128]{1,0:T(8,128)S(1)}, f32[104,128]{1,0:T(8,128)S(1)}, u32[]{:S(2)}, u32[]{:S(2)}) collective-permute-start(f32[104,128]{1,0:T(8,128)S(1)} %add_add_fusion), channel_id=1, source_target_pairs={{0,4},{1,5},{2,6},{3,7},{4,0},{5,1},{6,2},{7,3},{8,12},{9,13},{10,... | collective-permute-start | bytes 159752 | tf_op jit(solution)/shard_map/ppermute | solution.py:438

commit v3 on v2

--- a/solution.py
+++ b/solution.py
@@ -13,6 +13,8 @@
 SHEAR = 0.19
 NMOM = 13
 ROWS = 16
+TERMS = 5
+DEPTH = 128
 
 
 def params(**kw):
@@ -27,6 +29,12 @@
     high = a.astype(jnp.bfloat16)
     low = (a - high.astype(jnp.float32)).astype(jnp.bfloat16)
     return high, low
+
+
+def split3(a):
+    high, rest = split(a)
+    mid, low = split(a - high.astype(jnp.float32))
+    return [high.astype(jnp.float32), mid.astype(jnp.float32), low.astype(jnp.float32)]
 
 
 def project(table, plane):
@@ -82,7 +90,7 @@
 
 def old_moments(total, nx, side, speed, cross, weight, dist):
     count, lanes = speed.shape[1], dist.shape[1]
-    chunks = max(1, count // 128)
+    chunks = max(1, count // 256)
     whole = pl.BlockSpec(memory_space=pltpu.VMEM)
     return pl.pallas_call(
         functools.partial(moments_kernel, total, nx, chunks),
@@ -107,18 +115,25 @@
     )(*[pltpu.with_memory_space_constraint(a, pltpu.HBM) for a in (side, speed, cross, weight, dist)])
 
 
-def slope_kernel(nx, start, rows_ref, dist_ref, slope_ref, comp_ref):
+def slope_kernel(nx, start, rows_ref, dist_ref, slope_ref, speed_ref, feature_ref, comp_ref):
     count = slope_ref.shape[1]
     lanes = dist_ref.shape[1]
-    columns = jnp.transpose(rows_ref[:, start : start + count])
-    for k in range(3):
-        comp_ref[k] = jnp.broadcast_to(columns[:, k : k + 1], (count, lanes))
+    rows = rows_ref[:, start : start + count]
+    columns = jnp.transpose(rows)
+    speed_ref[...] = jnp.broadcast_to(jnp.abs(columns[:, 0:1]), (count, lanes))
+    for k in range(2):
+        comp_ref[k] = jnp.broadcast_to(columns[:, k + 1 : k + 2], (count, lanes))
+    x, y, z = rows[0:1], rows[1:2], rows[2:3]
+    high, mid, low = split3(jnp.concatenate([x * x + y * y + z * z, x, y, z, jnp.ones_like(x)], axis=0))
+    terms = jnp.concatenate([high, high, mid, mid, high, low], axis=0)
+    terms = jnp.concatenate([terms, jnp.zeros((DEPTH - 6 * TERMS, count), jnp.float32)], axis=0)
+    feature_ref[...] = jnp.transpose(terms).astype(jnp.bfloat16)
     group = 32
 
     def one(g, carry):
         at = pl.multiple_of(g * group, group)
-        y = comp_ref[1, pl.ds(at, group), :]
-        z = comp_ref[2, pl.ds(at, group), :]
+        y = comp_ref[0, pl.ds(at, group), :]
+        z = comp_ref[1, pl.ds(at, group), :]
         lane = lax.broadcasted_iota(jnp.int32, (group, lanes), 1)
         from_y = jnp.where(y > 0, lane + (lanes - NZ), lane + NZ) & (lanes - 1)
         from_z = (lane & ~(NZ - 1)) | (jnp.where(z > 0, lane + (NZ - 1), lane + 1) & (NZ - 1))
@@ -140,22 +155,24 @@
     return pl.pallas_call(
         functools.partial(slope_kernel, nx, half * count),
         in_specs=[whole] * 2,
-        out_specs=[whole] * 2,
+        out_specs=[whole] * 3,
         out_shape=[
             pltpu.VMEM((nx, count, lanes), jnp.float32),
-            pltpu.VMEM((3, count, lanes), jnp.float32),
+            pltpu.VMEM((count, lanes), jnp.float32),
+            pltpu.VMEM((count, DEPTH), jnp.bfloat16),
         ],
+        scratch_shapes=[pltpu.VMEM((2, count, lanes), jnp.float32)],
         compiler_params=params(),
         cost_estimate=cost(20 * count * nx * lanes, 8 * count * nx * lanes),
         name="slope",
     )(rows, dist)
 
 
-def map_kernel(nx, halves, ma_ref, mb_ref, *refs):
-    comps, slopes_in = refs[:halves], refs[halves : 2 * halves]
-    decay_ref, source_ref, send_ref, sign_ref, state = refs[2 * halves :]
+def map_kernel(nx, halves, ma_ref, mb_ref, rows_ref, *refs):
+    slopes_in, speeds, features = (refs[i * halves : (i + 1) * halves] for i in range(3))
+    decay_ref, source_ref, send_ref, sign_ref, state, bulk_terms, flux_terms = refs[3 * halves :]
     count, lanes = decay_ref.shape[1:]
-    sign_ref[...] = comps[0][0, 0:8, :]
+    part = count // halves
     m = [ma_ref[k * nx : (k + 1) * nx, :] + mb_ref[k * nx : (k + 1) * nx, :] for k in range(NMOM)]
     n = m[0]
     inv_n = 1.0 / n
@@ -165,54 +182,54 @@
     temp = (energy * inv_n - uu) * (1.0 / 3.0)
     second = ((m[4], m[7], m[8]), (m[7], m[5], m[9]), (m[8], m[9], m[6]))
     inv_t = 1.0 / temp
-    flux_scale = inv_n * inv_t * inv_t * (1.0 / 15.0)
     nu = KAPPA_CELL * n * jnp.exp(SHEAR * jnp.log(temp))
+    rate = inv_t * (-0.5 * LOG2E)
+    ratio = -2.0 / LOG2E
+    flux_scale = inv_n * inv_t * inv_t * (ratio / 15.0)
+    q = []
     for k in range(3):
         inner = u[0] * second[k][0] + u[1] * second[k][1] + u[2] * second[k][2]
-        q = 0.5 * (m[10 + k] - 2.0 * inner - u[k] * energy + 2.0 * n * u[k] * uu)
-        state[k] = u[k]
-        state[3 + k] = q * flux_scale
-    state[6] = inv_t
-    state[7] = inv_t * (-0.5 * LOG2E)
-    state[8] = nu * n * inv_t * jnp.sqrt(inv_t)
-    state[9] = nu
-    forward = comps[0][0, 0:1, 0:1][0, 0] > 0
+        q.append(0.5 * flux_scale * (m[10 + k] - 2.0 * inner - u[k] * energy + 2.0 * n * u[k] * uu))
+    twice = -2.0 * rate
+    bulk = [rate, twice * u[0], twice * u[1], twice * u[2], rate * uu]
+    flux = [jnp.zeros_like(n), q[0], q[1], q[2], -(u[0] * q[0] + u[1] * q[1] + u[2] * q[2])]
+    for terms, ref in ((bulk, bulk_terms), (flux, flux_terms)):
+        for k in range(TERMS):
+            high, mid, low = split3(terms[k])
+            for i, one in enumerate((high, mid, high, mid, low, high)):
+                ref[(i * TERMS + k) * nx : (i * TERMS + k + 1) * nx, :] = one
+        ref[6 * TERMS * nx :, :] = jnp.zeros(((32 - 6 * TERMS) * nx, lanes), jnp.float32)
+    state[0] = nu * n * inv_t * jnp.sqrt(inv_t)
+    state[1] = nu
+    sign_ref[...] = jnp.broadcast_to(rows_ref[0:1, 0:1], (8, lanes))
+    forward = rows_ref[0:1, 0:1][0, 0] > 0
+    rest = jnp.zeros((DEPTH - 32, 2 * lanes), jnp.bfloat16)
     group = 32
-    part = count // halves
 
     for j in range(nx):
         at_x = jnp.where(forward, j, nx - 1 - j)
         before = jnp.where(forward, j - 1, nx - j)
-        s = [jnp.broadcast_to(state[k, pl.ds(at_x, 1), :], (8, lanes)) for k in range(10)]
-        s = [jnp.concatenate([a] * (group // 8), axis=0) for a in s]
-
+        scale = jnp.broadcast_to(state[0, pl.ds(at_x, 1), :], (group, lanes))
+        rate_x = jnp.broadcast_to(state[1, pl.ds(at_x, 1), :], (group, lanes))
+        cells = jnp.concatenate([ref[pl.ds(at_x, 32, stride=nx), :] for ref in (bulk_terms, flux_terms)], axis=1)
+        cells = jnp.concatenate([cells.astype(jnp.bfloat16), rest], axis=0)
         for h in range(halves):
-            comp_ref, slope_ref = comps[h], slopes_in[h]
-
-            def one(g, carry):
-                at = pl.multiple_of(g * group, group)
-                own = pl.ds(at, group)
-                rows = pl.ds(h * part + at, group)
-                cx = comp_ref[0, own, :]
-                wx = cx - s[0]
-                wy = comp_ref[1, own, :] - s[1]
-                wz = comp_ref[2, own, :] - s[2]
-                ww = wx * wx + wy * wy + wz * wz
-                wq = wx * s[3] + wy * s[4] + wz * s[5]
-                shape = 1.0 + wq * (ww * s[6] - 5.0)
-                target = s[8] * jnp.exp2(ww * s[7]) * shape
-                speed = jnp.abs(cx)
-                inv = 1.0 / (speed + s[9])
+            both = jnp.dot(features[h][...], cells, preferred_element_type=jnp.float32)
+            for at in range(0, part, group):
+                own = slice(at, at + group)
+                rows = slice(h * part + at, h * part + at + group)
+                exponent, wq = both[own, :lanes], both[own, lanes:]
+                shape = 1.0 + wq * (exponent - 5.0 / ratio)
+                target = scale * jnp.exp2(exponent) * shape
+                speed = speeds[h][own, :]
+                inv = 1.0 / (speed + rate_x)
                 decay = speed * inv
-                source = (target - slope_ref[at_x, own, :]) * inv
+                source = (target - slopes_in[h][at_x, own, :]) * inv
                 if j > 0:
                     source = decay * source_ref[before, rows, :] + source
                     decay = decay * decay_ref[before, rows, :]
                 decay_ref[at_x, rows, :] = decay
                 source_ref[at_x, rows, :] = source
-                return carry
-
-            lax.fori_loop(0, part // group, one, 0)
 
     last = jnp.where(forward, nx - 1, 0)
     theirs = pl.ds(pl.multiple_of((1 - lax.axis_index("gx") % 2) * (count // 2), count // 2), count // 2)
@@ -220,15 +237,14 @@
     send_ref[1] = source_ref[last, theirs, :]
 
 
-def maps(nx, ma, mb, comps, slopes_in):
+def maps(nx, ma, mb, rows, parts):
     lanes = ma.shape[1]
-    halves = len(comps)
-    count = halves * comps[0].shape[1]
+    halves, count = len(parts), rows.shape[1]
     whole = pl.BlockSpec(memory_space=pltpu.VMEM)
     field = pltpu.VMEM((nx, count, lanes), jnp.float32)
     return pl.pallas_call(
         functools.partial(map_kernel, nx, halves),
-        in_specs=[whole] * (2 + 2 * halves),
+        in_specs=[whole] * (3 + 3 * halves),
         out_specs=[whole] * 4,
         out_shape=[
             field,
@@ -236,11 +252,15 @@
             pltpu.VMEM((2, count // 2, lanes), jnp.float32),
             pltpu.VMEM((8, lanes), jnp.float32),
         ],
-        scratch_shapes=[pltpu.VMEM((10, nx, lanes), jnp.float32)],
+        scratch_shapes=[
+            pltpu.VMEM((2, nx, lanes), jnp.float32),
+            pltpu.VMEM((32 * nx, lanes), jnp.float32),
+            pltpu.VMEM((32 * nx, lanes), jnp.float32),
+        ],
         compiler_params=params(),
         cost_estimate=cost(40 * count * nx * lanes, 12 * count * nx * lanes),
         name="maps",
-    )(ma, mb, *comps, *slopes_in)
+    )(ma, mb, rows, *[p[i] for i in range(3) for p in parts])
 
 
 def standing(sign_ref):
@@ -470,7 +490,7 @@
         return lambda sent: slopes(nx, h, halves, *lax.optimization_barrier((rows, held, sent))[:2])
 
     (ma, mb), made = partial_sums(partial, "vert", [slope_part(h) for h in range(halves)])
-    decay, source, send, sign = maps(nx, ma, mb, [m[1] for m in made], [m[0] for m in made])
+    decay, source, send, sign = maps(nx, ma, mb, rows, made)
     keep, got = entries(nx, sign, decay, source, send, inflow, side)
     new_partial, entry = new_moments(nx, keep, got, table, decay, source)
 

time: 41.3 us -> 40.2 us (0.973)
  Pallas kernels: 13.1 us -> 12 us
    pallas_call x1, Pallas kernels: 3.18 us -> 2.15 us  [maps(): pl.pallas_call(functools.partial(map_kernel, nx, halves), in_specs=[whole...]
where the time goes in v3:
time: 40.2 us; the launch traced here: 40.1 us
  starting transfers between devices  15.4 us (38%)
  Pallas kernels  12 us (30%)
  waiting for transfers between devices  11.3 us (28%)
  between operations  0.71 us (2%)
  other arithmetic  0.67 us (2%)
    ppermute x8, starting transfers between devices, exchange(): return lax.ppermute(a, axis, [(i, i ^ mask) for i in range(n)])  13.6 us
    pallas_call x2, Pallas kernels, slopes(): pl.pallas_call(functools.partial(slope_kernel, nx, half * count), in_spec...  4.69 us
    ppermute x8, waiting for transfers between devices, exchange(): return lax.ppermute(a, axis, [(i, i ^ mask) for i in range(n)])  4.42 us
    ppermute x1, waiting for transfers between devices, chip_hop(): got = lax.ppermute(face, 'gx', pairs)  4.02 us
    ppermute x2, waiting for transfers between devices, chip_exchange(): return lax.ppermute(a, 'gx', [(i, i ^ 1) for i in range(n)])  2.86 us
    pallas_call x1, Pallas kernels, write_dist(): pl.pallas_call(functools.partial(write_kernel, nx), grid=(count // chunk,...  2.29 us
    pallas_call x1, Pallas kernels, maps(): pl.pallas_call(functools.partial(map_kernel, nx, halves), in_specs=[whole...  2.15 us
    pallas_call x1, Pallas kernels, old_moments(): pl.pallas_call(functools.partial(moments_kernel, total, nx, chunks), in_s...  2.07 us
  transfers between devices with their start and end apart: 11, of which 8 were waited for; matrix products, arithmetic and copies ran while one was open for 0% of the time, Pallas kernels for 17%

profile of v3, /device:TPU:0, one launch (start us, length us, event | category | flops | bytes accessed | tf_op | source)
XLA Modules:
  0.0 40.1 jit_solution(11987101365107526976)
XLA Ops:
  0.6 2.1 %moments.1 = (f32[104,128]{1,0:T(8,128)S(1)}, bf16[32,512]{1,0:T(8,128)(2,1)S(1)}, f32[8,512]{1,0:T(8,128)S(1)}, f32[4096,128]{1,0:T(8,128)S(1)}) custom-call(s32[1,512]{1,0:T(1,128)} %bitcast.9, f32[1,512]{1,0:T(1,128)} %bitcast.10, f32[2,512]{1,0:T(2,128)} %cross_hbm.1, f32[1,512]{1,0:T(1,128)} %bitcast.11, f32[4096,128]{1,0:T(8,128)} %bitcast.8), custom_call_target="tpu_custom_call" | custom-call | flops 50331648 | bytes 2097152 | tf_op jit(solution)/shard_map/moments/pallas_call | solution.py:95
  2.7 4.0 %collective-permute-start.2 = (f32[104,128]{1,0:T(8,128)S(1)}, f32[104,128]{1,0:T(8,128)S(1)}, u32[]{:S(2)}, u32[]{:S(2)}) collective-permute-start(f32[104,128]{1,0:T(8,128)S(1)} %get-tuple-element.44), channel_id=1, source_target_pairs={{0,3},{1,2},{2,1},{3,0},{4,7},{5,6},{6,5},{7,4},{8,11},{9,10},{10,... | collective-permute-start | bytes 159752 | tf_op jit(solution)/shard_map/ppermute | solution.py:458
  6.7 0.4 %collective-permute-start.1 = (f32[104,128]{1,0:T(8,128)S(1)}, f32[104,128]{1,0:T(8,128)S(1)}, u32[]{:S(2)}, u32[]{:S(2)}) collective-permute-start(f32[104,128]{1,0:T(8,128)S(1)} %get-tuple-element.44), channel_id=1, source_target_pairs={{0,2},{1,3},{2,0},{3,1},{4,6},{5,7},{6,4},{7,5},{8,10},{9,11},{10,... | collective-permute-start | bytes 159752 | tf_op jit(solution)/shard_map/ppermute | solution.py:458
  7.2 0.2 collective-permute-start
  7.4 2.3 %slope.2 = (f32[8,256,128]{2,1,0:T(8,128)S(1)}, f32[256,128]{1,0:T(8,128)S(1)}, bf16[256,128]{1,0:T(8,128)(2,1)S(1)}) custom-call(f32[8,512]{1,0:T(8,128)S(1)} %get-tuple-element.55.rows_ref, f32[4096,128]{1,0:T(8,128)S(1)} %get-tuple-element.56.dist_ref), custom_call_target="tpu_custom_call" | custom-call | flops 5242880 | bytes 2097152 | tf_op jit(solution)/shard_map/slope/pallas_call | solution.py:155
  9.7 0.0 collective-permute-done.2
  9.7 1.1 %collective-permute-done.1 = f32[104,128]{1,0:T(8,128)S(1)} collective-permute-done((f32[104,128]{1,0:T(8,128)S(1)}, f32[104,128]{1,0:T(8,128)S(1)}, u32[]{:S(2)}, u32[]{:S(2)}) %collective-permute-start.1) | collective-permute-done | bytes 53280 | tf_op jit(solution)/shard_map/ppermute | solution.py:458
  10.9 0.4 %collective-permute-done = f32[104,128]{1,0:T(8,128)S(1)} collective-permute-done((f32[104,128]{1,0:T(8,128)S(1)}, f32[104,128]{1,0:T(8,128)S(1)}, u32[]{:S(2)}, u32[]{:S(2)}) %collective-permute-start) | collective-permute-done | bytes 53280 | tf_op jit(solution)/shard_map/ppermute | solution.py:458
  11.3 0.0 copy-start
  11.3 2.7 %collective-permute-start.3 = (f32[104,128]{1,0:T(8,128)S(1)}, f32[104,128]{1,0:T(8,128)S(1)}, u32[]{:S(2)}, u32[]{:S(2)}) collective-permute-start(f32[104,128]{1,0:T(8,128)S(1)} %add_add_fusion.1.ma_ref), channel_id=1, source_target_pairs={{0,4},{1,5},{2,6},{3,7},{4,0},{5,1},{6,2},{7,3},{8,12},{9,13},{10,... | collective-permute-start | bytes 159752 | tf_op jit(solution)/shard_map/ppermute | solution.py:458
  14.0 2.3 %slope.3 = (f32[8,256,128]{2,1,0:T(8,128)S(1)}, f32[256,128]{1,0:T(8,128)S(1)}, bf16[256,128]{1,0:T(8,128)(2,1)S(1)}) custom-call(f32[8,512]{1,0:T(8,128)S(1)} %get-tuple-element.55.rows_ref, f32[4096,128]{1,0:T(8,128)S(1)} %get-tuple-element.56.dist_ref), custom_call_target="tpu_custom_call" | custom-call | flops 5242880 | bytes 2097152 | tf_op jit(solution)/shard_map/slope/pallas_call | solution.py:155
  16.3 0.1 collective-permute-done.3.mb_ref
  16.4 2.1 %maps.1 = (f32[8,512,128]{2,1,0:T(8,128)S(1)}, f32[8,512,128]{2,1,0:T(8,128)S(1)}, f32[2,256,128]{2,1,0:T(8,128)S(1)}, f32[8,128]{1,0:T(8,128)S(1)}) custom-call(f32[104,128]{1,0:T(8,128)S(1)} %add_add_fusion.1.ma_ref, f32[104,128]{1,0:T(8,128)S(1)} %collective-permute-done.3.mb_ref, f32[8,512]{1,0:T(8,128)S(1)} %get-tuple-element.55.rows_ref, ...), custom_call_target="tpu_custom_call" | custom-call | flops 20971520 | bytes 6291456 | tf_op jit(solution)/shard_map/maps/pallas_call | solution.py:245
  18.6 0.1 collective-permute-start.4
  18.7 1.5 %collective-permute-done.4.got_ref = f32[2,256,128]{2,1,0:T(8,128)S(1)} collective-permute-done((f32[2,256,128]{2,1,0:T(8,128)S(1)}, f32[2,256,128]{2,1,0:T(8,128)S(1)}, u32[]{:S(2)}, u32[]{:S(2)}) %collective-permute-start.4) | collective-permute-done | bytes 262176 | tf_op jit(solution)/shard_map/ppermute | solution.py:361
  20.2 0.0 copy-done
  20.2 0.2 compose.1
  20.4 1.6 %collective-permute-start.5 = (f32[256,128]{1,0:T(8,128)S(1)}, f32[256,128]{1,0:T(8,128)S(1)}, u32[]{:S(2)}, u32[]{:S(2)}) collective-permute-start(f32[256,128]{1,0:T(8,128)S(1)} %get-tuple-element.71), channel_id=1, source_target_pairs={{0,16},{8,24},{16,0},{24,8},{1,17},{9,25},{17,1},{25,9},{2,18},{10... | collective-permute-start | bytes 393224 | tf_op jit(solution)/shard_map/ppermute | solution.py:369
  21.9 4.0 %collective-permute-done.5.got_ref = f32[256,128]{1,0:T(8,128)S(1)} collective-permute-done((f32[256,128]{1,0:T(8,128)S(1)}, f32[256,128]{1,0:T(8,128)S(1)}, u32[]{:S(2)}, u32[]{:S(2)}) %collective-permute-start.5) | collective-permute-done | bytes 131104 | tf_op jit(solution)/shard_map/ppermute | solution.py:369
  26.0 0.1 collective-permute-start.6
  26.1 1.3 %collective-permute-done.6.got_ref = f32[256,128]{1,0:T(8,128)S(1)} collective-permute-done((f32[256,128]{1,0:T(8,128)S(1)}, f32[256,128]{1,0:T(8,128)S(1)}, u32[]{:S(2)}, u32[]{:S(2)}) %collective-permute-start.6) | collective-permute-done | bytes 131104 | tf_op jit(solution)/shard_map/ppermute | solution.py:361
  27.4 0.6 %new_moments.1 = (f32[104,128]{1,0:T(8,128)S(1)}, f32[512,128]{1,0:T(8,128)S(1)}) custom-call(f32[256,128]{1,0:T(8,128)S(1)} %get-tuple-element.74.keep_ref, f32[256,128]{1,0:T(8,128)S(1)} %collective-permute-done.6.got_ref, bf16[32,512]{1,0:T(8,128)(2,1)S(1)} %get-tuple-element.76.table_ref, f32[8,512,128]{2,1,0:T(8,128)S(1)} %get-tuple-element.80.decay_ref, ...), custom_call_target="tpu_custom_call" | custom-call | flops 50331648 | bytes 4194304 | tf_op jit(solution)/shard_map/new_moments/pallas_call | solution.py:410
  28.0 1.6 %collective-permute-start.9 = (f32[104,128]{1,0:T(8,128)S(1)}, f32[104,128]{1,0:T(8,128)S(1)}, u32[]{:S(2)}, u32[]{:S(2)}) collective-permute-start(f32[104,128]{1,0:T(8,128)S(1)} %get-tuple-element.77), channel_id=1, source_target_pairs={{0,3},{1,2},{2,1},{3,0},{4,7},{5,6},{6,5},{7,4},{8,11},{9,10},{10,... | collective-permute-start | bytes 159752 | tf_op jit(solution)/shard_map/ppermute | solution.py:458
  29.6 0.4 collective-permute-start.8
  30.0 1.6 %collective-permute-start.7 = (f32[104,128]{1,0:T(8,128)S(1)}, f32[104,128]{1,0:T(8,128)S(1)}, u32[]{:S(2)}, u32[]{:S(2)}) collective-permute-start(f32[104,128]{1,0:T(8,128)S(1)} %get-tuple-element.77), channel_id=1, source_target_pairs={{0,1},{1,0},{2,3},{3,2},{4,5},{5,4},{6,7},{7,6},{8,9},{9,8},{10,11... | collective-permute-start | bytes 159752 | tf_op jit(solution)/shard_map/ppermute | solution.py:458
  31.5 2.3 %write_dist.1 = f32[4096,128]{1,0:T(8,128)} custom-call(f32[512,128]{1,0:T(8,128)S(1)} %get-tuple-element.79.entry_ref, f32[8,512,128]{2,1,0:T(8,128)S(1)} %get-tuple-element.80.decay_ref, f32[8,512,128]{2,1,0:T(8,128)S(1)} %get-tuple-element.81.source_ref), custom_call_target="tpu_custom_call" | custom-call | flops 1048576 | bytes 6291456 | tf_op jit(solution)/shard_map/write_dist/pallas_call | solution.py:432
  33.8 0.0 collective-permute-done.9
  33.8 0.0 collective-permute-done.8
  33.8 0.3 collective-permute-done.7
  34.1 2.8 %collective-permute-start.10 = (f32[104,128]{1,0:T(8,128)S(1)}, f32[104,128]{1,0:T(8,128)S(1)}, u32[]{:S(2)}, u32[]{:S(2)}) collective-permute-start(f32[104,128]{1,0:T(8,128)S(1)} %add_add_fusion), channel_id=1, source_target_pairs={{0,4},{1,5},{2,6},{3,7},{4,0},{5,1},{6,2},{7,3},{8,12},{9,13},{10,... | collective-permute-start | bytes 159752 | tf_op jit(solution)/shard_map/ppermute | solution.py:458
  37.0 2.5 %collective-permute-done.10 = f32[104,128]{1,0:T(8,128)S(1)} collective-permute-done((f32[104,128]{1,0:T(8,128)S(1)}, f32[104,128]{1,0:T(8,128)S(1)}, u32[]{:S(2)}, u32[]{:S(2)}) %collective-permute-start.10) | collective-permute-done | bytes 53280 | tf_op jit(solution)/shard_map/ppermute | solution.py:458
  39.4 0.6 %add_bitcast_fusion = f32[13,8,128]{2,1,0:T(8,128)} fusion(f32[104,128]{1,0:T(8,128)S(1)} %add_add_fusion, f32[104,128]{1,0:T(8,128)S(1)} %collective-permute-done.10), kind=kLoop, calls=%fused_computation | loop fusion | flops 13312 | bytes 159744 | tf_op jit(solution)/shard_map/reshape | solution.py:501
  (3 shorter events, 0.1 us)
Async XLA Ops:
  2.7 7.0 %collective-permute-start.2 = (f32[104,128]{1,0:T(8,128)S(1)}, f32[104,128]{1,0:T(8,128)S(1)}, u32[]{:S(2)}, u32[]{:S(2)}) collective-permute-start(f32[104,128]{1,0:T(8,128)S(1)} %get-tuple-element.44), channel_id=1, source_target_pairs={{0,3},{1,2},{2,1},{3,0},{4,7},{5,6},{6,5},{7,4},{8,11},{9,10},{10,... | collective-permute-start | bytes 159752 | tf_op jit(solution)/shard_map/ppermute | solution.py:458
  6.7 4.1 %collective-permute-start.1 = (f32[104,128]{1,0:T(8,128)S(1)}, f32[104,128]{1,0:T(8,128)S(1)}, u32[]{:S(2)}, u32[]{:S(2)}) collective-permute-start(f32[104,128]{1,0:T(8,128)S(1)} %get-tuple-element.44), channel_id=1, source_target_pairs={{0,2},{1,3},{2,0},{3,1},{4,6},{5,7},{6,4},{7,5},{8,10},{9,11},{10,... | collective-permute-start | bytes 159752 | tf_op jit(solution)/shard_map/ppermute | solution.py:458
  7.2 4.1 %collective-permute-start = (f32[104,128]{1,0:T(8,128)S(1)}, f32[104,128]{1,0:T(8,128)S(1)}, u32[]{:S(2)}, u32[]{:S(2)}) collective-permute-start(f32[104,128]{1,0:T(8,128)S(1)} %get-tuple-element.44), channel_id=1, source_target_pairs={{0,1},{1,0},{2,3},{3,2},{4,5},{5,4},{6,7},{7,6},{8,9},{9,8},{10,11... | collective-permute-start | bytes 159752 | tf_op jit(solution)/shard_map/ppermute | solution.py:458
  11.3 8.9 %copy-start = (f32[512,128]{1,0:T(8,128)S(1)}, f32[512,128]{1,0:T(8,128)}, u32[]{:S(2)}) copy-start(f32[512,128]{1,0:T(8,128)} %inflow_ref.1) | copy-start | bytes 786436
  11.3 5.1 %collective-permute-start.3 = (f32[104,128]{1,0:T(8,128)S(1)}, f32[104,128]{1,0:T(8,128)S(1)}, u32[]{:S(2)}, u32[]{:S(2)}) collective-permute-start(f32[104,128]{1,0:T(8,128)S(1)} %add_add_fusion.1.ma_ref), channel_id=1, source_target_pairs={{0,4},{1,5},{2,6},{3,7},{4,0},{5,1},{6,2},{7,3},{8,12},{9,13},{10,... | collective-permute-start | bytes 159752 | tf_op jit(solution)/shard_map/ppermute | solution.py:458
  18.6 1.6 %collective-permute-start.4 = (f32[2,256,128]{2,1,0:T(8,128)S(1)}, f32[2,256,128]{2,1,0:T(8,128)S(1)}, u32[]{:S(2)}, u32[]{:S(2)}) collective-permute-start(f32[2,256,128]{2,1,0:T(8,128)S(1)} %get-tuple-element.68), channel_id=1, source_target_pairs={{0,8},{8,0},{16,24},{24,16},{1,9},{9,1},{17,25},{25,17},{2,10},{10... | collective-permute-start | bytes 786440 | tf_op jit(solution)/shard_map/ppermute | solution.py:361
  20.4 5.6 %collective-permute-start.5 = (f32[256,128]{1,0:T(8,128)S(1)}, f32[256,128]{1,0:T(8,128)S(1)}, u32[]{:S(2)}, u32[]{:S(2)}) collective-permute-start(f32[256,128]{1,0:T(8,128)S(1)} %get-tuple-element.71), channel_id=1, source_target_pairs={{0,16},{8,24},{16,0},{24,8},{1,17},{9,25},{17,1},{25,9},{2,18},{10... | collective-permute-start | bytes 393224 | tf_op jit(solution)/shard_map/ppermute | solution.py:369
  26.0 1.4 %collective-permute-start.6 = (f32[256,128]{1,0:T(8,128)S(1)}, f32[256,128]{1,0:T(8,128)S(1)}, u32[]{:S(2)}, u32[]{:S(2)}) collective-permute-start(f32[256,128]{1,0:T(8,128)S(1)} %get-tuple-element.75), channel_id=1, source_target_pairs={{0,8},{8,0},{16,24},{24,16},{1,9},{9,1},{17,25},{25,17},{2,10},{10... | collective-permute-start | bytes 393224 | tf_op jit(solution)/shard_map/ppermute | solution.py:361
  28.0 5.8 %collective-permute-start.9 = (f32[104,128]{1,0:T(8,128)S(1)}, f32[104,128]{1,0:T(8,128)S(1)}, u32[]{:S(2)}, u32[]{:S(2)}) collective-permute-start(f32[104,128]{1,0:T(8,128)S(1)} %get-tuple-element.77), channel_id=1, source_target_pairs={{0,3},{1,2},{2,1},{3,0},{4,7},{5,6},{6,5},{7,4},{8,11},{9,10},{10,... | collective-permute-start | bytes 159752 | tf_op jit(solution)/shard_map/ppermute | solution.py:458
  29.6 4.2 %collective-permute-start.8 = (f32[104,128]{1,0:T(8,128)S(1)}, f32[104,128]{1,0:T(8,128)S(1)}, u32[]{:S(2)}, u32[]{:S(2)}) collective-permute-start(f32[104,128]{1,0:T(8,128)S(1)} %get-tuple-element.77), channel_id=1, source_target_pairs={{0,2},{1,3},{2,0},{3,1},{4,6},{5,7},{6,4},{7,5},{8,10},{9,11},{10,... | collective-permute-start | bytes 159752 | tf_op jit(solution)/shard_map/ppermute | solution.py:458
  30.0 4.1 %collective-permute-start.7 = (f32[104,128]{1,0:T(8,128)S(1)}, f32[104,128]{1,0:T(8,128)S(1)}, u32[]{:S(2)}, u32[]{:S(2)}) collective-permute-start(f32[104,128]{1,0:T(8,128)S(1)} %get-tuple-element.77), channel_id=1, source_target_pairs={{0,1},{1,0},{2,3},{3,2},{4,5},{5,4},{6,7},{7,6},{8,9},{9,8},{10,11... | collective-permute-start | bytes 159752 | tf_op jit(solution)/shard_map/ppermute | solution.py:458
  34.1 5.3 %collective-permute-start.10 = (f32[104,128]{1,0:T(8,128)S(1)}, f32[104,128]{1,0:T(8,128)S(1)}, u32[]{:S(2)}, u32[]{:S(2)}) collective-permute-start(f32[104,128]{1,0:T(8,128)S(1)} %add_add_fusion), channel_id=1, source_target_pairs={{0,4},{1,5},{2,6},{3,7},{4,0},{5,1},{6,2},{7,3},{8,12},{9,13},{10,... | collective-permute-start | bytes 159752 | tf_op jit(solution)/shard_map/ppermute | solution.py:458

commit v4 on v3

--- a/solution.py
+++ b/solution.py
@@ -10,6 +10,7 @@
 NZ = 32
 KAPPA_CELL = 0.02
 LOG2E = 1.4426950408889634
+RATIO = -2.0 / LOG2E
 SHEAR = 0.19
 NMOM = 13
 ROWS = 16
@@ -64,13 +65,16 @@
     z = cross_ref[1:2, :]
     xx, yy, zz = x * x, y * y, z * z
     square = xx + yy + zz
-    rows_ref[...] = jnp.concatenate([x, y, z] + [jnp.zeros_like(x)] * 5, axis=0)
+    stacked = jnp.concatenate([x, y, z] + [jnp.zeros_like(x)] * 5, axis=0)
+    for h in range(2):
+        rows_ref[h] = stacked[:, h * (count // 2) : (h + 1) * (count // 2)]
     rows = [jnp.ones_like(x), x, y, z, xx, yy, zz, x * y, x * z, y * z, x * square, y * square, z * square]
     rows += [jnp.zeros_like(x)] * (ROWS - NMOM)
     full = jnp.concatenate(rows, axis=0) * (weight_ref[...] * (1.0 / total))
     high, low = split(full)
     table = jnp.concatenate([high, low], axis=0)
-    table_ref[...] = table
+    for h in range(2):
+        table_ref[h] = table[:, h * (count // 2) : (h + 1) * (count // 2)]
     for c in range(chunks):
         parts[c].wait()
         tab = table[:, c * chunk : (c + 1) * chunk]
@@ -98,8 +102,8 @@
         out_specs=[whole] * 4,
         out_shape=[
             pltpu.VMEM((NMOM * nx, lanes), jnp.float32),
-            pltpu.VMEM((2 * ROWS, count), jnp.bfloat16),
-            pltpu.VMEM((8, count), jnp.float32),
+            pltpu.VMEM((2, 2 * ROWS, count // 2), jnp.bfloat16),
+            pltpu.VMEM((2, 8, count // 2), jnp.float32),
             pltpu.VMEM(dist.shape, jnp.float32),
         ],
         scratch_shapes=[
@@ -115,10 +119,17 @@
     )(*[pltpu.with_memory_space_constraint(a, pltpu.HBM) for a in (side, speed, cross, weight, dist)])
 
 
-def slope_kernel(nx, start, rows_ref, dist_ref, slope_ref, speed_ref, feature_ref, comp_ref):
+def half_index(own):
+    core = lax.axis_index("gx") % 2
+    return core if own else 1 - core
+
+
+def slope_kernel(nx, own, rows_ref, dist_ref, slope_ref, speed_ref, feature_ref, comp_ref):
     count = slope_ref.shape[1]
     lanes = dist_ref.shape[1]
-    rows = rows_ref[:, start : start + count]
+    half = half_index(own)
+    start = pl.multiple_of(half * count, count)
+    rows = rows_ref[half]
     columns = jnp.transpose(rows)
     speed_ref[...] = jnp.broadcast_to(jnp.abs(columns[:, 0:1]), (count, lanes))
     for k in range(2):
@@ -149,11 +160,11 @@
     lax.fori_loop(0, count // group, one, 0)
 
 
-def slopes(nx, half, halves, rows, dist):
-    count, lanes = rows.shape[1] // halves, dist.shape[1]
-    whole = pl.BlockSpec(memory_space=pltpu.VMEM)
-    return pl.pallas_call(
-        functools.partial(slope_kernel, nx, half * count),
+def slopes(nx, own, rows, dist):
+    count, lanes = rows.shape[2], dist.shape[1]
+    whole = pl.BlockSpec(memory_space=pltpu.VMEM)
+    return pl.pallas_call(
+        functools.partial(slope_kernel, nx, own),
         in_specs=[whole] * 2,
         out_specs=[whole] * 3,
         out_shape=[
@@ -168,11 +179,8 @@
     )(rows, dist)
 
 
-def map_kernel(nx, halves, ma_ref, mb_ref, rows_ref, *refs):
-    slopes_in, speeds, features = (refs[i * halves : (i + 1) * halves] for i in range(3))
-    decay_ref, source_ref, send_ref, sign_ref, state, bulk_terms, flux_terms = refs[3 * halves :]
-    count, lanes = decay_ref.shape[1:]
-    part = count // halves
+def state_of(nx, ma_ref, mb_ref, state, bulk_terms, flux_terms):
+    lanes = ma_ref.shape[1]
     m = [ma_ref[k * nx : (k + 1) * nx, :] + mb_ref[k * nx : (k + 1) * nx, :] for k in range(NMOM)]
     n = m[0]
     inv_n = 1.0 / n
@@ -184,8 +192,7 @@
     inv_t = 1.0 / temp
     nu = KAPPA_CELL * n * jnp.exp(SHEAR * jnp.log(temp))
     rate = inv_t * (-0.5 * LOG2E)
-    ratio = -2.0 / LOG2E
-    flux_scale = inv_n * inv_t * inv_t * (ratio / 15.0)
+    flux_scale = inv_n * inv_t * inv_t * (RATIO / 15.0)
     q = []
     for k in range(3):
         inner = u[0] * second[k][0] + u[1] * second[k][1] + u[2] * second[k][2]
@@ -201,11 +208,13 @@
         ref[6 * TERMS * nx :, :] = jnp.zeros(((32 - 6 * TERMS) * nx, lanes), jnp.float32)
     state[0] = nu * n * inv_t * jnp.sqrt(inv_t)
     state[1] = nu
-    sign_ref[...] = jnp.broadcast_to(rows_ref[0:1, 0:1], (8, lanes))
-    forward = rows_ref[0:1, 0:1][0, 0] > 0
+
+
+def sweep(nx, sign_ref, state, bulk_terms, flux_terms, slope_ref, speed_ref, feature_ref, decay_ref, source_ref, send_ref):
+    count, lanes = speed_ref.shape
+    forward = sign_ref[0:1, 0:1][0, 0] > 0
     rest = jnp.zeros((DEPTH - 32, 2 * lanes), jnp.bfloat16)
     group = 32
-
     for j in range(nx):
         at_x = jnp.where(forward, j, nx - 1 - j)
         before = jnp.where(forward, j - 1, nx - j)
@@ -213,54 +222,74 @@
         rate_x = jnp.broadcast_to(state[1, pl.ds(at_x, 1), :], (group, lanes))
         cells = jnp.concatenate([ref[pl.ds(at_x, 32, stride=nx), :] for ref in (bulk_terms, flux_terms)], axis=1)
         cells = jnp.concatenate([cells.astype(jnp.bfloat16), rest], axis=0)
-        for h in range(halves):
-            both = jnp.dot(features[h][...], cells, preferred_element_type=jnp.float32)
-            for at in range(0, part, group):
-                own = slice(at, at + group)
-                rows = slice(h * part + at, h * part + at + group)
-                exponent, wq = both[own, :lanes], both[own, lanes:]
-                shape = 1.0 + wq * (exponent - 5.0 / ratio)
-                target = scale * jnp.exp2(exponent) * shape
-                speed = speeds[h][own, :]
-                inv = 1.0 / (speed + rate_x)
-                decay = speed * inv
-                source = (target - slopes_in[h][at_x, own, :]) * inv
-                if j > 0:
-                    source = decay * source_ref[before, rows, :] + source
-                    decay = decay * decay_ref[before, rows, :]
-                decay_ref[at_x, rows, :] = decay
-                source_ref[at_x, rows, :] = source
-
-    last = jnp.where(forward, nx - 1, 0)
-    theirs = pl.ds(pl.multiple_of((1 - lax.axis_index("gx") % 2) * (count // 2), count // 2), count // 2)
-    send_ref[0] = decay_ref[last, theirs, :]
-    send_ref[1] = source_ref[last, theirs, :]
-
-
-def maps(nx, ma, mb, rows, parts):
-    lanes = ma.shape[1]
-    halves, count = len(parts), rows.shape[1]
+        both = jnp.dot(feature_ref[...], cells, preferred_element_type=jnp.float32)
+        for at in range(0, count, group):
+            rows = slice(at, at + group)
+            exponent, wq = both[rows, :lanes], both[rows, lanes:]
+            shape = 1.0 + wq * (exponent - 5.0 / RATIO)
+            target = scale * jnp.exp2(exponent) * shape
+            speed = speed_ref[rows, :]
+            inv = 1.0 / (speed + rate_x)
+            decay = speed * inv
+            source = (target - slope_ref[at_x, rows, :]) * inv
+            if j > 0:
+                source = decay * source_ref[before, rows, :] + source
+                decay = decay * decay_ref[before, rows, :]
+            decay_ref[at_x, rows, :] = decay
+            source_ref[at_x, rows, :] = source
+            if send_ref is not None and j == nx - 1:
+                send_ref[0, rows, :] = decay
+                send_ref[1, rows, :] = source
+
+
+def partner_kernel(nx, ma_ref, mb_ref, rows_ref, slope_ref, speed_ref, feature_ref,
+                   decay_ref, source_ref, send_ref, sign_ref, state, bulk_terms, flux_terms):
+    state_of(nx, ma_ref, mb_ref, state, bulk_terms, flux_terms)
+    sign_ref[...] = jnp.broadcast_to(rows_ref[0, 0:1, 0:1], sign_ref.shape)
+    sweep(nx, sign_ref, state, bulk_terms, flux_terms, slope_ref, speed_ref, feature_ref, decay_ref, source_ref, send_ref)
+
+
+def partner_maps(nx, ma, mb, rows, part):
+    count, lanes = part[1].shape
     whole = pl.BlockSpec(memory_space=pltpu.VMEM)
     field = pltpu.VMEM((nx, count, lanes), jnp.float32)
-    return pl.pallas_call(
-        functools.partial(map_kernel, nx, halves),
-        in_specs=[whole] * (3 + 3 * halves),
-        out_specs=[whole] * 4,
+    terms = pltpu.VMEM((32 * nx, lanes), jnp.float32)
+    return pl.pallas_call(
+        functools.partial(partner_kernel, nx),
+        in_specs=[whole] * 6,
+        out_specs=[whole] * 7,
         out_shape=[
             field,
             field,
-            pltpu.VMEM((2, count // 2, lanes), jnp.float32),
+            pltpu.VMEM((2, count, lanes), jnp.float32),
             pltpu.VMEM((8, lanes), jnp.float32),
+            pltpu.VMEM((2, nx, lanes), jnp.float32),
+            terms,
+            terms,
         ],
-        scratch_shapes=[
-            pltpu.VMEM((2, nx, lanes), jnp.float32),
-            pltpu.VMEM((32 * nx, lanes), jnp.float32),
-            pltpu.VMEM((32 * nx, lanes), jnp.float32),
-        ],
         compiler_params=params(),
         cost_estimate=cost(40 * count * nx * lanes, 12 * count * nx * lanes),
-        name="maps",
-    )(ma, mb, rows, *[p[i] for i in range(3) for p in parts])
+        name="partner_maps",
+    )(ma, mb, rows, *part)
+
+
+def own_kernel(nx, sign_ref, state, bulk_terms, flux_terms, slope_ref, speed_ref, feature_ref, decay_ref, source_ref):
+    sweep(nx, sign_ref, state, bulk_terms, flux_terms, slope_ref, speed_ref, feature_ref, decay_ref, source_ref, None)
+
+
+def own_maps(nx, sign, state, part):
+    count, lanes = part[1].shape
+    whole = pl.BlockSpec(memory_space=pltpu.VMEM)
+    field = pltpu.VMEM((nx, count, lanes), jnp.float32)
+    return pl.pallas_call(
+        functools.partial(own_kernel, nx),
+        in_specs=[whole] * 7,
+        out_specs=[whole] * 2,
+        out_shape=[field, field],
+        compiler_params=params(),
+        cost_estimate=cost(40 * count * nx * lanes, 12 * count * nx * lanes),
+        name="own_maps",
+    )(sign, *state, *part)
 
 
 def standing(sign_ref):
@@ -270,17 +299,12 @@
     return jnp.where(forward, core, 1 - core) == 0, jnp.where(forward, chip, chips - 1 - chip)
 
 
-def half_of(ref_rows, which):
-    half = ref_rows // 2
-    return pl.ds(pl.multiple_of(which * half, half), half)
-
-
 def compose_kernel(nx, sign_ref, got_ref, decay_ref, source_ref, inflow_ref, near_ref, face_ref, entry_ref, *chip_ref):
     first, _ = standing(sign_ref)
-    core = lax.axis_index("gx") % 2
-    mine = half_of(inflow_ref.shape[0], core)
+    half = entry_ref.shape[0]
+    mine = pl.ds(pl.multiple_of(half_index(True) * half, half), half)
     last = jnp.where(sign_ref[0:1, 0:1][0, 0] > 0, nx - 1, 0)
-    decay, source = decay_ref[last, mine, :], source_ref[last, mine, :]
+    decay, source = decay_ref[last], source_ref[last]
     got_decay, got_source = got_ref[0], got_ref[1]
     near_decay = jnp.where(first, decay, got_decay)
     near_source = jnp.where(first, source, got_source)
@@ -371,74 +395,75 @@
     return lax.ppermute(face, "gx", pairs[:2]), lax.ppermute(face, "gx", pairs[2:])
 
 
-def entries(nx, sign, decay, source, send, inflow, side):
-    near, face, entry, *chip = compose_chip(nx, sign, chip_exchange(send), decay, source, inflow)
-    got = entry
-    chips = lax.axis_size("gx") // 2
-    for step in range(chips - 1):
-        if step > 0:
-            entry, face = pass_face(step, sign, got, entry, chip[0])
-        low, high = chip_hop(face, step)
-        got = low if low is high else jnp.where(side[0] == 1, low, high)
-    keep, share = share_entry(chips - 1, sign, got, entry, near)
-    return keep, chip_exchange(share)
-
-
-def whole_entry(keep_ref, got_ref, entry_ref):
-    count = entry_ref.shape[0]
-    core = lax.axis_index("gx") % 2
-    entry_ref[half_of(count, core), :] = keep_ref[...]
-    entry_ref[half_of(count, 1 - core), :] = got_ref[...]
-
-
-def new_moments_kernel(nx, keep_ref, got_ref, table_ref, decay_ref, source_ref, mom_ref, entry_ref):
-    whole_entry(keep_ref, got_ref, entry_ref)
+def new_moments_kernel(nx, own, entry_ref, table_ref, decay_ref, source_ref, *refs):
+    mom_ref = refs[-1]
     entry = entry_ref[...]
     lanes = entry.shape[1]
-    table = table_ref[...]
+    table = table_ref[half_index(own)]
     for i in range(0, nx, 2):
         pair = range(min(2, nx - i))
         planes = [decay_ref[i + k] * entry + source_ref[i + k] for k in pair]
         got = project(table, jnp.concatenate(planes, axis=1))
         for k in pair:
-            mom_ref[pl.ds(i + k, NMOM, stride=nx), :] = got[:NMOM, k * lanes : (k + 1) * lanes]
-
-
-def new_moments(nx, keep, got, table, decay, source):
-    count, lanes = decay.shape[1:]
-    whole = pl.BlockSpec(memory_space=pltpu.VMEM)
-    return pl.pallas_call(
-        functools.partial(new_moments_kernel, nx),
-        in_specs=[whole] * 5,
-        out_specs=[whole] * 2,
-        out_shape=[pltpu.VMEM((NMOM * nx, lanes), jnp.float32), pltpu.VMEM((count, lanes), jnp.float32)],
+            part = got[:NMOM, k * lanes : (k + 1) * lanes]
+            place = pl.ds(i + k, NMOM, stride=nx)
+            mom_ref[place, :] = part + refs[0][place, :] if len(refs) > 1 else part
+
+
+def new_moments(nx, own, entry, table, decay, source, *more):
+    count, lanes = entry.shape
+    whole = pl.BlockSpec(memory_space=pltpu.VMEM)
+    return pl.pallas_call(
+        functools.partial(new_moments_kernel, nx, own),
+        in_specs=[whole] * (4 + len(more)),
+        out_specs=whole,
+        out_shape=pltpu.VMEM((NMOM * nx, lanes), jnp.float32),
         compiler_params=params(),
         cost_estimate=cost(2 * 48 * count * nx * lanes, 8 * count * nx * lanes),
         name="new_moments",
-    )(keep, got, table, decay, source)
-
-
-def write_kernel(nx, entry_ref, decay_ref, source_ref, dist_ref):
-    entry = entry_ref[...]
-    count = entry.shape[0]
-    for i in range(nx):
-        dist_ref[pl.ds(i, count, stride=nx), :] = decay_ref[i] * entry + source_ref[i]
-
-
-def write_dist(nx, entry, decay, source):
-    count, lanes = entry.shape
-    chunk = min(count, 128)
-    field = pl.BlockSpec((nx, chunk, lanes), lambda i: (0, i, 0))
-    return pl.pallas_call(
-        functools.partial(write_kernel, nx),
-        grid=(count // chunk,),
-        in_specs=[pl.BlockSpec((chunk, lanes), lambda i: (i, 0)), field, field],
-        out_specs=pl.BlockSpec((chunk * nx, lanes), lambda i: (i, 0)),
-        out_shape=jax.ShapeDtypeStruct((count * nx, lanes), jnp.float32),
-        compiler_params=params(),
-        cost_estimate=cost(2 * count * nx * lanes, 12 * count * nx * lanes),
+    )(entry, table, decay, source, *more)
+
+
+def write_kernel(nx, pieces, *refs):
+    halves, (out_hbm, held, sems) = (refs[:3], refs[3:6]), refs[6:]
+    half, lanes = halves[0][0].shape
+    size = half // pieces
+    copies = []
+    for h, (entry_ref, decay_ref, source_ref) in enumerate(halves):
+        start = half_index(h == 0) * half
+        for p in range(pieces):
+            rows = slice(p * size, (p + 1) * size)
+            entry = entry_ref[rows, :]
+            base = (h * half + p * size) * nx
+            for i in range(nx):
+                held[pl.ds(base + i, size, stride=nx), :] = decay_ref[i, rows, :] * entry + source_ref[i, rows, :]
+            to = pl.ds(pl.multiple_of((start + p * size) * nx, size * nx), size * nx)
+            copy = pltpu.make_async_copy(
+                held.at[pl.ds(base, size * nx), :], out_hbm.at[to, :], sems.at[h * pieces + p]
+            )
+            copy.start()
+            copies.append(copy)
+    for copy in copies:
+        copy.wait()
+
+
+def write_dist(nx, *halves):
+    half, lanes = halves[0].shape
+    pieces = max(1, half // 64)
+    whole = pl.BlockSpec(memory_space=pltpu.VMEM)
+    return pl.pallas_call(
+        functools.partial(write_kernel, nx, pieces),
+        in_specs=[whole] * 6,
+        out_specs=pl.BlockSpec(memory_space=pltpu.HBM),
+        out_shape=jax.ShapeDtypeStruct((2 * half * nx, lanes), jnp.float32),
+        scratch_shapes=[
+            pltpu.VMEM((2 * half * nx, lanes), jnp.float32),
+            pltpu.SemaphoreType.DMA((2 * pieces,)),
+        ],
+        compiler_params=params(),
+        cost_estimate=cost(4 * half * nx * lanes, 24 * half * nx * lanes),
         name="write_dist",
-    )(entry, decay, source)
+    )(*halves)
 
 
 def stages_of(n):
@@ -484,18 +509,32 @@
     flat = dist.reshape(count * nx, lanes)
     row = lambda a: a.reshape(1, count)
     partial, table, rows, held = old_moments(total, nx, row(side), row(speed_x), transverse, row(quad_weight), flat)
-    halves = 2 if count % 256 == 0 else 1
-
-    def slope_part(h):
-        return lambda sent: slopes(nx, h, halves, *lax.optimization_barrier((rows, held, sent))[:2])
-
-    (ma, mb), made = partial_sums(partial, "vert", [slope_part(h) for h in range(halves)])
-    decay, source, send, sign = maps(nx, ma, mb, rows, made)
-    keep, got = entries(nx, sign, decay, source, send, inflow, side)
-    new_partial, entry = new_moments(nx, keep, got, table, decay, source)
+
+    def slope_half(own):
+        return lambda sent: slopes(nx, own, *lax.optimization_barrier((rows, held, sent))[:2])
+
+    (ma, mb), (part, own_part) = partial_sums(partial, "vert", [slope_half(False), slope_half(True)])
+    decay, source, send, sign, *state = partner_maps(nx, ma, mb, rows, part)
+    arrived = chip_exchange(send)
+    own_decay, own_source = own_maps(nx, sign, state, own_part)
+    arrived, own_decay, own_source = lax.optimization_barrier((arrived, own_decay, own_source))
+    near, face, entry, *chip = compose_chip(nx, sign, arrived, own_decay, own_source, inflow)
+    got = entry
+    chips = lax.axis_size("gx") // 2
+    for step in range(chips - 1):
+        if step > 0:
+            entry, face = pass_face(step, sign, got, entry, chip[0])
+        low, high = chip_hop(face, step)
+        got = low if low is high else jnp.where(side[0] == 1, low, high)
+    keep, share = share_entry(chips - 1, sign, got, entry, near)
+    other = chip_exchange(share)
+    own_moments = new_moments(nx, True, keep, table, own_decay, own_source)
+    other, own_moments = lax.optimization_barrier((other, own_moments))
+    new_partial = new_moments(nx, False, other, table, decay, source, own_moments)
 
     def write(sent):
-        return write_dist(nx, *lax.optimization_barrier((entry, decay, source, sent))[:3])
+        args = lax.optimization_barrier((keep, own_decay, own_source, other, decay, source, sent))[:6]
+        return write_dist(nx, *args)
 
     (na, nb), (new_flat,) = partial_sums(new_partial, "vert", [write])
     return new_flat.reshape(count, nx, lanes), (na + nb).reshape(NMOM, nx, lanes)

time: 40.2 us -> 38.7 us (0.963)
  Pallas kernels: 12 us -> 11 us
    ppermute x2, waiting for transfers between devices: 2.86 us -> 1.59 us  [chip_exchange(): return lax.ppermute(a, 'gx', [(i, i ^ 1) for i in range(n)])]
    pallas_call x5 -> x7, Pallas kernels: 9.74 us -> 8.71 us  [the longest x2 4.71 us: slopes(): pl.pallas_call(functools.partial(slope_kernel, nx, own), in_specs=[whole]...]
    ppermute x8, waiting for transfers between devices: 4.42 us -> 5.25 us  [exchange(): return lax.ppermute(a, axis, [(i, i ^ mask) for i in range(n)])]
  transfers between devices with their start and end apart: 11 -> 11, of which waited for: 8 -> 10; matrix products, arithmetic and copies ran while one was open for 0% -> 0% of each run, Pallas kernels for 17% -> 19%
where the time goes in v4:
time: 38.7 us; the launch traced here: 38.6 us
  starting transfers between devices  15.4 us (40%)
  Pallas kernels  11 us (28%)
  waiting for transfers between devices  10.9 us (28%)
  between operations  0.72 us (2%)
  other arithmetic  0.67 us (2%)
    ppermute x8, starting transfers between devices, exchange(): return lax.ppermute(a, axis, [(i, i ^ mask) for i in range(n)])  13.6 us
    ppermute x8, waiting for transfers between devices, exchange(): return lax.ppermute(a, axis, [(i, i ^ mask) for i in range(n)])  5.25 us
    pallas_call x2, Pallas kernels, slopes(): pl.pallas_call(functools.partial(slope_kernel, nx, own), in_specs=[whole]...  4.71 us
    ppermute x1, waiting for transfers between devices, chip_hop(): got = lax.ppermute(face, 'gx', pairs)  4.01 us
    pallas_call x1, Pallas kernels, old_moments(): pl.pallas_call(functools.partial(moments_kernel, total, nx, chunks), in_s...  2.07 us
    ppermute x1, starting transfers between devices, chip_hop(): got = lax.ppermute(face, 'gx', pairs)  1.59 us
    ppermute x2, waiting for transfers between devices, chip_exchange(): return lax.ppermute(a, 'gx', [(i, i ^ 1) for i in range(n)])  1.59 us
    pallas_call x1, Pallas kernels, write_dist(): pl.pallas_call(functools.partial(write_kernel, nx, pieces), in_specs=[who...  1.44 us
  transfers between devices with their start and end apart: 11, of which 10 were waited for; matrix products, arithmetic and copies ran while one was open for 0% of the time, Pallas kernels for 19%

profile of v4, /device:TPU:0, one launch (start us, length us, event | category | flops | bytes accessed | tf_op | source)
XLA Modules:
  0.0 38.6 jit_solution(1093510428800815379)
XLA Ops:
  0.6 2.1 %moments.1 = (f32[104,128]{1,0:T(8,128)S(1)}, bf16[2,32,256]{2,1,0:T(8,128)(2,1)S(1)}, f32[2,8,256]{2,1,0:T(8,128)S(1)}, f32[4096,128]{1,0:T(8,128)S(1)}) custom-call(s32[1,512]{1,0:T(1,128)} %bitcast.9, f32[1,512]{1,0:T(1,128)} %bitcast.10, f32[2,512]{1,0:T(2,128)} %cross_hbm.1, f32[1,512]{1,0:T(1,128)} %bitcast.11, f32[4096,128]{1,0:T(8,128)} %bitcast.8), custom_call_target="tpu_custom_call" | custom-call | flops 50331648 | bytes 2097152 | tf_op jit(solution)/shard_map/moments/pallas_call | solution.py:99
  2.7 4.0 %collective-permute-start.2 = (f32[104,128]{1,0:T(8,128)S(1)}, f32[104,128]{1,0:T(8,128)S(1)}, u32[]{:S(2)}, u32[]{:S(2)}) collective-permute-start(f32[104,128]{1,0:T(8,128)S(1)} %get-tuple-element.55), channel_id=1, source_target_pairs={{0,3},{1,2},{2,1},{3,0},{4,7},{5,6},{6,5},{7,4},{8,11},{9,10},{10,... | collective-permute-start | bytes 159752 | tf_op jit(solution)/shard_map/ppermute | solution.py:483
  6.7 0.4 %collective-permute-start.1 = (f32[104,128]{1,0:T(8,128)S(1)}, f32[104,128]{1,0:T(8,128)S(1)}, u32[]{:S(2)}, u32[]{:S(2)}) collective-permute-start(f32[104,128]{1,0:T(8,128)S(1)} %get-tuple-element.55), channel_id=1, source_target_pairs={{0,2},{1,3},{2,0},{3,1},{4,6},{5,7},{6,4},{7,5},{8,10},{9,11},{10,... | collective-permute-start | bytes 159752 | tf_op jit(solution)/shard_map/ppermute | solution.py:483
  7.2 0.2 collective-permute-start
  7.4 2.4 %slope.2 = (f32[8,256,128]{2,1,0:T(8,128)S(1)}, f32[256,128]{1,0:T(8,128)S(1)}, bf16[256,128]{1,0:T(8,128)(2,1)S(1)}) custom-call(f32[2,8,256]{2,1,0:T(8,128)S(1)} %get-tuple-element.66.rows_ref, f32[4096,128]{1,0:T(8,128)S(1)} %get-tuple-element.67.dist_ref), custom_call_target="tpu_custom_call" | custom-call | flops 5242880 | bytes 2097152 | tf_op jit(solution)/shard_map/slope/pallas_call | solution.py:166
  9.7 0.0 collective-permute-done.2
  9.7 1.1 %collective-permute-done.1 = f32[104,128]{1,0:T(8,128)S(1)} collective-permute-done((f32[104,128]{1,0:T(8,128)S(1)}, f32[104,128]{1,0:T(8,128)S(1)}, u32[]{:S(2)}, u32[]{:S(2)}) %collective-permute-start.1) | collective-permute-done | bytes 53280 | tf_op jit(solution)/shard_map/ppermute | solution.py:483
  10.9 0.4 %collective-permute-done = f32[104,128]{1,0:T(8,128)S(1)} collective-permute-done((f32[104,128]{1,0:T(8,128)S(1)}, f32[104,128]{1,0:T(8,128)S(1)}, u32[]{:S(2)}, u32[]{:S(2)}) %collective-permute-start) | collective-permute-done | bytes 53280 | tf_op jit(solution)/shard_map/ppermute | solution.py:483
  11.3 0.0 copy-start
  11.3 2.7 %collective-permute-start.3 = (f32[104,128]{1,0:T(8,128)S(1)}, f32[104,128]{1,0:T(8,128)S(1)}, u32[]{:S(2)}, u32[]{:S(2)}) collective-permute-start(f32[104,128]{1,0:T(8,128)S(1)} %add_add_fusion.1.ma_ref), channel_id=1, source_target_pairs={{0,4},{1,5},{2,6},{3,7},{4,0},{5,1},{6,2},{7,3},{8,12},{9,13},{10,... | collective-permute-start | bytes 159752 | tf_op jit(solution)/shard_map/ppermute | solution.py:483
  14.0 2.4 %slope.3 = (f32[8,256,128]{2,1,0:T(8,128)S(1)}, f32[256,128]{1,0:T(8,128)S(1)}, bf16[256,128]{1,0:T(8,128)(2,1)S(1)}) custom-call(f32[2,8,256]{2,1,0:T(8,128)S(1)} %get-tuple-element.66.rows_ref, f32[4096,128]{1,0:T(8,128)S(1)} %get-tuple-element.67.dist_ref), custom_call_target="tpu_custom_call" | custom-call | flops 5242880 | bytes 2097152 | tf_op jit(solution)/shard_map/slope/pallas_call | solution.py:166
  16.4 0.1 collective-permute-done.3.mb_ref
  16.4 1.0 %partner_maps.1 = (f32[8,256,128]{2,1,0:T(8,128)S(1)}, f32[8,256,128]{2,1,0:T(8,128)S(1)}, f32[2,256,128]{2,1,0:T(8,128)S(1)}, f32[8,128]{1,0:T(8,128)S(1)}, f32...) custom-call(f32[104,128]{1,0:T(8,128)S(1)} %add_add_fusion.1.ma_ref, ...), custom_call_target="tpu_custom_call" | custom-call | flops 10485760 | bytes 3145728 | tf_op jit(solution)/shard_map/partner_maps/pallas_call | solution.py:257
  17.4 0.1 collective-permute-start.4
  17.5 0.9 %own_maps.1 = (f32[8,256,128]{2,1,0:T(8,128)S(1)}, f32[8,256,128]{2,1,0:T(8,128)S(1)}) custom-call(f32[8,128]{1,0:T(8,128)S(1)} %get-tuple-element.75.sign_ref, f32[2,8,128]{2,1,0:T(8,128)S(1)} %get-tuple-element.77.state, f32[256,128]{1,0:T(8,128)S(1)} %get-tuple-element.78.bulk_terms, f32[256,128]{1,0:T(8,128)S(1)} %get-tuple-element.79.flux_terms, ...), custom_call_target="tpu_custom_call" | custom-call | flops 10485760 | bytes 3145728 | tf_op jit(solution)/shard_map/own_maps/pallas_call | solution.py:284
  18.4 0.6 %collective-permute-done.4.got_ref = f32[2,256,128]{2,1,0:T(8,128)S(1)} collective-permute-done((f32[2,256,128]{2,1,0:T(8,128)S(1)}, f32[2,256,128]{2,1,0:T(8,128)S(1)}, u32[]{:S(2)}, u32[]{:S(2)}) %collective-permute-start.4) | collective-permute-done | bytes 262176 | tf_op jit(solution)/shard_map/ppermute | solution.py:385
  19.0 0.0 copy-done
  19.0 0.1 compose.1
  19.2 1.6 %collective-permute-start.5 = (f32[256,128]{1,0:T(8,128)S(1)}, f32[256,128]{1,0:T(8,128)S(1)}, u32[]{:S(2)}, u32[]{:S(2)}) collective-permute-start(f32[256,128]{1,0:T(8,128)S(1)} %get-tuple-element.88), channel_id=1, source_target_pairs={{0,16},{8,24},{16,0},{24,8},{1,17},{9,25},{17,1},{25,9},{2,18},{10... | collective-permute-start | bytes 393224 | tf_op jit(solution)/shard_map/ppermute | solution.py:393
  20.8 4.0 %collective-permute-done.5.got_ref = f32[256,128]{1,0:T(8,128)S(1)} collective-permute-done((f32[256,128]{1,0:T(8,128)S(1)}, f32[256,128]{1,0:T(8,128)S(1)}, u32[]{:S(2)}, u32[]{:S(2)}) %collective-permute-start.5) | collective-permute-done | bytes 131104 | tf_op jit(solution)/shard_map/ppermute | solution.py:393
  24.8 0.1 collective-permute-start.6
  24.9 0.3 new_moments.2.refs_0_
  25.2 1.0 %collective-permute-done.6.entry_ref.refs_3_ = f32[256,128]{1,0:T(8,128)S(1)} collective-permute-done((f32[256,128]{1,0:T(8,128)S(1)}, f32[256,128]{1,0:T(8,128)S(1)}, u32[]{:S(2)}, u32[]{:S(2)}) %collective-permute-start.6) | collective-permute-done | bytes 131104 | tf_op jit(solution)/shard_map/ppermute | solution.py:385
  26.2 0.3 new_moments.3
  26.6 1.6 %collective-permute-start.9 = (f32[104,128]{1,0:T(8,128)S(1)}, f32[104,128]{1,0:T(8,128)S(1)}, u32[]{:S(2)}, u32[]{:S(2)}) collective-permute-start(f32[104,128]{1,0:T(8,128)S(1)} %new_moments.3), channel_id=1, source_target_pairs={{0,3},{1,2},{2,1},{3,0},{4,7},{5,6},{6,5},{7,4},{8,11},{9,10},{10,... | collective-permute-start | bytes 159752 | tf_op jit(solution)/shard_map/ppermute | solution.py:483
  28.1 0.4 collective-permute-start.8
  28.5 1.6 %collective-permute-start.7 = (f32[104,128]{1,0:T(8,128)S(1)}, f32[104,128]{1,0:T(8,128)S(1)}, u32[]{:S(2)}, u32[]{:S(2)}) collective-permute-start(f32[104,128]{1,0:T(8,128)S(1)} %new_moments.3), channel_id=1, source_target_pairs={{0,1},{1,0},{2,3},{3,2},{4,5},{5,4},{6,7},{7,6},{8,9},{9,8},{10,11... | collective-permute-start | bytes 159752 | tf_op jit(solution)/shard_map/ppermute | solution.py:483
  30.1 1.4 %write_dist.1 = f32[4096,128]{1,0:T(8,128)} custom-call(f32[256,128]{1,0:T(8,128)S(1)} %get-tuple-element.98.entry_ref.refs_0_, f32[8,256,128]{2,1,0:T(8,128)S(1)} %get-tuple-element.99.decay_ref.refs_1_, f32[8,256,128]{2,1,0:T(8,128)S(1)} %get-tuple-element.100.source_ref.refs_2_, f32[256,128]{1,0:T(8,128)S(1)} %collective-permute-done.6.entry_ref.refs_3_, ...), custom_call_target="tpu_custom_call" | custom-call | flops 1048576 | bytes 6291456 | tf_op jit(solution)/shard_map/write_dist/pallas_call | solution.py:454
  31.5 0.3 collective-permute-done.9
  31.8 0.5 %collective-permute-done.8 = f32[104,128]{1,0:T(8,128)S(1)} collective-permute-done((f32[104,128]{1,0:T(8,128)S(1)}, f32[104,128]{1,0:T(8,128)S(1)}, u32[]{:S(2)}, u32[]{:S(2)}) %collective-permute-start.8) | collective-permute-done | bytes 53280 | tf_op jit(solution)/shard_map/ppermute | solution.py:483
  32.3 0.4 collective-permute-done.7
  32.7 2.8 %collective-permute-start.10 = (f32[104,128]{1,0:T(8,128)S(1)}, f32[104,128]{1,0:T(8,128)S(1)}, u32[]{:S(2)}, u32[]{:S(2)}) collective-permute-start(f32[104,128]{1,0:T(8,128)S(1)} %add_add_fusion), channel_id=1, source_target_pairs={{0,4},{1,5},{2,6},{3,7},{4,0},{5,1},{6,2},{7,3},{8,12},{9,13},{10,... | collective-permute-start | bytes 159752 | tf_op jit(solution)/shard_map/ppermute | solution.py:483
  35.5 2.5 %collective-permute-done.10 = f32[104,128]{1,0:T(8,128)S(1)} collective-permute-done((f32[104,128]{1,0:T(8,128)S(1)}, f32[104,128]{1,0:T(8,128)S(1)}, u32[]{:S(2)}, u32[]{:S(2)}) %collective-permute-start.10) | collective-permute-done | bytes 53280 | tf_op jit(solution)/shard_map/ppermute | solution.py:483
  38.0 0.6 %add_bitcast_fusion = f32[13,8,128]{2,1,0:T(8,128)} fusion(f32[104,128]{1,0:T(8,128)S(1)} %add_add_fusion, f32[104,128]{1,0:T(8,128)S(1)} %collective-permute-done.10), kind=kLoop, calls=%fused_computation | loop fusion | flops 13312 | bytes 159744 | tf_op jit(solution)/shard_map/reshape | solution.py:540
  (3 shorter events, 0.1 us)
Async XLA Ops:
  2.7 7.0 %collective-permute-start.2 = (f32[104,128]{1,0:T(8,128)S(1)}, f32[104,128]{1,0:T(8,128)S(1)}, u32[]{:S(2)}, u32[]{:S(2)}) collective-permute-start(f32[104,128]{1,0:T(8,128)S(1)} %get-tuple-element.55), channel_id=1, source_target_pairs={{0,3},{1,2},{2,1},{3,0},{4,7},{5,6},{6,5},{7,4},{8,11},{9,10},{10,... | collective-permute-start | bytes 159752 | tf_op jit(solution)/shard_map/ppermute | solution.py:483
  6.7 4.1 %collective-permute-start.1 = (f32[104,128]{1,0:T(8,128)S(1)}, f32[104,128]{1,0:T(8,128)S(1)}, u32[]{:S(2)}, u32[]{:S(2)}) collective-permute-start(f32[104,128]{1,0:T(8,128)S(1)} %get-tuple-element.55), channel_id=1, source_target_pairs={{0,2},{1,3},{2,0},{3,1},{4,6},{5,7},{6,4},{7,5},{8,10},{9,11},{10,... | collective-permute-start | bytes 159752 | tf_op jit(solution)/shard_map/ppermute | solution.py:483
  7.2 4.1 %collective-permute-start = (f32[104,128]{1,0:T(8,128)S(1)}, f32[104,128]{1,0:T(8,128)S(1)}, u32[]{:S(2)}, u32[]{:S(2)}) collective-permute-start(f32[104,128]{1,0:T(8,128)S(1)} %get-tuple-element.55), channel_id=1, source_target_pairs={{0,1},{1,0},{2,3},{3,2},{4,5},{5,4},{6,7},{7,6},{8,9},{9,8},{10,11... | collective-permute-start | bytes 159752 | tf_op jit(solution)/shard_map/ppermute | solution.py:483
  11.3 7.7 %copy-start = (f32[512,128]{1,0:T(8,128)S(1)}, f32[512,128]{1,0:T(8,128)}, u32[]{:S(2)}) copy-start(f32[512,128]{1,0:T(8,128)} %inflow_ref.1) | copy-start | bytes 786436
  11.3 5.1 %collective-permute-start.3 = (f32[104,128]{1,0:T(8,128)S(1)}, f32[104,128]{1,0:T(8,128)S(1)}, u32[]{:S(2)}, u32[]{:S(2)}) collective-permute-start(f32[104,128]{1,0:T(8,128)S(1)} %add_add_fusion.1.ma_ref), channel_id=1, source_target_pairs={{0,4},{1,5},{2,6},{3,7},{4,0},{5,1},{6,2},{7,3},{8,12},{9,13},{10,... | collective-permute-start | bytes 159752 | tf_op jit(solution)/shard_map/ppermute | solution.py:483
  17.4 1.6 %collective-permute-start.4 = (f32[2,256,128]{2,1,0:T(8,128)S(1)}, f32[2,256,128]{2,1,0:T(8,128)S(1)}, u32[]{:S(2)}, u32[]{:S(2)}) collective-permute-start(f32[2,256,128]{2,1,0:T(8,128)S(1)} %get-tuple-element.76), channel_id=1, source_target_pairs={{0,8},{8,0},{16,24},{24,16},{1,9},{9,1},{17,25},{25,17},{2,10},{10... | collective-permute-start | bytes 786440 | tf_op jit(solution)/shard_map/ppermute | solution.py:385
  19.2 5.6 %collective-permute-start.5 = (f32[256,128]{1,0:T(8,128)S(1)}, f32[256,128]{1,0:T(8,128)S(1)}, u32[]{:S(2)}, u32[]{:S(2)}) collective-permute-start(f32[256,128]{1,0:T(8,128)S(1)} %get-tuple-element.88), channel_id=1, source_target_pairs={{0,16},{8,24},{16,0},{24,8},{1,17},{9,25},{17,1},{25,9},{2,18},{10... | collective-permute-start | bytes 393224 | tf_op jit(solution)/shard_map/ppermute | solution.py:393
  24.8 1.4 %collective-permute-start.6 = (f32[256,128]{1,0:T(8,128)S(1)}, f32[256,128]{1,0:T(8,128)S(1)}, u32[]{:S(2)}, u32[]{:S(2)}) collective-permute-start(f32[256,128]{1,0:T(8,128)S(1)} %get-tuple-element.91), channel_id=1, source_target_pairs={{0,8},{8,0},{16,24},{24,16},{1,9},{9,1},{17,25},{25,17},{2,10},{10... | collective-permute-start | bytes 393224 | tf_op jit(solution)/shard_map/ppermute | solution.py:385
  26.6 5.2 %collective-permute-start.9 = (f32[104,128]{1,0:T(8,128)S(1)}, f32[104,128]{1,0:T(8,128)S(1)}, u32[]{:S(2)}, u32[]{:S(2)}) collective-permute-start(f32[104,128]{1,0:T(8,128)S(1)} %new_moments.3), channel_id=1, source_target_pairs={{0,3},{1,2},{2,1},{3,0},{4,7},{5,6},{6,5},{7,4},{8,11},{9,10},{10,... | collective-permute-start | bytes 159752 | tf_op jit(solution)/shard_map/ppermute | solution.py:483
  28.1 4.1 %collective-permute-start.8 = (f32[104,128]{1,0:T(8,128)S(1)}, f32[104,128]{1,0:T(8,128)S(1)}, u32[]{:S(2)}, u32[]{:S(2)}) collective-permute-start(f32[104,128]{1,0:T(8,128)S(1)} %new_moments.3), channel_id=1, source_target_pairs={{0,2},{1,3},{2,0},{3,1},{4,6},{5,7},{6,4},{7,5},{8,10},{9,11},{10,... | collective-permute-start | bytes 159752 | tf_op jit(solution)/shard_map/ppermute | solution.py:483
  28.5 4.1 %collective-permute-start.7 = (f32[104,128]{1,0:T(8,128)S(1)}, f32[104,128]{1,0:T(8,128)S(1)}, u32[]{:S(2)}, u32[]{:S(2)}) collective-permute-start(f32[104,128]{1,0:T(8,128)S(1)} %new_moments.3), channel_id=1, source_target_pairs={{0,1},{1,0},{2,3},{3,2},{4,5},{5,4},{6,7},{7,6},{8,9},{9,8},{10,11... | collective-permute-start | bytes 159752 | tf_op jit(solution)/shard_map/ppermute | solution.py:483
  32.7 5.3 %collective-permute-start.10 = (f32[104,128]{1,0:T(8,128)S(1)}, f32[104,128]{1,0:T(8,128)S(1)}, u32[]{:S(2)}, u32[]{:S(2)}) collective-permute-start(f32[104,128]{1,0:T(8,128)S(1)} %add_add_fusion), channel_id=1, source_target_pairs={{0,4},{1,5},{2,6},{3,7},{4,0},{5,1},{6,2},{7,3},{8,12},{9,13},{10,... | collective-permute-start | bytes 159752 | tf_op jit(solution)/shard_map/ppermute | solution.py:483

commit v5 on v4

--- a/solution.py
+++ b/solution.py
@@ -215,31 +215,35 @@
     forward = sign_ref[0:1, 0:1][0, 0] > 0
     rest = jnp.zeros((DEPTH - 32, 2 * lanes), jnp.bfloat16)
     group = 32
+    places, cells = [], []
     for j in range(nx):
         at_x = jnp.where(forward, j, nx - 1 - j)
-        before = jnp.where(forward, j - 1, nx - j)
-        scale = jnp.broadcast_to(state[0, pl.ds(at_x, 1), :], (group, lanes))
-        rate_x = jnp.broadcast_to(state[1, pl.ds(at_x, 1), :], (group, lanes))
-        cells = jnp.concatenate([ref[pl.ds(at_x, 32, stride=nx), :] for ref in (bulk_terms, flux_terms)], axis=1)
-        cells = jnp.concatenate([cells.astype(jnp.bfloat16), rest], axis=0)
-        both = jnp.dot(feature_ref[...], cells, preferred_element_type=jnp.float32)
-        for at in range(0, count, group):
-            rows = slice(at, at + group)
-            exponent, wq = both[rows, :lanes], both[rows, lanes:]
+        both = jnp.concatenate([ref[pl.ds(at_x, 32, stride=nx), :] for ref in (bulk_terms, flux_terms)], axis=1)
+        places.append(at_x)
+        cells.append(jnp.concatenate([both.astype(jnp.bfloat16), rest], axis=0))
+    group = 64
+    for at in range(0, count, group):
+        rows = slice(at, at + group)
+        speed = speed_ref[rows, :]
+        run_decay = run_source = None
+        for j in range(nx):
+            at_x = places[j]
+            both = jnp.dot(feature_ref[rows, :], cells[j], preferred_element_type=jnp.float32)
+            exponent, wq = both[:, :lanes], both[:, lanes:]
             shape = 1.0 + wq * (exponent - 5.0 / RATIO)
-            target = scale * jnp.exp2(exponent) * shape
-            speed = speed_ref[rows, :]
-            inv = 1.0 / (speed + rate_x)
+            target = state[0, pl.ds(at_x, 1), :] * jnp.exp2(exponent) * shape
+            inv = 1.0 / (speed + state[1, pl.ds(at_x, 1), :])
             decay = speed * inv
             source = (target - slope_ref[at_x, rows, :]) * inv
             if j > 0:
-                source = decay * source_ref[before, rows, :] + source
-                decay = decay * decay_ref[before, rows, :]
+                source = decay * run_source + source
+                decay = decay * run_decay
+            run_decay, run_source = decay, source
             decay_ref[at_x, rows, :] = decay
             source_ref[at_x, rows, :] = source
-            if send_ref is not None and j == nx - 1:
-                send_ref[0, rows, :] = decay
-                send_ref[1, rows, :] = source
+        if send_ref is not None:
+            send_ref[0, rows, :] = run_decay
+            send_ref[1, rows, :] = run_source
 
 
 def partner_kernel(nx, ma_ref, mb_ref, rows_ref, slope_ref, speed_ref, feature_ref,

time: 38.7 us -> 38.5 us (level)
  Pallas kernels: 11 us -> 10.6 us
where the time goes in v5:
time: 38.5 us; the launch traced here: 38.4 us
  starting transfers between devices  15.4 us (40%)
  waiting for transfers between devices  11.1 us (29%)
  Pallas kernels  10.6 us (28%)
  between operations  0.72 us (2%)
  other arithmetic  0.67 us (2%)
    ppermute x8, starting transfers between devices, exchange(): return lax.ppermute(a, axis, [(i, i ^ mask) for i in range(n)])  13.6 us
    ppermute x8, waiting for transfers between devices, exchange(): return lax.ppermute(a, axis, [(i, i ^ mask) for i in range(n)])  5.25 us
    pallas_call x2, Pallas kernels, slopes(): pl.pallas_call(functools.partial(slope_kernel, nx, own), in_specs=[whole]...  4.71 us
    ppermute x1, waiting for transfers between devices, chip_hop(): got = lax.ppermute(face, 'gx', pairs)  4.02 us
    pallas_call x1, Pallas kernels, old_moments(): pl.pallas_call(functools.partial(moments_kernel, total, nx, chunks), in_s...  2.07 us
    ppermute x2, waiting for transfers between devices, chip_exchange(): return lax.ppermute(a, 'gx', [(i, i ^ 1) for i in range(n)])  1.8 us
    ppermute x1, starting transfers between devices, chip_hop(): got = lax.ppermute(face, 'gx', pairs)  1.58 us
    pallas_call x1, Pallas kernels, write_dist(): pl.pallas_call(functools.partial(write_kernel, nx, pieces), in_specs=[who...  1.44 us
  transfers between devices with their start and end apart: 11, of which 10 were waited for; matrix products, arithmetic and copies ran while one was open for 0% of the time, Pallas kernels for 19%

profile of v5, /device:TPU:0, one launch (start us, length us, event | category | flops | bytes accessed | tf_op | source)
XLA Modules:
  0.0 38.4 jit_solution(466943993637019916)
XLA Ops:
  0.6 2.1 %moments.1 = (f32[104,128]{1,0:T(8,128)S(1)}, bf16[2,32,256]{2,1,0:T(8,128)(2,1)S(1)}, f32[2,8,256]{2,1,0:T(8,128)S(1)}, f32[4096,128]{1,0:T(8,128)S(1)}) custom-call(s32[1,512]{1,0:T(1,128)} %bitcast.9, f32[1,512]{1,0:T(1,128)} %bitcast.10, f32[2,512]{1,0:T(2,128)} %cross_hbm.1, f32[1,512]{1,0:T(1,128)} %bitcast.11, f32[4096,128]{1,0:T(8,128)} %bitcast.8), custom_call_target="tpu_custom_call" | custom-call | flops 50331648 | bytes 2097152 | tf_op jit(solution)/shard_map/moments/pallas_call | solution.py:99
  2.7 4.0 %collective-permute-start.2 = (f32[104,128]{1,0:T(8,128)S(1)}, f32[104,128]{1,0:T(8,128)S(1)}, u32[]{:S(2)}, u32[]{:S(2)}) collective-permute-start(f32[104,128]{1,0:T(8,128)S(1)} %get-tuple-element.55), channel_id=1, source_target_pairs={{0,3},{1,2},{2,1},{3,0},{4,7},{5,6},{6,5},{7,4},{8,11},{9,10},{10,... | collective-permute-start | bytes 159752 | tf_op jit(solution)/shard_map/ppermute | solution.py:487
  6.7 0.4 %collective-permute-start.1 = (f32[104,128]{1,0:T(8,128)S(1)}, f32[104,128]{1,0:T(8,128)S(1)}, u32[]{:S(2)}, u32[]{:S(2)}) collective-permute-start(f32[104,128]{1,0:T(8,128)S(1)} %get-tuple-element.55), channel_id=1, source_target_pairs={{0,2},{1,3},{2,0},{3,1},{4,6},{5,7},{6,4},{7,5},{8,10},{9,11},{10,... | collective-permute-start | bytes 159752 | tf_op jit(solution)/shard_map/ppermute | solution.py:487
  7.2 0.2 collective-permute-start
  7.4 2.4 %slope.2 = (f32[8,256,128]{2,1,0:T(8,128)S(1)}, f32[256,128]{1,0:T(8,128)S(1)}, bf16[256,128]{1,0:T(8,128)(2,1)S(1)}) custom-call(f32[2,8,256]{2,1,0:T(8,128)S(1)} %get-tuple-element.66.rows_ref, f32[4096,128]{1,0:T(8,128)S(1)} %get-tuple-element.67.dist_ref), custom_call_target="tpu_custom_call" | custom-call | flops 5242880 | bytes 2097152 | tf_op jit(solution)/shard_map/slope/pallas_call | solution.py:166
  9.7 0.0 collective-permute-done.2
  9.7 1.1 %collective-permute-done.1 = f32[104,128]{1,0:T(8,128)S(1)} collective-permute-done((f32[104,128]{1,0:T(8,128)S(1)}, f32[104,128]{1,0:T(8,128)S(1)}, u32[]{:S(2)}, u32[]{:S(2)}) %collective-permute-start.1) | collective-permute-done | bytes 53280 | tf_op jit(solution)/shard_map/ppermute | solution.py:487
  10.9 0.4 %collective-permute-done = f32[104,128]{1,0:T(8,128)S(1)} collective-permute-done((f32[104,128]{1,0:T(8,128)S(1)}, f32[104,128]{1,0:T(8,128)S(1)}, u32[]{:S(2)}, u32[]{:S(2)}) %collective-permute-start) | collective-permute-done | bytes 53280 | tf_op jit(solution)/shard_map/ppermute | solution.py:487
  11.3 0.0 copy-start
  11.3 2.7 %collective-permute-start.3 = (f32[104,128]{1,0:T(8,128)S(1)}, f32[104,128]{1,0:T(8,128)S(1)}, u32[]{:S(2)}, u32[]{:S(2)}) collective-permute-start(f32[104,128]{1,0:T(8,128)S(1)} %add_add_fusion.1.ma_ref), channel_id=1, source_target_pairs={{0,4},{1,5},{2,6},{3,7},{4,0},{5,1},{6,2},{7,3},{8,12},{9,13},{10,... | collective-permute-start | bytes 159752 | tf_op jit(solution)/shard_map/ppermute | solution.py:487
  14.0 2.4 %slope.3 = (f32[8,256,128]{2,1,0:T(8,128)S(1)}, f32[256,128]{1,0:T(8,128)S(1)}, bf16[256,128]{1,0:T(8,128)(2,1)S(1)}) custom-call(f32[2,8,256]{2,1,0:T(8,128)S(1)} %get-tuple-element.66.rows_ref, f32[4096,128]{1,0:T(8,128)S(1)} %get-tuple-element.67.dist_ref), custom_call_target="tpu_custom_call" | custom-call | flops 5242880 | bytes 2097152 | tf_op jit(solution)/shard_map/slope/pallas_call | solution.py:166
  16.4 0.1 collective-permute-done.3.mb_ref
  16.4 0.8 %partner_maps.1 = (f32[8,256,128]{2,1,0:T(8,128)S(1)}, f32[8,256,128]{2,1,0:T(8,128)S(1)}, f32[2,256,128]{2,1,0:T(8,128)S(1)}, f32[8,128]{1,0:T(8,128)S(1)}, f32...) custom-call(f32[104,128]{1,0:T(8,128)S(1)} %add_add_fusion.1.ma_ref, ...), custom_call_target="tpu_custom_call" | custom-call | flops 10485760 | bytes 3145728 | tf_op jit(solution)/shard_map/partner_maps/pallas_call | solution.py:261
  17.2 0.1 collective-permute-start.4
  17.3 0.7 %own_maps.1 = (f32[8,256,128]{2,1,0:T(8,128)S(1)}, f32[8,256,128]{2,1,0:T(8,128)S(1)}) custom-call(f32[8,128]{1,0:T(8,128)S(1)} %get-tuple-element.75.sign_ref, f32[2,8,128]{2,1,0:T(8,128)S(1)} %get-tuple-element.77.state, f32[256,128]{1,0:T(8,128)S(1)} %get-tuple-element.78.bulk_terms, f32[256,128]{1,0:T(8,128)S(1)} %get-tuple-element.79.flux_terms, ...), custom_call_target="tpu_custom_call" | custom-call | flops 10485760 | bytes 3145728 | tf_op jit(solution)/shard_map/own_maps/pallas_call | solution.py:288
  18.0 0.8 %collective-permute-done.4.got_ref = f32[2,256,128]{2,1,0:T(8,128)S(1)} collective-permute-done((f32[2,256,128]{2,1,0:T(8,128)S(1)}, f32[2,256,128]{2,1,0:T(8,128)S(1)}, u32[]{:S(2)}, u32[]{:S(2)}) %collective-permute-start.4) | collective-permute-done | bytes 262176 | tf_op jit(solution)/shard_map/ppermute | solution.py:389
  18.8 0.0 copy-done
  18.8 0.1 compose.1
  19.0 1.6 %collective-permute-start.5 = (f32[256,128]{1,0:T(8,128)S(1)}, f32[256,128]{1,0:T(8,128)S(1)}, u32[]{:S(2)}, u32[]{:S(2)}) collective-permute-start(f32[256,128]{1,0:T(8,128)S(1)} %get-tuple-element.88), channel_id=1, source_target_pairs={{0,16},{8,24},{16,0},{24,8},{1,17},{9,25},{17,1},{25,9},{2,18},{10... | collective-permute-start | bytes 393224 | tf_op jit(solution)/shard_map/ppermute | solution.py:397
  20.5 4.0 %collective-permute-done.5.got_ref = f32[256,128]{1,0:T(8,128)S(1)} collective-permute-done((f32[256,128]{1,0:T(8,128)S(1)}, f32[256,128]{1,0:T(8,128)S(1)}, u32[]{:S(2)}, u32[]{:S(2)}) %collective-permute-start.5) | collective-permute-done | bytes 131104 | tf_op jit(solution)/shard_map/ppermute | solution.py:397
  24.6 0.1 collective-permute-start.6
  24.7 0.3 new_moments.2.refs_0_
  25.0 1.0 %collective-permute-done.6.entry_ref.refs_3_ = f32[256,128]{1,0:T(8,128)S(1)} collective-permute-done((f32[256,128]{1,0:T(8,128)S(1)}, f32[256,128]{1,0:T(8,128)S(1)}, u32[]{:S(2)}, u32[]{:S(2)}) %collective-permute-start.6) | collective-permute-done | bytes 131104 | tf_op jit(solution)/shard_map/ppermute | solution.py:389
  26.0 0.3 new_moments.3
  26.4 1.6 %collective-permute-start.9 = (f32[104,128]{1,0:T(8,128)S(1)}, f32[104,128]{1,0:T(8,128)S(1)}, u32[]{:S(2)}, u32[]{:S(2)}) collective-permute-start(f32[104,128]{1,0:T(8,128)S(1)} %new_moments.3), channel_id=1, source_target_pairs={{0,3},{1,2},{2,1},{3,0},{4,7},{5,6},{6,5},{7,4},{8,11},{9,10},{10,... | collective-permute-start | bytes 159752 | tf_op jit(solution)/shard_map/ppermute | solution.py:487
  27.9 0.4 collective-permute-start.8
  28.3 1.6 %collective-permute-start.7 = (f32[104,128]{1,0:T(8,128)S(1)}, f32[104,128]{1,0:T(8,128)S(1)}, u32[]{:S(2)}, u32[]{:S(2)}) collective-permute-start(f32[104,128]{1,0:T(8,128)S(1)} %new_moments.3), channel_id=1, source_target_pairs={{0,1},{1,0},{2,3},{3,2},{4,5},{5,4},{6,7},{7,6},{8,9},{9,8},{10,11... | collective-permute-start | bytes 159752 | tf_op jit(solution)/shard_map/ppermute | solution.py:487
  29.9 1.4 %write_dist.1 = f32[4096,128]{1,0:T(8,128)} custom-call(f32[256,128]{1,0:T(8,128)S(1)} %get-tuple-element.98.entry_ref.refs_0_, f32[8,256,128]{2,1,0:T(8,128)S(1)} %get-tuple-element.99.decay_ref.refs_1_, f32[8,256,128]{2,1,0:T(8,128)S(1)} %get-tuple-element.100.source_ref.refs_2_, f32[256,128]{1,0:T(8,128)S(1)} %collective-permute-done.6.entry_ref.refs_3_, ...), custom_call_target="tpu_custom_call" | custom-call | flops 1048576 | bytes 6291456 | tf_op jit(solution)/shard_map/write_dist/pallas_call | solution.py:458
  31.3 0.3 collective-permute-done.9
  31.6 0.5 %collective-permute-done.8 = f32[104,128]{1,0:T(8,128)S(1)} collective-permute-done((f32[104,128]{1,0:T(8,128)S(1)}, f32[104,128]{1,0:T(8,128)S(1)}, u32[]{:S(2)}, u32[]{:S(2)}) %collective-permute-start.8) | collective-permute-done | bytes 53280 | tf_op jit(solution)/shard_map/ppermute | solution.py:487
  32.1 0.4 collective-permute-done.7
  32.5 2.8 %collective-permute-start.10 = (f32[104,128]{1,0:T(8,128)S(1)}, f32[104,128]{1,0:T(8,128)S(1)}, u32[]{:S(2)}, u32[]{:S(2)}) collective-permute-start(f32[104,128]{1,0:T(8,128)S(1)} %add_add_fusion), channel_id=1, source_target_pairs={{0,4},{1,5},{2,6},{3,7},{4,0},{5,1},{6,2},{7,3},{8,12},{9,13},{10,... | collective-permute-start | bytes 159752 | tf_op jit(solution)/shard_map/ppermute | solution.py:487
  35.3 2.5 %collective-permute-done.10 = f32[104,128]{1,0:T(8,128)S(1)} collective-permute-done((f32[104,128]{1,0:T(8,128)S(1)}, f32[104,128]{1,0:T(8,128)S(1)}, u32[]{:S(2)}, u32[]{:S(2)}) %collective-permute-start.10) | collective-permute-done | bytes 53280 | tf_op jit(solution)/shard_map/ppermute | solution.py:487
  37.8 0.6 %add_bitcast_fusion = f32[13,8,128]{2,1,0:T(8,128)} fusion(f32[104,128]{1,0:T(8,128)S(1)} %add_add_fusion, f32[104,128]{1,0:T(8,128)S(1)} %collective-permute-done.10), kind=kLoop, calls=%fused_computation | loop fusion | flops 13312 | bytes 159744 | tf_op jit(solution)/shard_map/reshape | solution.py:544
  (3 shorter events, 0.1 us)
Async XLA Ops:
  2.7 7.0 %collective-permute-start.2 = (f32[104,128]{1,0:T(8,128)S(1)}, f32[104,128]{1,0:T(8,128)S(1)}, u32[]{:S(2)}, u32[]{:S(2)}) collective-permute-start(f32[104,128]{1,0:T(8,128)S(1)} %get-tuple-element.55), channel_id=1, source_target_pairs={{0,3},{1,2},{2,1},{3,0},{4,7},{5,6},{6,5},{7,4},{8,11},{9,10},{10,... | collective-permute-start | bytes 159752 | tf_op jit(solution)/shard_map/ppermute | solution.py:487
  6.7 4.1 %collective-permute-start.1 = (f32[104,128]{1,0:T(8,128)S(1)}, f32[104,128]{1,0:T(8,128)S(1)}, u32[]{:S(2)}, u32[]{:S(2)}) collective-permute-start(f32[104,128]{1,0:T(8,128)S(1)} %get-tuple-element.55), channel_id=1, source_target_pairs={{0,2},{1,3},{2,0},{3,1},{4,6},{5,7},{6,4},{7,5},{8,10},{9,11},{10,... | collective-permute-start | bytes 159752 | tf_op jit(solution)/shard_map/ppermute | solution.py:487
  7.2 4.1 %collective-permute-start = (f32[104,128]{1,0:T(8,128)S(1)}, f32[104,128]{1,0:T(8,128)S(1)}, u32[]{:S(2)}, u32[]{:S(2)}) collective-permute-start(f32[104,128]{1,0:T(8,128)S(1)} %get-tuple-element.55), channel_id=1, source_target_pairs={{0,1},{1,0},{2,3},{3,2},{4,5},{5,4},{6,7},{7,6},{8,9},{9,8},{10,11... | collective-permute-start | bytes 159752 | tf_op jit(solution)/shard_map/ppermute | solution.py:487
  11.3 7.5 %copy-start = (f32[512,128]{1,0:T(8,128)S(1)}, f32[512,128]{1,0:T(8,128)}, u32[]{:S(2)}) copy-start(f32[512,128]{1,0:T(8,128)} %inflow_ref.1) | copy-start | bytes 786436
  11.3 5.1 %collective-permute-start.3 = (f32[104,128]{1,0:T(8,128)S(1)}, f32[104,128]{1,0:T(8,128)S(1)}, u32[]{:S(2)}, u32[]{:S(2)}) collective-permute-start(f32[104,128]{1,0:T(8,128)S(1)} %add_add_fusion.1.ma_ref), channel_id=1, source_target_pairs={{0,4},{1,5},{2,6},{3,7},{4,0},{5,1},{6,2},{7,3},{8,12},{9,13},{10,... | collective-permute-start | bytes 159752 | tf_op jit(solution)/shard_map/ppermute | solution.py:487
  17.2 1.6 %collective-permute-start.4 = (f32[2,256,128]{2,1,0:T(8,128)S(1)}, f32[2,256,128]{2,1,0:T(8,128)S(1)}, u32[]{:S(2)}, u32[]{:S(2)}) collective-permute-start(f32[2,256,128]{2,1,0:T(8,128)S(1)} %get-tuple-element.76), channel_id=1, source_target_pairs={{0,8},{8,0},{16,24},{24,16},{1,9},{9,1},{17,25},{25,17},{2,10},{10... | collective-permute-start | bytes 786440 | tf_op jit(solution)/shard_map/ppermute | solution.py:389
  19.0 5.6 %collective-permute-start.5 = (f32[256,128]{1,0:T(8,128)S(1)}, f32[256,128]{1,0:T(8,128)S(1)}, u32[]{:S(2)}, u32[]{:S(2)}) collective-permute-start(f32[256,128]{1,0:T(8,128)S(1)} %get-tuple-element.88), channel_id=1, source_target_pairs={{0,16},{8,24},{16,0},{24,8},{1,17},{9,25},{17,1},{25,9},{2,18},{10... | collective-permute-start | bytes 393224 | tf_op jit(solution)/shard_map/ppermute | solution.py:397
  24.6 1.4 %collective-permute-start.6 = (f32[256,128]{1,0:T(8,128)S(1)}, f32[256,128]{1,0:T(8,128)S(1)}, u32[]{:S(2)}, u32[]{:S(2)}) collective-permute-start(f32[256,128]{1,0:T(8,128)S(1)} %get-tuple-element.91), channel_id=1, source_target_pairs={{0,8},{8,0},{16,24},{24,16},{1,9},{9,1},{17,25},{25,17},{2,10},{10... | collective-permute-start | bytes 393224 | tf_op jit(solution)/shard_map/ppermute | solution.py:389
  26.4 5.2 %collective-permute-start.9 = (f32[104,128]{1,0:T(8,128)S(1)}, f32[104,128]{1,0:T(8,128)S(1)}, u32[]{:S(2)}, u32[]{:S(2)}) collective-permute-start(f32[104,128]{1,0:T(8,128)S(1)} %new_moments.3), channel_id=1, source_target_pairs={{0,3},{1,2},{2,1},{3,0},{4,7},{5,6},{6,5},{7,4},{8,11},{9,10},{10,... | collective-permute-start | bytes 159752 | tf_op jit(solution)/shard_map/ppermute | solution.py:487
  27.9 4.1 %collective-permute-start.8 = (f32[104,128]{1,0:T(8,128)S(1)}, f32[104,128]{1,0:T(8,128)S(1)}, u32[]{:S(2)}, u32[]{:S(2)}) collective-permute-start(f32[104,128]{1,0:T(8,128)S(1)} %new_moments.3), channel_id=1, source_target_pairs={{0,2},{1,3},{2,0},{3,1},{4,6},{5,7},{6,4},{7,5},{8,10},{9,11},{10,... | collective-permute-start | bytes 159752 | tf_op jit(solution)/shard_map/ppermute | solution.py:487
  28.3 4.1 %collective-permute-start.7 = (f32[104,128]{1,0:T(8,128)S(1)}, f32[104,128]{1,0:T(8,128)S(1)}, u32[]{:S(2)}, u32[]{:S(2)}) collective-permute-start(f32[104,128]{1,0:T(8,128)S(1)} %new_moments.3), channel_id=1, source_target_pairs={{0,1},{1,0},{2,3},{3,2},{4,5},{5,4},{6,7},{7,6},{8,9},{9,8},{10,11... | collective-permute-start | bytes 159752 | tf_op jit(solution)/shard_map/ppermute | solution.py:487
  32.5 5.3 %collective-permute-start.10 = (f32[104,128]{1,0:T(8,128)S(1)}, f32[104,128]{1,0:T(8,128)S(1)}, u32[]{:S(2)}, u32[]{:S(2)}) collective-permute-start(f32[104,128]{1,0:T(8,128)S(1)} %add_add_fusion), channel_id=1, source_target_pairs={{0,4},{1,5},{2,6},{3,7},{4,0},{5,1},{6,2},{7,3},{8,12},{9,13},{10,... | collective-permute-start | bytes 159752 | tf_op jit(solution)/shard_map/ppermute | solution.py:487

commit v6 on v5

--- a/solution.py
+++ b/solution.py
@@ -78,8 +78,8 @@
     for c in range(chunks):
         parts[c].wait()
         tab = table[:, c * chunk : (c + 1) * chunk]
-        for i in range(0, nx, 2):
-            pair = range(min(2, nx - i))
+        for i in range(0, nx, 1):
+            pair = range(min(1, nx - i))
             planes = [dist_ref[pl.ds(c * chunk * nx + i + k, chunk, stride=nx), :] for k in pair]
             lanes = planes[0].shape[1]
             got = project(tab, jnp.concatenate(planes, axis=1))
@@ -221,7 +221,7 @@
         both = jnp.concatenate([ref[pl.ds(at_x, 32, stride=nx), :] for ref in (bulk_terms, flux_terms)], axis=1)
         places.append(at_x)
         cells.append(jnp.concatenate([both.astype(jnp.bfloat16), rest], axis=0))
-    group = 64
+    group = 32
     for at in range(0, count, group):
         rows = slice(at, at + group)
         speed = speed_ref[rows, :]
@@ -404,8 +404,8 @@
     entry = entry_ref[...]
     lanes = entry.shape[1]
     table = table_ref[half_index(own)]
-    for i in range(0, nx, 2):
-        pair = range(min(2, nx - i))
+    for i in range(0, nx, 1):
+        pair = range(min(1, nx - i))
         planes = [decay_ref[i + k] * entry + source_ref[i + k] for k in pair]
         got = project(table, jnp.concatenate(planes, axis=1))
         for k in pair:

time: 38.5 us -> 38.5 us (level)
  no operation moved by 1% of the time
where the time goes in v6:
time: 38.5 us; the launch traced here: 38.3 us
  starting transfers between devices  15.4 us (40%)
  waiting for transfers between devices  11.1 us (29%)
  Pallas kernels  10.4 us (27%)
  between operations  0.72 us (2%)
  other arithmetic  0.67 us (2%)
    ppermute x8, starting transfers between devices, exchange(): return lax.ppermute(a, axis, [(i, i ^ mask) for i in range(n)])  13.7 us
    ppermute x8, waiting for transfers between devices, exchange(): return lax.ppermute(a, axis, [(i, i ^ mask) for i in range(n)])  5.24 us
    pallas_call x2, Pallas kernels, slopes(): pl.pallas_call(functools.partial(slope_kernel, nx, own), in_specs=[whole]...  4.71 us
    ppermute x1, waiting for transfers between devices, chip_hop(): got = lax.ppermute(face, 'gx', pairs)  4.02 us
    pallas_call x1, Pallas kernels, old_moments(): pl.pallas_call(functools.partial(moments_kernel, total, nx, chunks), in_s...  2.01 us
    ppermute x2, waiting for transfers between devices, chip_exchange(): return lax.ppermute(a, 'gx', [(i, i ^ 1) for i in range(n)])  1.84 us
    ppermute x1, starting transfers between devices, chip_hop(): got = lax.ppermute(face, 'gx', pairs)  1.58 us
    pallas_call x1, Pallas kernels, write_dist(): pl.pallas_call(functools.partial(write_kernel, nx, pieces), in_specs=[who...  1.44 us
  transfers between devices with their start and end apart: 11, of which 10 were waited for; matrix products, arithmetic and copies ran while one was open for 0% of the time, Pallas kernels for 19%

profile of v6, /device:TPU:0, one launch (start us, length us, event | category | flops | bytes accessed | tf_op | source)
XLA Modules:
  0.0 38.3 jit_solution(12780831896897370358)
XLA Ops:
  0.6 2.0 %moments.1 = (f32[104,128]{1,0:T(8,128)S(1)}, bf16[2,32,256]{2,1,0:T(8,128)(2,1)S(1)}, f32[2,8,256]{2,1,0:T(8,128)S(1)}, f32[4096,128]{1,0:T(8,128)S(1)}) custom-call(s32[1,512]{1,0:T(1,128)} %bitcast.9, f32[1,512]{1,0:T(1,128)} %bitcast.10, f32[2,512]{1,0:T(2,128)} %cross_hbm.1, f32[1,512]{1,0:T(1,128)} %bitcast.11, f32[4096,128]{1,0:T(8,128)} %bitcast.8), custom_call_target="tpu_custom_call" | custom-call | flops 50331648 | bytes 2097152 | tf_op jit(solution)/shard_map/moments/pallas_call | solution.py:99
  2.6 4.0 %collective-permute-start.2 = (f32[104,128]{1,0:T(8,128)S(1)}, f32[104,128]{1,0:T(8,128)S(1)}, u32[]{:S(2)}, u32[]{:S(2)}) collective-permute-start(f32[104,128]{1,0:T(8,128)S(1)} %get-tuple-element.55), channel_id=1, source_target_pairs={{0,3},{1,2},{2,1},{3,0},{4,7},{5,6},{6,5},{7,4},{8,11},{9,10},{10,... | collective-permute-start | bytes 159752 | tf_op jit(solution)/shard_map/ppermute | solution.py:487
  6.7 0.4 %collective-permute-start.1 = (f32[104,128]{1,0:T(8,128)S(1)}, f32[104,128]{1,0:T(8,128)S(1)}, u32[]{:S(2)}, u32[]{:S(2)}) collective-permute-start(f32[104,128]{1,0:T(8,128)S(1)} %get-tuple-element.55), channel_id=1, source_target_pairs={{0,2},{1,3},{2,0},{3,1},{4,6},{5,7},{6,4},{7,5},{8,10},{9,11},{10,... | collective-permute-start | bytes 159752 | tf_op jit(solution)/shard_map/ppermute | solution.py:487
  7.1 0.2 collective-permute-start
  7.3 2.4 %slope.2 = (f32[8,256,128]{2,1,0:T(8,128)S(1)}, f32[256,128]{1,0:T(8,128)S(1)}, bf16[256,128]{1,0:T(8,128)(2,1)S(1)}) custom-call(f32[2,8,256]{2,1,0:T(8,128)S(1)} %get-tuple-element.66.rows_ref, f32[4096,128]{1,0:T(8,128)S(1)} %get-tuple-element.67.dist_ref), custom_call_target="tpu_custom_call" | custom-call | flops 5242880 | bytes 2097152 | tf_op jit(solution)/shard_map/slope/pallas_call | solution.py:166
  9.7 0.0 collective-permute-done.2
  9.7 1.1 %collective-permute-done.1 = f32[104,128]{1,0:T(8,128)S(1)} collective-permute-done((f32[104,128]{1,0:T(8,128)S(1)}, f32[104,128]{1,0:T(8,128)S(1)}, u32[]{:S(2)}, u32[]{:S(2)}) %collective-permute-start.1) | collective-permute-done | bytes 53280 | tf_op jit(solution)/shard_map/ppermute | solution.py:487
  10.8 0.4 %collective-permute-done = f32[104,128]{1,0:T(8,128)S(1)} collective-permute-done((f32[104,128]{1,0:T(8,128)S(1)}, f32[104,128]{1,0:T(8,128)S(1)}, u32[]{:S(2)}, u32[]{:S(2)}) %collective-permute-start) | collective-permute-done | bytes 53280 | tf_op jit(solution)/shard_map/ppermute | solution.py:487
  11.3 0.0 copy-start
  11.3 2.7 %collective-permute-start.3 = (f32[104,128]{1,0:T(8,128)S(1)}, f32[104,128]{1,0:T(8,128)S(1)}, u32[]{:S(2)}, u32[]{:S(2)}) collective-permute-start(f32[104,128]{1,0:T(8,128)S(1)} %add_add_fusion.1.ma_ref), channel_id=1, source_target_pairs={{0,4},{1,5},{2,6},{3,7},{4,0},{5,1},{6,2},{7,3},{8,12},{9,13},{10,... | collective-permute-start | bytes 159752 | tf_op jit(solution)/shard_map/ppermute | solution.py:487
  13.9 2.4 %slope.3 = (f32[8,256,128]{2,1,0:T(8,128)S(1)}, f32[256,128]{1,0:T(8,128)S(1)}, bf16[256,128]{1,0:T(8,128)(2,1)S(1)}) custom-call(f32[2,8,256]{2,1,0:T(8,128)S(1)} %get-tuple-element.66.rows_ref, f32[4096,128]{1,0:T(8,128)S(1)} %get-tuple-element.67.dist_ref), custom_call_target="tpu_custom_call" | custom-call | flops 5242880 | bytes 2097152 | tf_op jit(solution)/shard_map/slope/pallas_call | solution.py:166
  16.3 0.1 collective-permute-done.3.mb_ref
  16.4 0.8 %partner_maps.1 = (f32[8,256,128]{2,1,0:T(8,128)S(1)}, f32[8,256,128]{2,1,0:T(8,128)S(1)}, f32[2,256,128]{2,1,0:T(8,128)S(1)}, f32[8,128]{1,0:T(8,128)S(1)}, f32...) custom-call(f32[104,128]{1,0:T(8,128)S(1)} %add_add_fusion.1.ma_ref, ...), custom_call_target="tpu_custom_call" | custom-call | flops 10485760 | bytes 3145728 | tf_op jit(solution)/shard_map/partner_maps/pallas_call | solution.py:261
  17.1 0.1 collective-permute-start.4
  17.2 0.7 %own_maps.1 = (f32[8,256,128]{2,1,0:T(8,128)S(1)}, f32[8,256,128]{2,1,0:T(8,128)S(1)}) custom-call(f32[8,128]{1,0:T(8,128)S(1)} %get-tuple-element.75.sign_ref, f32[2,8,128]{2,1,0:T(8,128)S(1)} %get-tuple-element.77.state, f32[256,128]{1,0:T(8,128)S(1)} %get-tuple-element.78.bulk_terms, f32[256,128]{1,0:T(8,128)S(1)} %get-tuple-element.79.flux_terms, ...), custom_call_target="tpu_custom_call" | custom-call | flops 10485760 | bytes 3145728 | tf_op jit(solution)/shard_map/own_maps/pallas_call | solution.py:288
  17.9 0.8 %collective-permute-done.4.got_ref = f32[2,256,128]{2,1,0:T(8,128)S(1)} collective-permute-done((f32[2,256,128]{2,1,0:T(8,128)S(1)}, f32[2,256,128]{2,1,0:T(8,128)S(1)}, u32[]{:S(2)}, u32[]{:S(2)}) %collective-permute-start.4) | collective-permute-done | bytes 262176 | tf_op jit(solution)/shard_map/ppermute | solution.py:389
  18.7 0.0 copy-done
  18.7 0.1 compose.1
  18.9 1.6 %collective-permute-start.5 = (f32[256,128]{1,0:T(8,128)S(1)}, f32[256,128]{1,0:T(8,128)S(1)}, u32[]{:S(2)}, u32[]{:S(2)}) collective-permute-start(f32[256,128]{1,0:T(8,128)S(1)} %get-tuple-element.88), channel_id=1, source_target_pairs={{0,16},{8,24},{16,0},{24,8},{1,17},{9,25},{17,1},{25,9},{2,18},{10... | collective-permute-start | bytes 393224 | tf_op jit(solution)/shard_map/ppermute | solution.py:397
  20.5 4.0 %collective-permute-done.5.got_ref = f32[256,128]{1,0:T(8,128)S(1)} collective-permute-done((f32[256,128]{1,0:T(8,128)S(1)}, f32[256,128]{1,0:T(8,128)S(1)}, u32[]{:S(2)}, u32[]{:S(2)}) %collective-permute-start.5) | collective-permute-done | bytes 131104 | tf_op jit(solution)/shard_map/ppermute | solution.py:397
  24.5 0.1 collective-permute-start.6
  24.6 0.3 new_moments.2.refs_0_
  24.9 1.0 %collective-permute-done.6.entry_ref.refs_3_ = f32[256,128]{1,0:T(8,128)S(1)} collective-permute-done((f32[256,128]{1,0:T(8,128)S(1)}, f32[256,128]{1,0:T(8,128)S(1)}, u32[]{:S(2)}, u32[]{:S(2)}) %collective-permute-start.6) | collective-permute-done | bytes 131104 | tf_op jit(solution)/shard_map/ppermute | solution.py:389
  26.0 0.3 new_moments.3
  26.3 1.6 %collective-permute-start.9 = (f32[104,128]{1,0:T(8,128)S(1)}, f32[104,128]{1,0:T(8,128)S(1)}, u32[]{:S(2)}, u32[]{:S(2)}) collective-permute-start(f32[104,128]{1,0:T(8,128)S(1)} %new_moments.3), channel_id=1, source_target_pairs={{0,3},{1,2},{2,1},{3,0},{4,7},{5,6},{6,5},{7,4},{8,11},{9,10},{10,... | collective-permute-start | bytes 159752 | tf_op jit(solution)/shard_map/ppermute | solution.py:487
  27.9 0.4 collective-permute-start.8
  28.2 1.6 %collective-permute-start.7 = (f32[104,128]{1,0:T(8,128)S(1)}, f32[104,128]{1,0:T(8,128)S(1)}, u32[]{:S(2)}, u32[]{:S(2)}) collective-permute-start(f32[104,128]{1,0:T(8,128)S(1)} %new_moments.3), channel_id=1, source_target_pairs={{0,1},{1,0},{2,3},{3,2},{4,5},{5,4},{6,7},{7,6},{8,9},{9,8},{10,11... | collective-permute-start | bytes 159752 | tf_op jit(solution)/shard_map/ppermute | solution.py:487
  29.8 1.4 %write_dist.1 = f32[4096,128]{1,0:T(8,128)} custom-call(f32[256,128]{1,0:T(8,128)S(1)} %get-tuple-element.98.entry_ref.refs_0_, f32[8,256,128]{2,1,0:T(8,128)S(1)} %get-tuple-element.99.decay_ref.refs_1_, f32[8,256,128]{2,1,0:T(8,128)S(1)} %get-tuple-element.100.source_ref.refs_2_, f32[256,128]{1,0:T(8,128)S(1)} %collective-permute-done.6.entry_ref.refs_3_, ...), custom_call_target="tpu_custom_call" | custom-call | flops 1048576 | bytes 6291456 | tf_op jit(solution)/shard_map/write_dist/pallas_call | solution.py:458
  31.3 0.3 collective-permute-done.9
  31.5 0.5 %collective-permute-done.8 = f32[104,128]{1,0:T(8,128)S(1)} collective-permute-done((f32[104,128]{1,0:T(8,128)S(1)}, f32[104,128]{1,0:T(8,128)S(1)}, u32[]{:S(2)}, u32[]{:S(2)}) %collective-permute-start.8) | collective-permute-done | bytes 53280 | tf_op jit(solution)/shard_map/ppermute | solution.py:487
  32.0 0.4 collective-permute-done.7
  32.4 2.8 %collective-permute-start.10 = (f32[104,128]{1,0:T(8,128)S(1)}, f32[104,128]{1,0:T(8,128)S(1)}, u32[]{:S(2)}, u32[]{:S(2)}) collective-permute-start(f32[104,128]{1,0:T(8,128)S(1)} %add_add_fusion), channel_id=1, source_target_pairs={{0,4},{1,5},{2,6},{3,7},{4,0},{5,1},{6,2},{7,3},{8,12},{9,13},{10,... | collective-permute-start | bytes 159752 | tf_op jit(solution)/shard_map/ppermute | solution.py:487
  35.2 2.5 %collective-permute-done.10 = f32[104,128]{1,0:T(8,128)S(1)} collective-permute-done((f32[104,128]{1,0:T(8,128)S(1)}, f32[104,128]{1,0:T(8,128)S(1)}, u32[]{:S(2)}, u32[]{:S(2)}) %collective-permute-start.10) | collective-permute-done | bytes 53280 | tf_op jit(solution)/shard_map/ppermute | solution.py:487
  37.7 0.6 %add_bitcast_fusion = f32[13,8,128]{2,1,0:T(8,128)} fusion(f32[104,128]{1,0:T(8,128)S(1)} %add_add_fusion, f32[104,128]{1,0:T(8,128)S(1)} %collective-permute-done.10), kind=kLoop, calls=%fused_computation | loop fusion | flops 13312 | bytes 159744 | tf_op jit(solution)/shard_map/reshape | solution.py:544
  (3 shorter events, 0.1 us)
Async XLA Ops:
  2.6 7.0 %collective-permute-start.2 = (f32[104,128]{1,0:T(8,128)S(1)}, f32[104,128]{1,0:T(8,128)S(1)}, u32[]{:S(2)}, u32[]{:S(2)}) collective-permute-start(f32[104,128]{1,0:T(8,128)S(1)} %get-tuple-element.55), channel_id=1, source_target_pairs={{0,3},{1,2},{2,1},{3,0},{4,7},{5,6},{6,5},{7,4},{8,11},{9,10},{10,... | collective-permute-start | bytes 159752 | tf_op jit(solution)/shard_map/ppermute | solution.py:487
  6.7 4.1 %collective-permute-start.1 = (f32[104,128]{1,0:T(8,128)S(1)}, f32[104,128]{1,0:T(8,128)S(1)}, u32[]{:S(2)}, u32[]{:S(2)}) collective-permute-start(f32[104,128]{1,0:T(8,128)S(1)} %get-tuple-element.55), channel_id=1, source_target_pairs={{0,2},{1,3},{2,0},{3,1},{4,6},{5,7},{6,4},{7,5},{8,10},{9,11},{10,... | collective-permute-start | bytes 159752 | tf_op jit(solution)/shard_map/ppermute | solution.py:487
  7.1 4.1 %collective-permute-start = (f32[104,128]{1,0:T(8,128)S(1)}, f32[104,128]{1,0:T(8,128)S(1)}, u32[]{:S(2)}, u32[]{:S(2)}) collective-permute-start(f32[104,128]{1,0:T(8,128)S(1)} %get-tuple-element.55), channel_id=1, source_target_pairs={{0,1},{1,0},{2,3},{3,2},{4,5},{5,4},{6,7},{7,6},{8,9},{9,8},{10,11... | collective-permute-start | bytes 159752 | tf_op jit(solution)/shard_map/ppermute | solution.py:487
  11.3 7.5 %copy-start = (f32[512,128]{1,0:T(8,128)S(1)}, f32[512,128]{1,0:T(8,128)}, u32[]{:S(2)}) copy-start(f32[512,128]{1,0:T(8,128)} %inflow_ref.1) | copy-start | bytes 786436
  11.3 5.1 %collective-permute-start.3 = (f32[104,128]{1,0:T(8,128)S(1)}, f32[104,128]{1,0:T(8,128)S(1)}, u32[]{:S(2)}, u32[]{:S(2)}) collective-permute-start(f32[104,128]{1,0:T(8,128)S(1)} %add_add_fusion.1.ma_ref), channel_id=1, source_target_pairs={{0,4},{1,5},{2,6},{3,7},{4,0},{5,1},{6,2},{7,3},{8,12},{9,13},{10,... | collective-permute-start | bytes 159752 | tf_op jit(solution)/shard_map/ppermute | solution.py:487
  17.1 1.6 %collective-permute-start.4 = (f32[2,256,128]{2,1,0:T(8,128)S(1)}, f32[2,256,128]{2,1,0:T(8,128)S(1)}, u32[]{:S(2)}, u32[]{:S(2)}) collective-permute-start(f32[2,256,128]{2,1,0:T(8,128)S(1)} %get-tuple-element.76), channel_id=1, source_target_pairs={{0,8},{8,0},{16,24},{24,16},{1,9},{9,1},{17,25},{25,17},{2,10},{10... | collective-permute-start | bytes 786440 | tf_op jit(solution)/shard_map/ppermute | solution.py:389
  18.9 5.6 %collective-permute-start.5 = (f32[256,128]{1,0:T(8,128)S(1)}, f32[256,128]{1,0:T(8,128)S(1)}, u32[]{:S(2)}, u32[]{:S(2)}) collective-permute-start(f32[256,128]{1,0:T(8,128)S(1)} %get-tuple-element.88), channel_id=1, source_target_pairs={{0,16},{8,24},{16,0},{24,8},{1,17},{9,25},{17,1},{25,9},{2,18},{10... | collective-permute-start | bytes 393224 | tf_op jit(solution)/shard_map/ppermute | solution.py:397
  24.5 1.4 %collective-permute-start.6 = (f32[256,128]{1,0:T(8,128)S(1)}, f32[256,128]{1,0:T(8,128)S(1)}, u32[]{:S(2)}, u32[]{:S(2)}) collective-permute-start(f32[256,128]{1,0:T(8,128)S(1)} %get-tuple-element.91), channel_id=1, source_target_pairs={{0,8},{8,0},{16,24},{24,16},{1,9},{9,1},{17,25},{25,17},{2,10},{10... | collective-permute-start | bytes 393224 | tf_op jit(solution)/shard_map/ppermute | solution.py:389
  26.3 5.3 %collective-permute-start.9 = (f32[104,128]{1,0:T(8,128)S(1)}, f32[104,128]{1,0:T(8,128)S(1)}, u32[]{:S(2)}, u32[]{:S(2)}) collective-permute-start(f32[104,128]{1,0:T(8,128)S(1)} %new_moments.3), channel_id=1, source_target_pairs={{0,3},{1,2},{2,1},{3,0},{4,7},{5,6},{6,5},{7,4},{8,11},{9,10},{10,... | collective-permute-start | bytes 159752 | tf_op jit(solution)/shard_map/ppermute | solution.py:487
  27.9 4.1 %collective-permute-start.8 = (f32[104,128]{1,0:T(8,128)S(1)}, f32[104,128]{1,0:T(8,128)S(1)}, u32[]{:S(2)}, u32[]{:S(2)}) collective-permute-start(f32[104,128]{1,0:T(8,128)S(1)} %new_moments.3), channel_id=1, source_target_pairs={{0,2},{1,3},{2,0},{3,1},{4,6},{5,7},{6,4},{7,5},{8,10},{9,11},{10,... | collective-permute-start | bytes 159752 | tf_op jit(solution)/shard_map/ppermute | solution.py:487
  28.2 4.1 %collective-permute-start.7 = (f32[104,128]{1,0:T(8,128)S(1)}, f32[104,128]{1,0:T(8,128)S(1)}, u32[]{:S(2)}, u32[]{:S(2)}) collective-permute-start(f32[104,128]{1,0:T(8,128)S(1)} %new_moments.3), channel_id=1, source_target_pairs={{0,1},{1,0},{2,3},{3,2},{4,5},{5,4},{6,7},{7,6},{8,9},{9,8},{10,11... | collective-permute-start | bytes 159752 | tf_op jit(solution)/shard_map/ppermute | solution.py:487
  32.4 5.3 %collective-permute-start.10 = (f32[104,128]{1,0:T(8,128)S(1)}, f32[104,128]{1,0:T(8,128)S(1)}, u32[]{:S(2)}, u32[]{:S(2)}) collective-permute-start(f32[104,128]{1,0:T(8,128)S(1)} %add_add_fusion), channel_id=1, source_target_pairs={{0,4},{1,5},{2,6},{3,7},{4,0},{5,1},{6,2},{7,3},{8,12},{9,13},{10,... | collective-permute-start | bytes 159752 | tf_op jit(solution)/shard_map/ppermute | solution.py:487

commit v7 on v6

--- a/solution.py
+++ b/solution.py
@@ -45,16 +45,16 @@
     return first[:ROWS] + first[ROWS:] + second
 
 
-def moments_kernel(total, nx, chunks, side_hbm, speed_hbm, cross_hbm, weight_hbm, dist_hbm,
-                   mom_ref, table_ref, rows_ref, dist_ref, side_ref, speed_ref, cross_ref, weight_ref, sems):
-    count = speed_ref.shape[1]
-    chunk = count // chunks
+def moments_kernel(total, nx, side_hbm, speed_hbm, cross_hbm, weight_hbm, dist_hbm,
+                   mom_ref, table_ref, rows_ref, own_ref, other_ref, side_ref, speed_ref, cross_ref, weight_ref, sems):
+    half = speed_ref.shape[1] // 2
+    size = half * nx
     small = [(side_hbm, side_ref), (speed_hbm, speed_ref), (cross_hbm, cross_ref), (weight_hbm, weight_ref)]
-    copies = [pltpu.make_async_copy(a, b, sems.at[chunks + i]) for i, (a, b) in enumerate(small)]
+    copies = [pltpu.make_async_copy(a, b, sems.at[2 + i]) for i, (a, b) in enumerate(small)]
     parts = []
-    for i in range(chunks):
-        rows = pl.ds(i * chunk * nx, chunk * nx)
-        parts.append(pltpu.make_async_copy(dist_hbm.at[rows, :], dist_ref.at[rows, :], sems.at[i]))
+    for i, ref in enumerate((own_ref, other_ref)):
+        rows = pl.ds(pl.multiple_of(half_index(i == 0) * size, size), size)
+        parts.append(pltpu.make_async_copy(dist_hbm.at[rows, :], ref, sems.at[i]))
     for c in copies + parts:
         c.start()
     for c in copies:
@@ -67,51 +67,43 @@
     square = xx + yy + zz
     stacked = jnp.concatenate([x, y, z] + [jnp.zeros_like(x)] * 5, axis=0)
     for h in range(2):
-        rows_ref[h] = stacked[:, h * (count // 2) : (h + 1) * (count // 2)]
+        rows_ref[h] = stacked[:, h * half : (h + 1) * half]
     rows = [jnp.ones_like(x), x, y, z, xx, yy, zz, x * y, x * z, y * z, x * square, y * square, z * square]
     rows += [jnp.zeros_like(x)] * (ROWS - NMOM)
     full = jnp.concatenate(rows, axis=0) * (weight_ref[...] * (1.0 / total))
     high, low = split(full)
     table = jnp.concatenate([high, low], axis=0)
     for h in range(2):
-        table_ref[h] = table[:, h * (count // 2) : (h + 1) * (count // 2)]
-    for c in range(chunks):
+        table_ref[h] = table[:, h * half : (h + 1) * half]
+    for c, ref in enumerate((own_ref, other_ref)):
         parts[c].wait()
-        tab = table[:, c * chunk : (c + 1) * chunk]
-        for i in range(0, nx, 1):
-            pair = range(min(1, nx - i))
-            planes = [dist_ref[pl.ds(c * chunk * nx + i + k, chunk, stride=nx), :] for k in pair]
-            lanes = planes[0].shape[1]
-            got = project(tab, jnp.concatenate(planes, axis=1))
-            for k in pair:
-                part = got[:NMOM, k * lanes : (k + 1) * lanes]
-                place = pl.ds(i + k, NMOM, stride=nx)
-                if c == 0:
-                    mom_ref[place, :] = part
-                else:
-                    mom_ref[place, :] += part
+        tab = table_ref[half_index(c == 0)]
+        for i in range(nx):
+            part = project(tab, ref[pl.ds(i, half, stride=nx), :])[:NMOM]
+            place = pl.ds(i, NMOM, stride=nx)
+            mom_ref[place, :] = part if c == 0 else mom_ref[place, :] + part
 
 
 def old_moments(total, nx, side, speed, cross, weight, dist):
     count, lanes = speed.shape[1], dist.shape[1]
-    chunks = max(1, count // 256)
-    whole = pl.BlockSpec(memory_space=pltpu.VMEM)
-    return pl.pallas_call(
-        functools.partial(moments_kernel, total, nx, chunks),
+    whole = pl.BlockSpec(memory_space=pltpu.VMEM)
+    return pl.pallas_call(
+        functools.partial(moments_kernel, total, nx),
         in_specs=[pl.BlockSpec(memory_space=pltpu.HBM)] * 5,
-        out_specs=[whole] * 4,
+        out_specs=[whole] * 5,
         out_shape=[
             pltpu.VMEM((NMOM * nx, lanes), jnp.float32),
             pltpu.VMEM((2, 2 * ROWS, count // 2), jnp.bfloat16),
             pltpu.VMEM((2, 8, count // 2), jnp.float32),
-            pltpu.VMEM(dist.shape, jnp.float32),
+            pltpu.VMEM((count * nx // 2, lanes), jnp.float32),
+            pltpu.VMEM((count * nx // 2, lanes), jnp.float32),
         ],
         scratch_shapes=[
             pltpu.VMEM(side.shape, jnp.int32),
             pltpu.VMEM(speed.shape, jnp.float32),
             pltpu.VMEM(cross.shape, jnp.float32),
             pltpu.VMEM(weight.shape, jnp.float32),
-            pltpu.SemaphoreType.DMA((chunks + 4,)),
+            pltpu.SemaphoreType.DMA((6,)),
         ],
         compiler_params=params(),
         cost_estimate=cost(2 * 48 * count * nx * lanes, 4 * count * nx * lanes),
@@ -127,9 +119,7 @@
 def slope_kernel(nx, own, rows_ref, dist_ref, slope_ref, speed_ref, feature_ref, comp_ref):
     count = slope_ref.shape[1]
     lanes = dist_ref.shape[1]
-    half = half_index(own)
-    start = pl.multiple_of(half * count, count)
-    rows = rows_ref[half]
+    rows = rows_ref[half_index(own)]
     columns = jnp.transpose(rows)
     speed_ref[...] = jnp.broadcast_to(jnp.abs(columns[:, 0:1]), (count, lanes))
     for k in range(2):
@@ -151,7 +141,7 @@
         ay, az = KAPPA_CELL * jnp.abs(y), KAPPA_CELL * jnp.abs(z)
         both = ay + az
         for i in range(nx):
-            d = dist_ref[pl.ds((start + at) * nx + i, group, stride=nx), :]
+            d = dist_ref[pl.ds(at * nx + i, group, stride=nx), :]
             near_y = jnp.take_along_axis(d, from_y, axis=1)
             near_z = jnp.take_along_axis(d, from_z, axis=1)
             slope_ref[i, pl.ds(at, group), :] = both * d - ay * near_y - az * near_z
@@ -179,9 +169,9 @@
     )(rows, dist)
 
 
-def state_of(nx, ma_ref, mb_ref, state, bulk_terms, flux_terms):
-    lanes = ma_ref.shape[1]
-    m = [ma_ref[k * nx : (k + 1) * nx, :] + mb_ref[k * nx : (k + 1) * nx, :] for k in range(NMOM)]
+def state_of(nx, sum_ref, state, bulk_terms, flux_terms):
+    lanes = sum_ref.shape[1]
+    m = [sum_ref[k * nx : (k + 1) * nx, :] for k in range(NMOM)]
     n = m[0]
     inv_n = 1.0 / n
     u = [m[1] * inv_n, m[2] * inv_n, m[3] * inv_n]
@@ -210,9 +200,8 @@
     state[1] = nu
 
 
-def sweep(nx, sign_ref, state, bulk_terms, flux_terms, slope_ref, speed_ref, feature_ref, decay_ref, source_ref, send_ref):
+def sweep(nx, forward, state, bulk_terms, flux_terms, slope_ref, speed_ref, feature_ref, fields, last_ref):
     count, lanes = speed_ref.shape
-    forward = sign_ref[0:1, 0:1][0, 0] > 0
     rest = jnp.zeros((DEPTH - 32, 2 * lanes), jnp.bfloat16)
     group = 32
     places, cells = [], []
@@ -239,61 +228,44 @@
                 source = decay * run_source + source
                 decay = decay * run_decay
             run_decay, run_source = decay, source
-            decay_ref[at_x, rows, :] = decay
-            source_ref[at_x, rows, :] = source
-        if send_ref is not None:
-            send_ref[0, rows, :] = run_decay
-            send_ref[1, rows, :] = run_source
-
-
-def partner_kernel(nx, ma_ref, mb_ref, rows_ref, slope_ref, speed_ref, feature_ref,
-                   decay_ref, source_ref, send_ref, sign_ref, state, bulk_terms, flux_terms):
-    state_of(nx, ma_ref, mb_ref, state, bulk_terms, flux_terms)
-    sign_ref[...] = jnp.broadcast_to(rows_ref[0, 0:1, 0:1], sign_ref.shape)
-    sweep(nx, sign_ref, state, bulk_terms, flux_terms, slope_ref, speed_ref, feature_ref, decay_ref, source_ref, send_ref)
-
-
-def partner_maps(nx, ma, mb, rows, part):
+            if fields:
+                fields[0][at_x, rows, :] = decay
+                fields[1][at_x, rows, :] = source
+        if last_ref is not None:
+            last_ref[0, rows, :] = run_decay
+            last_ref[1, rows, :] = run_source
+
+
+def map_kernel(nx, kind, sum_ref, rows_ref, slope_ref, speed_ref, feature_ref, *refs):
+    outs, (state, bulk_terms, flux_terms) = refs[:-3], refs[-3:]
+    state_of(nx, sum_ref, state, bulk_terms, flux_terms)
+    forward = rows_ref[0, 0:1, 0:1][0, 0] > 0
+    if kind == "own":
+        outs[2][...] = jnp.broadcast_to(rows_ref[0, 0:1, 0:1], outs[2].shape)
+    fields, last_ref = outs[:2], None
+    sweep(nx, forward, state, bulk_terms, flux_terms, slope_ref, speed_ref, feature_ref, fields, last_ref)
+
+
+def map_scratch(nx, lanes):
+    return [pltpu.VMEM((rows, lanes), jnp.float32) if rows else pltpu.VMEM((2, nx, lanes), jnp.float32)
+            for rows in (0, 32 * nx, 32 * nx)]
+
+
+def maps(nx, kind, total, rows, part):
     count, lanes = part[1].shape
     whole = pl.BlockSpec(memory_space=pltpu.VMEM)
     field = pltpu.VMEM((nx, count, lanes), jnp.float32)
-    terms = pltpu.VMEM((32 * nx, lanes), jnp.float32)
-    return pl.pallas_call(
-        functools.partial(partner_kernel, nx),
-        in_specs=[whole] * 6,
-        out_specs=[whole] * 7,
-        out_shape=[
-            field,
-            field,
-            pltpu.VMEM((2, count, lanes), jnp.float32),
-            pltpu.VMEM((8, lanes), jnp.float32),
-            pltpu.VMEM((2, nx, lanes), jnp.float32),
-            terms,
-            terms,
-        ],
+    outs = [field, field] + ([pltpu.VMEM((8, lanes), jnp.float32)] if kind == "own" else [])
+    return pl.pallas_call(
+        functools.partial(map_kernel, nx, kind),
+        in_specs=[whole] * 5,
+        out_specs=[whole] * len(outs),
+        out_shape=outs,
+        scratch_shapes=map_scratch(nx, lanes),
         compiler_params=params(),
         cost_estimate=cost(40 * count * nx * lanes, 12 * count * nx * lanes),
-        name="partner_maps",
-    )(ma, mb, rows, *part)
-
-
-def own_kernel(nx, sign_ref, state, bulk_terms, flux_terms, slope_ref, speed_ref, feature_ref, decay_ref, source_ref):
-    sweep(nx, sign_ref, state, bulk_terms, flux_terms, slope_ref, speed_ref, feature_ref, decay_ref, source_ref, None)
-
-
-def own_maps(nx, sign, state, part):
-    count, lanes = part[1].shape
-    whole = pl.BlockSpec(memory_space=pltpu.VMEM)
-    field = pltpu.VMEM((nx, count, lanes), jnp.float32)
-    return pl.pallas_call(
-        functools.partial(own_kernel, nx),
-        in_specs=[whole] * 7,
-        out_specs=[whole] * 2,
-        out_shape=[field, field],
-        compiler_params=params(),
-        cost_estimate=cost(40 * count * nx * lanes, 12 * count * nx * lanes),
-        name="own_maps",
-    )(sign, *state, *part)
+        name=kind + "_maps",
+    )(total, rows, *part)
 
 
 def standing(sign_ref):
@@ -303,11 +275,16 @@
     return jnp.where(forward, core, 1 - core) == 0, jnp.where(forward, chip, chips - 1 - chip)
 
 
-def compose_kernel(nx, sign_ref, got_ref, decay_ref, source_ref, inflow_ref, near_ref, face_ref, entry_ref, *chip_ref):
+def compose_kernel(nx, sum_ref, rows_ref, slope_ref, speed_ref, feature_ref, sign_ref, decay_ref, source_ref, inflow_ref,
+                   near_ref, face_ref, entry_ref, *refs):
+    chip_ref, (got_ref, state, bulk_terms, flux_terms) = refs[:-4], refs[-4:]
+    state_of(nx, sum_ref, state, bulk_terms, flux_terms)
+    forward = rows_ref[0, 0:1, 0:1][0, 0] > 0
+    sweep(nx, forward, state, bulk_terms, flux_terms, slope_ref, speed_ref, feature_ref, (), got_ref)
     first, _ = standing(sign_ref)
     half = entry_ref.shape[0]
     mine = pl.ds(pl.multiple_of(half_index(True) * half, half), half)
-    last = jnp.where(sign_ref[0:1, 0:1][0, 0] > 0, nx - 1, 0)
+    last = jnp.where(forward, nx - 1, 0)
     decay, source = decay_ref[last], source_ref[last]
     got_decay, got_source = got_ref[0], got_ref[1]
     near_decay = jnp.where(first, decay, got_decay)
@@ -323,8 +300,8 @@
     face_ref[...] = chip_decay * entry + chip_source
 
 
-def compose_chip(nx, sign, got, decay, source, inflow):
-    _, half, lanes = got.shape
+def compose_chip(nx, total, rows, part, sign, decay, source, inflow):
+    half, lanes = part[1].shape
     whole = pl.BlockSpec(memory_space=pltpu.VMEM)
     pair = pltpu.VMEM((2, half, lanes), jnp.float32)
     outs = [pair] + [pltpu.VMEM((half, lanes), jnp.float32)] * 2
@@ -332,13 +309,14 @@
         outs.append(pair)
     return pl.pallas_call(
         functools.partial(compose_kernel, nx),
-        in_specs=[whole] * 5,
+        in_specs=[whole] * 9,
         out_specs=[whole] * len(outs),
         out_shape=outs,
-        compiler_params=params(),
-        cost_estimate=cost(10 * half * lanes, 40 * half * lanes),
+        scratch_shapes=[pair] + map_scratch(nx, lanes),
+        compiler_params=params(),
+        cost_estimate=cost(40 * half * nx * lanes, 12 * half * nx * lanes),
         name="compose",
-    )(sign, got, decay, source, inflow)
+    )(total, rows, *part, sign, decay, source, inflow)
 
 
 def pass_kernel(step, sign_ref, got_ref, entry_ref, chip_ref, next_ref, face_ref):
@@ -512,17 +490,22 @@
     count, nx, lanes = dist.shape
     flat = dist.reshape(count * nx, lanes)
     row = lambda a: a.reshape(1, count)
-    partial, table, rows, held = old_moments(total, nx, row(side), row(speed_x), transverse, row(quad_weight), flat)
-
-    def slope_half(own):
-        return lambda sent: slopes(nx, own, *lax.optimization_barrier((rows, held, sent))[:2])
-
-    (ma, mb), (part, own_part) = partial_sums(partial, "vert", [slope_half(False), slope_half(True)])
-    decay, source, send, sign, *state = partner_maps(nx, ma, mb, rows, part)
-    arrived = chip_exchange(send)
-    own_decay, own_source = own_maps(nx, sign, state, own_part)
+    partial, table, rows, own_dist, other_dist = old_moments(total, nx, row(side), row(speed_x), transverse, row(quad_weight), flat)
+    received = []
+
+    def own_planes(sent):
+        received.append(chip_exchange(other_dist))
+        return slopes(nx, True, *lax.optimization_barrier((rows, own_dist, sent))[:2])
+
+    def partner_planes(sent):
+        return slopes(nx, True, *lax.optimization_barrier((rows, received[0], sent))[:2])
+
+    (ma, mb), (own_part, far_part) = partial_sums(partial, "vert", [own_planes, partner_planes])
+    summed = ma + mb
+    arrived = chip_exchange(summed)
+    own_decay, own_source, sign = maps(nx, "own", summed, rows, own_part)
     arrived, own_decay, own_source = lax.optimization_barrier((arrived, own_decay, own_source))
-    near, face, entry, *chip = compose_chip(nx, sign, arrived, own_decay, own_source, inflow)
+    near, face, entry, *chip = compose_chip(nx, arrived, rows, far_part, sign, own_decay, own_source, inflow)
     got = entry
     chips = lax.axis_size("gx") // 2
     for step in range(chips - 1):
@@ -530,6 +513,12 @@
             entry, face = pass_face(step, sign, got, entry, chip[0])
         low, high = chip_hop(face, step)
         got = low if low is high else jnp.where(side[0] == 1, low, high)
+        if step == 0:
+            other_part = slopes(nx, False, *lax.optimization_barrier((rows, other_dist, face))[:2])
+            decay, source = maps(nx, "other", summed, rows, other_part)
+            got, decay, source = lax.optimization_barrier((got, decay, source))
+    if chips == 1:
+        decay, source = maps(nx, "other", summed, rows, slopes(nx, False, rows, other_dist))
     keep, share = share_entry(chips - 1, sign, got, entry, near)
     other = chip_exchange(share)
     own_moments = new_moments(nx, True, keep, table, own_decay, own_source)

time: 38.5 us -> 38.3 us (level)
  Pallas kernels: 10.4 us -> 13.2 us
  waiting for transfers between devices: 11.1 us -> 8.41 us
    ppermute x1, waiting for transfers between devices: 4.02 us -> 1.01 us  [chip_hop(): got = lax.ppermute(face, 'gx', pairs)]
    pallas_call x2 -> x3, Pallas kernels: 4.71 us -> 7.07 us  [slopes(): pl.pallas_call(functools.partial(slope_kernel, nx, own), in_specs=[whole]...]
    ppermute x8, starting transfers between devices: 13.7 us -> 12.9 us  [exchange(): return lax.ppermute(a, axis, [(i, i ^ mask) for i in range(n)])]
    ppermute x8, waiting for transfers between devices: 5.24 us -> 5.83 us  [exchange(): return lax.ppermute(a, axis, [(i, i ^ mask) for i in range(n)])]
    ppermute x2 -> x3, starting transfers between devices: 0.14 us -> 0.66 us  [chip_exchange(): return lax.ppermute(a, 'gx', [(i, i ^ 1) for i in range(n)])]
    pallas_call x1, Pallas kernels: 0.15 us -> 0.66 us  [compose_chip(): pl.pallas_call(functools.partial(compose_kernel, nx), in_specs=[whole] *...]
    ppermute x2 -> x3, waiting for transfers between devices: 1.84 us -> 1.58 us  [chip_exchange(): return lax.ppermute(a, 'gx', [(i, i ^ 1) for i in range(n)])]
  transfers between devices with their start and end apart: 11 -> 12, of which waited for: 10 -> 10; matrix products, arithmetic and copies ran while one was open for 0% -> 0% of each run, Pallas kernels for 19% -> 27%
where the time goes in v7:
time: 38.3 us; the launch traced here: 38.1 us
  starting transfers between devices  15.1 us (39%)
  Pallas kernels  13.2 us (34%)
  waiting for transfers between devices  8.41 us (22%)
  between operations  0.73 us (2%)
  other arithmetic  0.68 us (2%)
    ppermute x8, starting transfers between devices, exchange(): return lax.ppermute(a, axis, [(i, i ^ mask) for i in range(n)])  12.9 us
    pallas_call x3, Pallas kernels, slopes(): pl.pallas_call(functools.partial(slope_kernel, nx, own), in_specs=[whole]...  7.07 us
    ppermute x8, waiting for transfers between devices, exchange(): return lax.ppermute(a, axis, [(i, i ^ mask) for i in range(n)])  5.83 us
    pallas_call x1, Pallas kernels, old_moments(): pl.pallas_call(functools.partial(moments_kernel, total, nx), in_specs=[pl...  2 us
    ppermute x1, starting transfers between devices, chip_hop(): got = lax.ppermute(face, 'gx', pairs)  1.59 us
    ppermute x3, waiting for transfers between devices, chip_exchange(): return lax.ppermute(a, 'gx', [(i, i ^ 1) for i in range(n)])  1.58 us
    pallas_call x1, Pallas kernels, write_dist(): pl.pallas_call(functools.partial(write_kernel, nx, pieces), in_specs=[who...  1.44 us
    pallas_call x2, Pallas kernels, maps(): pl.pallas_call(functools.partial(map_kernel, nx, kind), in_specs=[whole]...  1.33 us
  transfers between devices with their start and end apart: 12, of which 10 were waited for; matrix products, arithmetic and copies ran while one was open for 0% of the time, Pallas kernels for 27%

profile of v7, /device:TPU:0, one launch (start us, length us, event | category | flops | bytes accessed | tf_op | source)
XLA Modules:
  0.0 38.1 jit_solution(8975622208480275292)
XLA Ops:
  0.6 2.0 %moments.1 = (f32[104,128]{1,0:T(8,128)S(1)}, bf16[2,32,256]{2,1,0:T(8,128)(2,1)S(1)}, f32[2,8,256]{2,1,0:T(8,128)S(1)}, f32[2048,128]{1,0:T(8,128)S(1)}, f32[2048,128]{1,0:T(8,128)S(1)}) custom-call(s32[1,512]{1,0:T(1,128)} %bitcast.9, f32[1,512]{1,0:T(1,128)} %bitcast.10, f32[2,512]{1,0:T(2,128)} %cross_hbm.1, f32[1,512]{1,0:T(1,128)} %bitcast.11, ...), custom_call_target="tpu_custom_call" | custom-call | flops 50331648 | bytes 2097152 | tf_op jit(solution)/shard_map/moments/pallas_call | solution.py:90
  2.6 0.0 copy-start
  2.7 0.5 %collective-permute-start.4 = (f32[2048,128]{1,0:T(8,128)S(1)}, f32[2048,128]{1,0:T(8,128)S(1)}, u32[]{:S(2)}, u32[]{:S(2)}) collective-permute-start(f32[2048,128]{1,0:T(8,128)S(1)} %get-tuple-element.92.dist_ref), channel_id=1, source_target_pairs={{0,8},{8,0},{16,24},{24,16},{1,9},{9,1},{17,25},{25,17},{2,10},{10... | collective-permute-start | bytes 3145736 | tf_op jit(solution)/shard_map/ppermute | solution.py:367
  3.2 3.6 %collective-permute-start.2 = (f32[104,128]{1,0:T(8,128)S(1)}, f32[104,128]{1,0:T(8,128)S(1)}, u32[]{:S(2)}, u32[]{:S(2)}) collective-permute-start(f32[104,128]{1,0:T(8,128)S(1)} %get-tuple-element.60), channel_id=1, source_target_pairs={{0,3},{1,2},{2,1},{3,0},{4,7},{5,6},{6,5},{7,4},{8,11},{9,10},{10,... | collective-permute-start | bytes 159752 | tf_op jit(solution)/shard_map/ppermute | solution.py:465
  6.7 0.4 %collective-permute-start.1 = (f32[104,128]{1,0:T(8,128)S(1)}, f32[104,128]{1,0:T(8,128)S(1)}, u32[]{:S(2)}, u32[]{:S(2)}) collective-permute-start(f32[104,128]{1,0:T(8,128)S(1)} %get-tuple-element.60), channel_id=1, source_target_pairs={{0,2},{1,3},{2,0},{3,1},{4,6},{5,7},{6,4},{7,5},{8,10},{9,11},{10,... | collective-permute-start | bytes 159752 | tf_op jit(solution)/shard_map/ppermute | solution.py:465
  7.2 0.2 collective-permute-start
  7.4 2.4 %slope.3 = (f32[8,256,128]{2,1,0:T(8,128)S(1)}, f32[256,128]{1,0:T(8,128)S(1)}, bf16[256,128]{1,0:T(8,128)(2,1)S(1)}) custom-call(f32[2,8,256]{2,1,0:T(8,128)S(1)} %get-tuple-element.91.rows_ref, f32[2048,128]{1,0:T(8,128)S(1)} %get-tuple-element.64.dist_ref), custom_call_target="tpu_custom_call" | custom-call | flops 5242880 | bytes 2097152 | tf_op jit(solution)/shard_map/slope/pallas_call | solution.py:156
  9.8 0.0 collective-permute-done.2
  9.8 1.1 %collective-permute-done.1 = f32[104,128]{1,0:T(8,128)S(1)} collective-permute-done((f32[104,128]{1,0:T(8,128)S(1)}, f32[104,128]{1,0:T(8,128)S(1)}, u32[]{:S(2)}, u32[]{:S(2)}) %collective-permute-start.1) | collective-permute-done | bytes 53280 | tf_op jit(solution)/shard_map/ppermute | solution.py:465
  10.9 0.4 %collective-permute-done = f32[104,128]{1,0:T(8,128)S(1)} collective-permute-done((f32[104,128]{1,0:T(8,128)S(1)}, f32[104,128]{1,0:T(8,128)S(1)}, u32[]{:S(2)}, u32[]{:S(2)}) %collective-permute-start) | collective-permute-done | bytes 53280 | tf_op jit(solution)/shard_map/ppermute | solution.py:465
  11.4 2.7 %collective-permute-start.3 = (f32[104,128]{1,0:T(8,128)S(1)}, f32[104,128]{1,0:T(8,128)S(1)}, u32[]{:S(2)}, u32[]{:S(2)}) collective-permute-start(f32[104,128]{1,0:T(8,128)S(1)} %add_add_fusion.1), channel_id=1, source_target_pairs={{0,4},{1,5},{2,6},{3,7},{4,0},{5,1},{6,2},{7,3},{8,12},{9,13},{10,... | collective-permute-start | bytes 159752 | tf_op jit(solution)/shard_map/ppermute | solution.py:465
  14.0 0.0 collective-permute-done.4.dist_ref
  14.0 2.4 %slope.4 = (f32[8,256,128]{2,1,0:T(8,128)S(1)}, f32[256,128]{1,0:T(8,128)S(1)}, bf16[256,128]{1,0:T(8,128)(2,1)S(1)}) custom-call(f32[2,8,256]{2,1,0:T(8,128)S(1)} %get-tuple-element.91.rows_ref, f32[2048,128]{1,0:T(8,128)S(1)} %collective-permute-done.4.dist_ref), custom_call_target="tpu_custom_call" | custom-call | flops 5242880 | bytes 2097152 | tf_op jit(solution)/shard_map/slope/pallas_call | solution.py:156
  16.4 0.1 collective-permute-done.3
  16.5 0.1 collective-permute-start.5
  16.5 0.7 %own_maps.1 = (f32[8,256,128]{2,1,0:T(8,128)S(1)}, f32[8,256,128]{2,1,0:T(8,128)S(1)}, f32[8,128]{1,0:T(8,128)S(1)}) custom-call(f32[104,128]{1,0:T(8,128)S(1)} %add.27.sum_ref, f32[2,8,256]{2,1,0:T(8,128)S(1)} %get-tuple-element.91.rows_ref, f32[8,256,128]{2,1,0:T(8,128)S(1)} %get-tuple-element.78.slope_ref, f32[256,128]{1,0:T(8,128)S(1)} %get-tuple-element.79.speed_ref, ...), custom_call_target="tpu_custom_call" | custom-call | flops 10485760 | bytes 3145728 | tf_op jit(solution)/shard_map/own_maps/pallas_call | solution.py:259
  17.2 0.6 %collective-permute-done.5.sum_ref = f32[104,128]{1,0:T(8,128)S(1)} collective-permute-done((f32[104,128]{1,0:T(8,128)S(1)}, f32[104,128]{1,0:T(8,128)S(1)}, u32[]{:S(2)}, u32[]{:S(2)}) %collective-permute-start.5) | collective-permute-done | bytes 53280 | tf_op jit(solution)/shard_map/ppermute | solution.py:367
  17.8 0.0 copy-done
  17.8 0.7 %compose.1 = (f32[2,256,128]{2,1,0:T(8,128)S(1)}, f32[256,128]{1,0:T(8,128)S(1)}, f32[256,128]{1,0:T(8,128)S(1)}) custom-call(f32[104,128]{1,0:T(8,128)S(1)} %collective-permute-done.5.sum_ref, f32[2,8,256]{2,1,0:T(8,128)S(1)} %get-tuple-element.91.rows_ref, f32[8,256,128]{2,1,0:T(8,128)S(1)} %get-tuple-element.85.slope_ref, ...), custom_call_target="tpu_custom_call" | custom-call | flops 10485760 | bytes 3145728 | tf_op jit(solution)/shard_map/compose/pallas_call | solution.py:310
  18.4 1.6 %collective-permute-start.6 = (f32[256,128]{1,0:T(8,128)S(1)}, f32[256,128]{1,0:T(8,128)S(1)}, u32[]{:S(2)}, u32[]{:S(2)}) collective-permute-start(f32[256,128]{1,0:T(8,128)S(1)} %get-tuple-element.90), channel_id=1, source_target_pairs={{0,16},{8,24},{16,0},{24,8},{1,17},{9,25},{17,1},{25,9},{2,18},{10... | collective-permute-start | bytes 393224 | tf_op jit(solution)/shard_map/ppermute | solution.py:375
  20.0 2.4 %slope.5 = (f32[8,256,128]{2,1,0:T(8,128)S(1)}, f32[256,128]{1,0:T(8,128)S(1)}, bf16[256,128]{1,0:T(8,128)(2,1)S(1)}) custom-call(f32[2,8,256]{2,1,0:T(8,128)S(1)} %get-tuple-element.91.rows_ref, f32[2048,128]{1,0:T(8,128)S(1)} %get-tuple-element.92.dist_ref), custom_call_target="tpu_custom_call" | custom-call | flops 5242880 | bytes 2097152 | tf_op jit(solution)/shard_map/slope/pallas_call | solution.py:156
  22.4 0.7 %other_maps.1 = (f32[8,256,128]{2,1,0:T(8,128)S(1)}, f32[8,256,128]{2,1,0:T(8,128)S(1)}) custom-call(f32[104,128]{1,0:T(8,128)S(1)} %add.27.sum_ref, f32[2,8,256]{2,1,0:T(8,128)S(1)} %get-tuple-element.91.rows_ref, f32[8,256,128]{2,1,0:T(8,128)S(1)} %get-tuple-element.93.slope_ref, f32[256,128]{1,0:T(8,128)S(1)} %get-tuple-element.94.speed_ref, ...), custom_call_target="tpu_custom_call" | custom-call | flops 10485760 | bytes 3145728 | tf_op jit(solution)/shard_map/other_maps/pallas_call | solution.py:259
  23.1 1.0 %collective-permute-done.6.got_ref = f32[256,128]{1,0:T(8,128)S(1)} collective-permute-done((f32[256,128]{1,0:T(8,128)S(1)}, f32[256,128]{1,0:T(8,128)S(1)}, u32[]{:S(2)}, u32[]{:S(2)}) %collective-permute-start.6) | collective-permute-done | bytes 131104 | tf_op jit(solution)/shard_map/ppermute | solution.py:375
  24.1 0.1 share.1
  24.1 0.1 collective-permute-start.7
  24.2 0.3 new_moments.2.refs_0_
  24.5 1.0 %collective-permute-done.7.entry_ref.refs_3_ = f32[256,128]{1,0:T(8,128)S(1)} collective-permute-done((f32[256,128]{1,0:T(8,128)S(1)}, f32[256,128]{1,0:T(8,128)S(1)}, u32[]{:S(2)}, u32[]{:S(2)}) %collective-permute-start.7) | collective-permute-done | bytes 131104 | tf_op jit(solution)/shard_map/ppermute | solution.py:367
  25.5 0.3 new_moments.3
  25.8 1.7 %collective-permute-start.10 = (f32[104,128]{1,0:T(8,128)S(1)}, f32[104,128]{1,0:T(8,128)S(1)}, u32[]{:S(2)}, u32[]{:S(2)}) collective-permute-start(f32[104,128]{1,0:T(8,128)S(1)} %new_moments.3), channel_id=1, source_target_pairs={{0,3},{1,2},{2,1},{3,0},{4,7},{5,6},{6,5},{7,4},{8,11},{9,10},{10,... | collective-permute-start | bytes 159752 | tf_op jit(solution)/shard_map/ppermute | solution.py:465
  27.5 0.7 %collective-permute-start.9 = (f32[104,128]{1,0:T(8,128)S(1)}, f32[104,128]{1,0:T(8,128)S(1)}, u32[]{:S(2)}, u32[]{:S(2)}) collective-permute-start(f32[104,128]{1,0:T(8,128)S(1)} %new_moments.3), channel_id=1, source_target_pairs={{0,2},{1,3},{2,0},{3,1},{4,6},{5,7},{6,4},{7,5},{8,10},{9,11},{10,... | collective-permute-start | bytes 159752 | tf_op jit(solution)/shard_map/ppermute | solution.py:465
  28.2 1.2 %collective-permute-start.8 = (f32[104,128]{1,0:T(8,128)S(1)}, f32[104,128]{1,0:T(8,128)S(1)}, u32[]{:S(2)}, u32[]{:S(2)}) collective-permute-start(f32[104,128]{1,0:T(8,128)S(1)} %new_moments.3), channel_id=1, source_target_pairs={{0,1},{1,0},{2,3},{3,2},{4,5},{5,4},{6,7},{7,6},{8,9},{9,8},{10,11... | collective-permute-start | bytes 159752 | tf_op jit(solution)/shard_map/ppermute | solution.py:465
  29.4 1.4 %write_dist.1 = f32[4096,128]{1,0:T(8,128)} custom-call(f32[256,128]{1,0:T(8,128)S(1)} %get-tuple-element.108.entry_ref.refs_0_, f32[8,256,128]{2,1,0:T(8,128)S(1)} %get-tuple-element.109.decay_ref.refs_1_, f32[8,256,128]{2,1,0:T(8,128)S(1)} %get-tuple-element.110.source_ref.refs_2_, f32[256,128]{1,0:T(8,128)S(1)} %collective-permute-done.7.entry_ref.refs_3_, ...), custom_call_target="tpu_custom_call" | custom-call | flops 1048576 | bytes 6291456 | tf_op jit(solution)/shard_map/write_dist/pallas_call | solution.py:436
  30.8 0.3 collective-permute-done.10
  31.1 0.6 %collective-permute-done.9 = f32[104,128]{1,0:T(8,128)S(1)} collective-permute-done((f32[104,128]{1,0:T(8,128)S(1)}, f32[104,128]{1,0:T(8,128)S(1)}, u32[]{:S(2)}, u32[]{:S(2)}) %collective-permute-start.9) | collective-permute-done | bytes 53280 | tf_op jit(solution)/shard_map/ppermute | solution.py:465
  31.7 0.7 %collective-permute-done.8 = f32[104,128]{1,0:T(8,128)S(1)} collective-permute-done((f32[104,128]{1,0:T(8,128)S(1)}, f32[104,128]{1,0:T(8,128)S(1)}, u32[]{:S(2)}, u32[]{:S(2)}) %collective-permute-start.8) | collective-permute-done | bytes 53280 | tf_op jit(solution)/shard_map/ppermute | solution.py:465
  32.4 2.5 %collective-permute-start.11 = (f32[104,128]{1,0:T(8,128)S(1)}, f32[104,128]{1,0:T(8,128)S(1)}, u32[]{:S(2)}, u32[]{:S(2)}) collective-permute-start(f32[104,128]{1,0:T(8,128)S(1)} %add_add_fusion), channel_id=1, source_target_pairs={{0,4},{1,5},{2,6},{3,7},{4,0},{5,1},{6,2},{7,3},{8,12},{9,13},{10,... | collective-permute-start | bytes 159752 | tf_op jit(solution)/shard_map/ppermute | solution.py:465
  34.8 2.7 %collective-permute-done.11 = f32[104,128]{1,0:T(8,128)S(1)} collective-permute-done((f32[104,128]{1,0:T(8,128)S(1)}, f32[104,128]{1,0:T(8,128)S(1)}, u32[]{:S(2)}, u32[]{:S(2)}) %collective-permute-start.11) | collective-permute-done | bytes 53280 | tf_op jit(solution)/shard_map/ppermute | solution.py:465
  37.5 0.6 %add_bitcast_fusion = f32[13,8,128]{2,1,0:T(8,128)} fusion(f32[104,128]{1,0:T(8,128)S(1)} %add_add_fusion, f32[104,128]{1,0:T(8,128)S(1)} %collective-permute-done.11), kind=kLoop, calls=%fused_computation | loop fusion | flops 13312 | bytes 159744 | tf_op jit(solution)/shard_map/reshape | solution.py:533
  (3 shorter events, 0.0 us)
Async XLA Ops:
  2.6 15.1 %copy-start = (f32[512,128]{1,0:T(8,128)S(1)}, f32[512,128]{1,0:T(8,128)}, u32[]{:S(2)}) copy-start(f32[512,128]{1,0:T(8,128)} %inflow_ref.1) | copy-start | bytes 786436
  2.7 11.4 %collective-permute-start.4 = (f32[2048,128]{1,0:T(8,128)S(1)}, f32[2048,128]{1,0:T(8,128)S(1)}, u32[]{:S(2)}, u32[]{:S(2)}) collective-permute-start(f32[2048,128]{1,0:T(8,128)S(1)} %get-tuple-element.92.dist_ref), channel_id=1, source_target_pairs={{0,8},{8,0},{16,24},{24,16},{1,9},{9,1},{17,25},{25,17},{2,10},{10... | collective-permute-start | bytes 3145736 | tf_op jit(solution)/shard_map/ppermute | solution.py:367
  3.2 6.6 %collective-permute-start.2 = (f32[104,128]{1,0:T(8,128)S(1)}, f32[104,128]{1,0:T(8,128)S(1)}, u32[]{:S(2)}, u32[]{:S(2)}) collective-permute-start(f32[104,128]{1,0:T(8,128)S(1)} %get-tuple-element.60), channel_id=1, source_target_pairs={{0,3},{1,2},{2,1},{3,0},{4,7},{5,6},{6,5},{7,4},{8,11},{9,10},{10,... | collective-permute-start | bytes 159752 | tf_op jit(solution)/shard_map/ppermute | solution.py:465
  6.7 4.1 %collective-permute-start.1 = (f32[104,128]{1,0:T(8,128)S(1)}, f32[104,128]{1,0:T(8,128)S(1)}, u32[]{:S(2)}, u32[]{:S(2)}) collective-permute-start(f32[104,128]{1,0:T(8,128)S(1)} %get-tuple-element.60), channel_id=1, source_target_pairs={{0,2},{1,3},{2,0},{3,1},{4,6},{5,7},{6,4},{7,5},{8,10},{9,11},{10,... | collective-permute-start | bytes 159752 | tf_op jit(solution)/shard_map/ppermute | solution.py:465
  7.2 4.1 %collective-permute-start = (f32[104,128]{1,0:T(8,128)S(1)}, f32[104,128]{1,0:T(8,128)S(1)}, u32[]{:S(2)}, u32[]{:S(2)}) collective-permute-start(f32[104,128]{1,0:T(8,128)S(1)} %get-tuple-element.60), channel_id=1, source_target_pairs={{0,1},{1,0},{2,3},{3,2},{4,5},{5,4},{6,7},{7,6},{8,9},{9,8},{10,11... | collective-permute-start | bytes 159752 | tf_op jit(solution)/shard_map/ppermute | solution.py:465
  11.4 5.1 %collective-permute-start.3 = (f32[104,128]{1,0:T(8,128)S(1)}, f32[104,128]{1,0:T(8,128)S(1)}, u32[]{:S(2)}, u32[]{:S(2)}) collective-permute-start(f32[104,128]{1,0:T(8,128)S(1)} %add_add_fusion.1), channel_id=1, source_target_pairs={{0,4},{1,5},{2,6},{3,7},{4,0},{5,1},{6,2},{7,3},{8,12},{9,13},{10,... | collective-permute-start | bytes 159752 | tf_op jit(solution)/shard_map/ppermute | solution.py:465
  16.5 1.3 %collective-permute-start.5 = (f32[104,128]{1,0:T(8,128)S(1)}, f32[104,128]{1,0:T(8,128)S(1)}, u32[]{:S(2)}, u32[]{:S(2)}) collective-permute-start(f32[104,128]{1,0:T(8,128)S(1)} %add.27.sum_ref), channel_id=1, source_target_pairs={{0,8},{8,0},{16,24},{24,16},{1,9},{9,1},{17,25},{25,17},{2,10},{10... | collective-permute-start | bytes 159752 | tf_op jit(solution)/shard_map/ppermute | solution.py:367
  18.4 5.6 %collective-permute-start.6 = (f32[256,128]{1,0:T(8,128)S(1)}, f32[256,128]{1,0:T(8,128)S(1)}, u32[]{:S(2)}, u32[]{:S(2)}) collective-permute-start(f32[256,128]{1,0:T(8,128)S(1)} %get-tuple-element.90), channel_id=1, source_target_pairs={{0,16},{8,24},{16,0},{24,8},{1,17},{9,25},{17,1},{25,9},{2,18},{10... | collective-permute-start | bytes 393224 | tf_op jit(solution)/shard_map/ppermute | solution.py:375
  24.1 1.4 %collective-permute-start.7 = (f32[256,128]{1,0:T(8,128)S(1)}, f32[256,128]{1,0:T(8,128)S(1)}, u32[]{:S(2)}, u32[]{:S(2)}) collective-permute-start(f32[256,128]{1,0:T(8,128)S(1)} %get-tuple-element.101), channel_id=1, source_target_pairs={{0,8},{8,0},{16,24},{24,16},{1,9},{9,1},{17,25},{25,17},{2,10},{10... | collective-permute-start | bytes 393224 | tf_op jit(solution)/shard_map/ppermute | solution.py:367
  25.8 5.3 %collective-permute-start.10 = (f32[104,128]{1,0:T(8,128)S(1)}, f32[104,128]{1,0:T(8,128)S(1)}, u32[]{:S(2)}, u32[]{:S(2)}) collective-permute-start(f32[104,128]{1,0:T(8,128)S(1)} %new_moments.3), channel_id=1, source_target_pairs={{0,3},{1,2},{2,1},{3,0},{4,7},{5,6},{6,5},{7,4},{8,11},{9,10},{10,... | collective-permute-start | bytes 159752 | tf_op jit(solution)/shard_map/ppermute | solution.py:465
  27.5 4.1 %collective-permute-start.9 = (f32[104,128]{1,0:T(8,128)S(1)}, f32[104,128]{1,0:T(8,128)S(1)}, u32[]{:S(2)}, u32[]{:S(2)}) collective-permute-start(f32[104,128]{1,0:T(8,128)S(1)} %new_moments.3), channel_id=1, source_target_pairs={{0,2},{1,3},{2,0},{3,1},{4,6},{5,7},{6,4},{7,5},{8,10},{9,11},{10,... | collective-permute-start | bytes 159752 | tf_op jit(solution)/shard_map/ppermute | solution.py:465
  28.2 4.1 %collective-permute-start.8 = (f32[104,128]{1,0:T(8,128)S(1)}, f32[104,128]{1,0:T(8,128)S(1)}, u32[]{:S(2)}, u32[]{:S(2)}) collective-permute-start(f32[104,128]{1,0:T(8,128)S(1)} %new_moments.3), channel_id=1, source_target_pairs={{0,1},{1,0},{2,3},{3,2},{4,5},{5,4},{6,7},{7,6},{8,9},{9,8},{10,11... | collective-permute-start | bytes 159752 | tf_op jit(solution)/shard_map/ppermute | solution.py:465
  32.4 5.1 %collective-permute-start.11 = (f32[104,128]{1,0:T(8,128)S(1)}, f32[104,128]{1,0:T(8,128)S(1)}, u32[]{:S(2)}, u32[]{:S(2)}) collective-permute-start(f32[104,128]{1,0:T(8,128)S(1)} %add_add_fusion), channel_id=1, source_target_pairs={{0,4},{1,5},{2,6},{3,7},{4,0},{5,1},{6,2},{7,3},{8,12},{9,13},{10,... | collective-permute-start | bytes 159752 | tf_op jit(solution)/shard_map/ppermute | solution.py:465

commit v8 on v7

--- a/solution.py
+++ b/solution.py
@@ -529,7 +529,7 @@
         args = lax.optimization_barrier((keep, own_decay, own_source, other, decay, source, sent))[:6]
         return write_dist(nx, *args)
 
-    (na, nb), (new_flat,) = partial_sums(new_partial, "vert", [write])
+    (na, nb), (_, new_flat) = partial_sums(new_partial, "vert", [lambda sent: sent, write])
     return new_flat.reshape(count, nx, lanes), (na + nb).reshape(NMOM, nx, lanes)
 
 

time: 38.3 us -> 38.3 us (level)
  no operation moved by 1% of the time
where the time goes in v8:
time: 38.3 us; the launch traced here: 38.1 us
  starting transfers between devices  15.1 us (39%)
  Pallas kernels  13.2 us (34%)
  waiting for transfers between devices  8.41 us (22%)
  between operations  0.73 us (2%)
  other arithmetic  0.67 us (2%)
    ppermute x8, starting transfers between devices, exchange(): return lax.ppermute(a, axis, [(i, i ^ mask) for i in range(n)])  12.9 us
    pallas_call x3, Pallas kernels, slopes(): pl.pallas_call(functools.partial(slope_kernel, nx, own), in_specs=[whole]...  7.07 us
    ppermute x8, waiting for transfers between devices, exchange(): return lax.ppermute(a, axis, [(i, i ^ mask) for i in range(n)])  5.83 us
    pallas_call x1, Pallas kernels, old_moments(): pl.pallas_call(functools.partial(moments_kernel, total, nx), in_specs=[pl...  2 us
    ppermute x1, starting transfers between devices, chip_hop(): got = lax.ppermute(face, 'gx', pairs)  1.59 us
    ppermute x3, waiting for transfers between devices, chip_exchange(): return lax.ppermute(a, 'gx', [(i, i ^ 1) for i in range(n)])  1.58 us
    pallas_call x1, Pallas kernels, write_dist(): pl.pallas_call(functools.partial(write_kernel, nx, pieces), in_specs=[who...  1.44 us
    pallas_call x2, Pallas kernels, maps(): pl.pallas_call(functools.partial(map_kernel, nx, kind), in_specs=[whole]...  1.33 us
  transfers between devices with their start and end apart: 12, of which 10 were waited for; matrix products, arithmetic and copies ran while one was open for 0% of the time, Pallas kernels for 27%

profile of v8, /device:TPU:0, one launch (start us, length us, event | category | flops | bytes accessed | tf_op | source)
XLA Modules:
  0.0 38.1 jit_solution(6397641819298724512)
XLA Ops:
  0.6 2.0 %moments.1 = (f32[104,128]{1,0:T(8,128)S(1)}, bf16[2,32,256]{2,1,0:T(8,128)(2,1)S(1)}, f32[2,8,256]{2,1,0:T(8,128)S(1)}, f32[2048,128]{1,0:T(8,128)S(1)}, f32[2048,128]{1,0:T(8,128)S(1)}) custom-call(s32[1,512]{1,0:T(1,128)} %bitcast.9, f32[1,512]{1,0:T(1,128)} %bitcast.10, f32[2,512]{1,0:T(2,128)} %cross_hbm.1, f32[1,512]{1,0:T(1,128)} %bitcast.11, ...), custom_call_target="tpu_custom_call" | custom-call | flops 50331648 | bytes 2097152 | tf_op jit(solution)/shard_map/moments/pallas_call | solution.py:90
  2.6 0.0 copy-start
  2.7 0.5 %collective-permute-start.4 = (f32[2048,128]{1,0:T(8,128)S(1)}, f32[2048,128]{1,0:T(8,128)S(1)}, u32[]{:S(2)}, u32[]{:S(2)}) collective-permute-start(f32[2048,128]{1,0:T(8,128)S(1)} %get-tuple-element.93.dist_ref), channel_id=1, source_target_pairs={{0,8},{8,0},{16,24},{24,16},{1,9},{9,1},{17,25},{25,17},{2,10},{10... | collective-permute-start | bytes 3145736 | tf_op jit(solution)/shard_map/ppermute | solution.py:367
  3.2 3.6 %collective-permute-start.2 = (f32[104,128]{1,0:T(8,128)S(1)}, f32[104,128]{1,0:T(8,128)S(1)}, u32[]{:S(2)}, u32[]{:S(2)}) collective-permute-start(f32[104,128]{1,0:T(8,128)S(1)} %get-tuple-element.61), channel_id=1, source_target_pairs={{0,3},{1,2},{2,1},{3,0},{4,7},{5,6},{6,5},{7,4},{8,11},{9,10},{10,... | collective-permute-start | bytes 159752 | tf_op jit(solution)/shard_map/ppermute | solution.py:465
  6.7 0.4 %collective-permute-start.1 = (f32[104,128]{1,0:T(8,128)S(1)}, f32[104,128]{1,0:T(8,128)S(1)}, u32[]{:S(2)}, u32[]{:S(2)}) collective-permute-start(f32[104,128]{1,0:T(8,128)S(1)} %get-tuple-element.61), channel_id=1, source_target_pairs={{0,2},{1,3},{2,0},{3,1},{4,6},{5,7},{6,4},{7,5},{8,10},{9,11},{10,... | collective-permute-start | bytes 159752 | tf_op jit(solution)/shard_map/ppermute | solution.py:465
  7.2 0.2 collective-permute-start
  7.4 2.4 %slope.3 = (f32[8,256,128]{2,1,0:T(8,128)S(1)}, f32[256,128]{1,0:T(8,128)S(1)}, bf16[256,128]{1,0:T(8,128)(2,1)S(1)}) custom-call(f32[2,8,256]{2,1,0:T(8,128)S(1)} %get-tuple-element.92.rows_ref, f32[2048,128]{1,0:T(8,128)S(1)} %get-tuple-element.65.dist_ref), custom_call_target="tpu_custom_call" | custom-call | flops 5242880 | bytes 2097152 | tf_op jit(solution)/shard_map/slope/pallas_call | solution.py:156
  9.8 0.0 collective-permute-done.2
  9.8 1.1 %collective-permute-done.1 = f32[104,128]{1,0:T(8,128)S(1)} collective-permute-done((f32[104,128]{1,0:T(8,128)S(1)}, f32[104,128]{1,0:T(8,128)S(1)}, u32[]{:S(2)}, u32[]{:S(2)}) %collective-permute-start.1) | collective-permute-done | bytes 53280 | tf_op jit(solution)/shard_map/ppermute | solution.py:465
  10.9 0.4 %collective-permute-done = f32[104,128]{1,0:T(8,128)S(1)} collective-permute-done((f32[104,128]{1,0:T(8,128)S(1)}, f32[104,128]{1,0:T(8,128)S(1)}, u32[]{:S(2)}, u32[]{:S(2)}) %collective-permute-start) | collective-permute-done | bytes 53280 | tf_op jit(solution)/shard_map/ppermute | solution.py:465
  11.4 2.7 %collective-permute-start.3 = (f32[104,128]{1,0:T(8,128)S(1)}, f32[104,128]{1,0:T(8,128)S(1)}, u32[]{:S(2)}, u32[]{:S(2)}) collective-permute-start(f32[104,128]{1,0:T(8,128)S(1)} %add_add_fusion.1), channel_id=1, source_target_pairs={{0,4},{1,5},{2,6},{3,7},{4,0},{5,1},{6,2},{7,3},{8,12},{9,13},{10,... | collective-permute-start | bytes 159752 | tf_op jit(solution)/shard_map/ppermute | solution.py:465
  14.0 0.0 collective-permute-done.4.dist_ref
  14.0 2.4 %slope.4 = (f32[8,256,128]{2,1,0:T(8,128)S(1)}, f32[256,128]{1,0:T(8,128)S(1)}, bf16[256,128]{1,0:T(8,128)(2,1)S(1)}) custom-call(f32[2,8,256]{2,1,0:T(8,128)S(1)} %get-tuple-element.92.rows_ref, f32[2048,128]{1,0:T(8,128)S(1)} %collective-permute-done.4.dist_ref), custom_call_target="tpu_custom_call" | custom-call | flops 5242880 | bytes 2097152 | tf_op jit(solution)/shard_map/slope/pallas_call | solution.py:156
  16.4 0.1 collective-permute-done.3
  16.5 0.1 collective-permute-start.5
  16.5 0.7 %own_maps.1 = (f32[8,256,128]{2,1,0:T(8,128)S(1)}, f32[8,256,128]{2,1,0:T(8,128)S(1)}, f32[8,128]{1,0:T(8,128)S(1)}) custom-call(f32[104,128]{1,0:T(8,128)S(1)} %add.27.sum_ref, f32[2,8,256]{2,1,0:T(8,128)S(1)} %get-tuple-element.92.rows_ref, f32[8,256,128]{2,1,0:T(8,128)S(1)} %get-tuple-element.79.slope_ref, f32[256,128]{1,0:T(8,128)S(1)} %get-tuple-element.80.speed_ref, ...), custom_call_target="tpu_custom_call" | custom-call | flops 10485760 | bytes 3145728 | tf_op jit(solution)/shard_map/own_maps/pallas_call | solution.py:259
  17.2 0.6 %collective-permute-done.5.sum_ref = f32[104,128]{1,0:T(8,128)S(1)} collective-permute-done((f32[104,128]{1,0:T(8,128)S(1)}, f32[104,128]{1,0:T(8,128)S(1)}, u32[]{:S(2)}, u32[]{:S(2)}) %collective-permute-start.5) | collective-permute-done | bytes 53280 | tf_op jit(solution)/shard_map/ppermute | solution.py:367
  17.8 0.0 copy-done
  17.8 0.7 %compose.1 = (f32[2,256,128]{2,1,0:T(8,128)S(1)}, f32[256,128]{1,0:T(8,128)S(1)}, f32[256,128]{1,0:T(8,128)S(1)}) custom-call(f32[104,128]{1,0:T(8,128)S(1)} %collective-permute-done.5.sum_ref, f32[2,8,256]{2,1,0:T(8,128)S(1)} %get-tuple-element.92.rows_ref, f32[8,256,128]{2,1,0:T(8,128)S(1)} %get-tuple-element.86.slope_ref, ...), custom_call_target="tpu_custom_call" | custom-call | flops 10485760 | bytes 3145728 | tf_op jit(solution)/shard_map/compose/pallas_call | solution.py:310
  18.4 1.6 %collective-permute-start.6 = (f32[256,128]{1,0:T(8,128)S(1)}, f32[256,128]{1,0:T(8,128)S(1)}, u32[]{:S(2)}, u32[]{:S(2)}) collective-permute-start(f32[256,128]{1,0:T(8,128)S(1)} %get-tuple-element.91), channel_id=1, source_target_pairs={{0,16},{8,24},{16,0},{24,8},{1,17},{9,25},{17,1},{25,9},{2,18},{10... | collective-permute-start | bytes 393224 | tf_op jit(solution)/shard_map/ppermute | solution.py:375
  20.0 2.4 %slope.5 = (f32[8,256,128]{2,1,0:T(8,128)S(1)}, f32[256,128]{1,0:T(8,128)S(1)}, bf16[256,128]{1,0:T(8,128)(2,1)S(1)}) custom-call(f32[2,8,256]{2,1,0:T(8,128)S(1)} %get-tuple-element.92.rows_ref, f32[2048,128]{1,0:T(8,128)S(1)} %get-tuple-element.93.dist_ref), custom_call_target="tpu_custom_call" | custom-call | flops 5242880 | bytes 2097152 | tf_op jit(solution)/shard_map/slope/pallas_call | solution.py:156
  22.4 0.7 %other_maps.1 = (f32[8,256,128]{2,1,0:T(8,128)S(1)}, f32[8,256,128]{2,1,0:T(8,128)S(1)}) custom-call(f32[104,128]{1,0:T(8,128)S(1)} %add.27.sum_ref, f32[2,8,256]{2,1,0:T(8,128)S(1)} %get-tuple-element.92.rows_ref, f32[8,256,128]{2,1,0:T(8,128)S(1)} %get-tuple-element.94.slope_ref, f32[256,128]{1,0:T(8,128)S(1)} %get-tuple-element.95.speed_ref, ...), custom_call_target="tpu_custom_call" | custom-call | flops 10485760 | bytes 3145728 | tf_op jit(solution)/shard_map/other_maps/pallas_call | solution.py:259
  23.1 1.0 %collective-permute-done.6.got_ref = f32[256,128]{1,0:T(8,128)S(1)} collective-permute-done((f32[256,128]{1,0:T(8,128)S(1)}, f32[256,128]{1,0:T(8,128)S(1)}, u32[]{:S(2)}, u32[]{:S(2)}) %collective-permute-start.6) | collective-permute-done | bytes 131104 | tf_op jit(solution)/shard_map/ppermute | solution.py:375
  24.1 0.1 share.1
  24.1 0.1 collective-permute-start.7
  24.2 0.3 new_moments.2.refs_0_
  24.5 1.0 %collective-permute-done.7.entry_ref.refs_3_ = f32[256,128]{1,0:T(8,128)S(1)} collective-permute-done((f32[256,128]{1,0:T(8,128)S(1)}, f32[256,128]{1,0:T(8,128)S(1)}, u32[]{:S(2)}, u32[]{:S(2)}) %collective-permute-start.7) | collective-permute-done | bytes 131104 | tf_op jit(solution)/shard_map/ppermute | solution.py:367
  25.5 0.3 new_moments.3
  25.8 1.7 %collective-permute-start.10 = (f32[104,128]{1,0:T(8,128)S(1)}, f32[104,128]{1,0:T(8,128)S(1)}, u32[]{:S(2)}, u32[]{:S(2)}) collective-permute-start(f32[104,128]{1,0:T(8,128)S(1)} %new_moments.3), channel_id=1, source_target_pairs={{0,3},{1,2},{2,1},{3,0},{4,7},{5,6},{6,5},{7,4},{8,11},{9,10},{10,... | collective-permute-start | bytes 159752 | tf_op jit(solution)/shard_map/ppermute | solution.py:465
  27.5 0.7 %collective-permute-start.9 = (f32[104,128]{1,0:T(8,128)S(1)}, f32[104,128]{1,0:T(8,128)S(1)}, u32[]{:S(2)}, u32[]{:S(2)}) collective-permute-start(f32[104,128]{1,0:T(8,128)S(1)} %new_moments.3), channel_id=1, source_target_pairs={{0,2},{1,3},{2,0},{3,1},{4,6},{5,7},{6,4},{7,5},{8,10},{9,11},{10,... | collective-permute-start | bytes 159752 | tf_op jit(solution)/shard_map/ppermute | solution.py:465
  28.2 1.2 %collective-permute-start.8 = (f32[104,128]{1,0:T(8,128)S(1)}, f32[104,128]{1,0:T(8,128)S(1)}, u32[]{:S(2)}, u32[]{:S(2)}) collective-permute-start(f32[104,128]{1,0:T(8,128)S(1)} %new_moments.3), channel_id=1, source_target_pairs={{0,1},{1,0},{2,3},{3,2},{4,5},{5,4},{6,7},{7,6},{8,9},{9,8},{10,11... | collective-permute-start | bytes 159752 | tf_op jit(solution)/shard_map/ppermute | solution.py:465
  29.4 1.7 %collective-permute-done.10 = f32[104,128]{1,0:T(8,128)S(1)} collective-permute-done((f32[104,128]{1,0:T(8,128)S(1)}, f32[104,128]{1,0:T(8,128)S(1)}, u32[]{:S(2)}, u32[]{:S(2)}) %collective-permute-start.10) | collective-permute-done | bytes 53280 | tf_op jit(solution)/shard_map/ppermute | solution.py:465
  31.1 0.6 %collective-permute-done.9 = f32[104,128]{1,0:T(8,128)S(1)} collective-permute-done((f32[104,128]{1,0:T(8,128)S(1)}, f32[104,128]{1,0:T(8,128)S(1)}, u32[]{:S(2)}, u32[]{:S(2)}) %collective-permute-start.9) | collective-permute-done | bytes 53280 | tf_op jit(solution)/shard_map/ppermute | solution.py:465
  31.7 0.7 %collective-permute-done.8 = f32[104,128]{1,0:T(8,128)S(1)} collective-permute-done((f32[104,128]{1,0:T(8,128)S(1)}, f32[104,128]{1,0:T(8,128)S(1)}, u32[]{:S(2)}, u32[]{:S(2)}) %collective-permute-start.8) | collective-permute-done | bytes 53280 | tf_op jit(solution)/shard_map/ppermute | solution.py:465
  32.4 2.5 %collective-permute-start.11 = (f32[104,128]{1,0:T(8,128)S(1)}, f32[104,128]{1,0:T(8,128)S(1)}, u32[]{:S(2)}, u32[]{:S(2)}) collective-permute-start(f32[104,128]{1,0:T(8,128)S(1)} %add_add_fusion), channel_id=1, source_target_pairs={{0,4},{1,5},{2,6},{3,7},{4,0},{5,1},{6,2},{7,3},{8,12},{9,13},{10,... | collective-permute-start | bytes 159752 | tf_op jit(solution)/shard_map/ppermute | solution.py:465
  34.8 1.4 %write_dist.1 = f32[4096,128]{1,0:T(8,128)} custom-call(f32[256,128]{1,0:T(8,128)S(1)} %get-tuple-element.112.entry_ref.refs_0_, f32[8,256,128]{2,1,0:T(8,128)S(1)} %get-tuple-element.113.decay_ref.refs_1_, f32[8,256,128]{2,1,0:T(8,128)S(1)} %get-tuple-element.114.source_ref.refs_2_, f32[256,128]{1,0:T(8,128)S(1)} %collective-permute-done.7.entry_ref.refs_3_, ...), custom_call_target="tpu_custom_call" | custom-call | flops 1048576 | bytes 6291456 | tf_op jit(solution)/shard_map/write_dist/pallas_call | solution.py:436
  36.3 1.2 %collective-permute-done.11 = f32[104,128]{1,0:T(8,128)S(1)} collective-permute-done((f32[104,128]{1,0:T(8,128)S(1)}, f32[104,128]{1,0:T(8,128)S(1)}, u32[]{:S(2)}, u32[]{:S(2)}) %collective-permute-start.11) | collective-permute-done | bytes 53280 | tf_op jit(solution)/shard_map/ppermute | solution.py:465
  37.5 0.6 %add_bitcast_fusion = f32[13,8,128]{2,1,0:T(8,128)} fusion(f32[104,128]{1,0:T(8,128)S(1)} %add_add_fusion, f32[104,128]{1,0:T(8,128)S(1)} %collective-permute-done.11), kind=kLoop, calls=%fused_computation | loop fusion | flops 13312 | bytes 159744 | tf_op jit(solution)/shard_map/reshape | solution.py:533
  (3 shorter events, 0.0 us)
Async XLA Ops:
  2.6 15.1 %copy-start = (f32[512,128]{1,0:T(8,128)S(1)}, f32[512,128]{1,0:T(8,128)}, u32[]{:S(2)}) copy-start(f32[512,128]{1,0:T(8,128)} %inflow_ref.1) | copy-start | bytes 786436
  2.7 11.4 %collective-permute-start.4 = (f32[2048,128]{1,0:T(8,128)S(1)}, f32[2048,128]{1,0:T(8,128)S(1)}, u32[]{:S(2)}, u32[]{:S(2)}) collective-permute-start(f32[2048,128]{1,0:T(8,128)S(1)} %get-tuple-element.93.dist_ref), channel_id=1, source_target_pairs={{0,8},{8,0},{16,24},{24,16},{1,9},{9,1},{17,25},{25,17},{2,10},{10... | collective-permute-start | bytes 3145736 | tf_op jit(solution)/shard_map/ppermute | solution.py:367
  3.2 6.6 %collective-permute-start.2 = (f32[104,128]{1,0:T(8,128)S(1)}, f32[104,128]{1,0:T(8,128)S(1)}, u32[]{:S(2)}, u32[]{:S(2)}) collective-permute-start(f32[104,128]{1,0:T(8,128)S(1)} %get-tuple-element.61), channel_id=1, source_target_pairs={{0,3},{1,2},{2,1},{3,0},{4,7},{5,6},{6,5},{7,4},{8,11},{9,10},{10,... | collective-permute-start | bytes 159752 | tf_op jit(solution)/shard_map/ppermute | solution.py:465
  6.7 4.1 %collective-permute-start.1 = (f32[104,128]{1,0:T(8,128)S(1)}, f32[104,128]{1,0:T(8,128)S(1)}, u32[]{:S(2)}, u32[]{:S(2)}) collective-permute-start(f32[104,128]{1,0:T(8,128)S(1)} %get-tuple-element.61), channel_id=1, source_target_pairs={{0,2},{1,3},{2,0},{3,1},{4,6},{5,7},{6,4},{7,5},{8,10},{9,11},{10,... | collective-permute-start | bytes 159752 | tf_op jit(solution)/shard_map/ppermute | solution.py:465
  7.2 4.1 %collective-permute-start = (f32[104,128]{1,0:T(8,128)S(1)}, f32[104,128]{1,0:T(8,128)S(1)}, u32[]{:S(2)}, u32[]{:S(2)}) collective-permute-start(f32[104,128]{1,0:T(8,128)S(1)} %get-tuple-element.61), channel_id=1, source_target_pairs={{0,1},{1,0},{2,3},{3,2},{4,5},{5,4},{6,7},{7,6},{8,9},{9,8},{10,11... | collective-permute-start | bytes 159752 | tf_op jit(solution)/shard_map/ppermute | solution.py:465
  11.4 5.1 %collective-permute-start.3 = (f32[104,128]{1,0:T(8,128)S(1)}, f32[104,128]{1,0:T(8,128)S(1)}, u32[]{:S(2)}, u32[]{:S(2)}) collective-permute-start(f32[104,128]{1,0:T(8,128)S(1)} %add_add_fusion.1), channel_id=1, source_target_pairs={{0,4},{1,5},{2,6},{3,7},{4,0},{5,1},{6,2},{7,3},{8,12},{9,13},{10,... | collective-permute-start | bytes 159752 | tf_op jit(solution)/shard_map/ppermute | solution.py:465
  16.5 1.3 %collective-permute-start.5 = (f32[104,128]{1,0:T(8,128)S(1)}, f32[104,128]{1,0:T(8,128)S(1)}, u32[]{:S(2)}, u32[]{:S(2)}) collective-permute-start(f32[104,128]{1,0:T(8,128)S(1)} %add.27.sum_ref), channel_id=1, source_target_pairs={{0,8},{8,0},{16,24},{24,16},{1,9},{9,1},{17,25},{25,17},{2,10},{10... | collective-permute-start | bytes 159752 | tf_op jit(solution)/shard_map/ppermute | solution.py:367
  18.4 5.6 %collective-permute-start.6 = (f32[256,128]{1,0:T(8,128)S(1)}, f32[256,128]{1,0:T(8,128)S(1)}, u32[]{:S(2)}, u32[]{:S(2)}) collective-permute-start(f32[256,128]{1,0:T(8,128)S(1)} %get-tuple-element.91), channel_id=1, source_target_pairs={{0,16},{8,24},{16,0},{24,8},{1,17},{9,25},{17,1},{25,9},{2,18},{10... | collective-permute-start | bytes 393224 | tf_op jit(solution)/shard_map/ppermute | solution.py:375
  24.1 1.4 %collective-permute-start.7 = (f32[256,128]{1,0:T(8,128)S(1)}, f32[256,128]{1,0:T(8,128)S(1)}, u32[]{:S(2)}, u32[]{:S(2)}) collective-permute-start(f32[256,128]{1,0:T(8,128)S(1)} %get-tuple-element.102), channel_id=1, source_target_pairs={{0,8},{8,0},{16,24},{24,16},{1,9},{9,1},{17,25},{25,17},{2,10},{10... | collective-permute-start | bytes 393224 | tf_op jit(solution)/shard_map/ppermute | solution.py:367
  25.8 5.3 %collective-permute-start.10 = (f32[104,128]{1,0:T(8,128)S(1)}, f32[104,128]{1,0:T(8,128)S(1)}, u32[]{:S(2)}, u32[]{:S(2)}) collective-permute-start(f32[104,128]{1,0:T(8,128)S(1)} %new_moments.3), channel_id=1, source_target_pairs={{0,3},{1,2},{2,1},{3,0},{4,7},{5,6},{6,5},{7,4},{8,11},{9,10},{10,... | collective-permute-start | bytes 159752 | tf_op jit(solution)/shard_map/ppermute | solution.py:465
  27.5 4.1 %collective-permute-start.9 = (f32[104,128]{1,0:T(8,128)S(1)}, f32[104,128]{1,0:T(8,128)S(1)}, u32[]{:S(2)}, u32[]{:S(2)}) collective-permute-start(f32[104,128]{1,0:T(8,128)S(1)} %new_moments.3), channel_id=1, source_target_pairs={{0,2},{1,3},{2,0},{3,1},{4,6},{5,7},{6,4},{7,5},{8,10},{9,11},{10,... | collective-permute-start | bytes 159752 | tf_op jit(solution)/shard_map/ppermute | solution.py:465
  28.2 4.1 %collective-permute-start.8 = (f32[104,128]{1,0:T(8,128)S(1)}, f32[104,128]{1,0:T(8,128)S(1)}, u32[]{:S(2)}, u32[]{:S(2)}) collective-permute-start(f32[104,128]{1,0:T(8,128)S(1)} %new_moments.3), channel_id=1, source_target_pairs={{0,1},{1,0},{2,3},{3,2},{4,5},{5,4},{6,7},{7,6},{8,9},{9,8},{10,11... | collective-permute-start | bytes 159752 | tf_op jit(solution)/shard_map/ppermute | solution.py:465
  32.4 5.1 %collective-permute-start.11 = (f32[104,128]{1,0:T(8,128)S(1)}, f32[104,128]{1,0:T(8,128)S(1)}, u32[]{:S(2)}, u32[]{:S(2)}) collective-permute-start(f32[104,128]{1,0:T(8,128)S(1)} %add_add_fusion), channel_id=1, source_target_pairs={{0,4},{1,5},{2,6},{3,7},{4,0},{5,1},{6,2},{7,3},{8,12},{9,13},{10,... | collective-permute-start | bytes 159752 | tf_op jit(solution)/shard_map/ppermute | solution.py:465
